TPU v7x, 32 devices: a whole 2x2x4 slice. The times are simulated.
32 devices in a mesh: dp: 8 (over z, y), tensor: 4 (over x, core).
Axes of the slice: x: 2, y: 2, z: 4, core: 2. Of those that a mesh axis runs over, the one named last changes fastest.
Arguments:
- tokens: bfloat16 [1024, 8192], P(('dp', 'tensor')), may hold values from -6 to 6
- base_weight: bfloat16 [8192, 4096], P(None, 'tensor'), may hold values from -0.0625 to 0.0625
- out_grad: bfloat16 [1024, 4096], P('dp', 'tensor'), may hold values from -6 to 6
- block_index: int32 [8, 2], replicated, may hold values from 0 to 63
- block_owner: int32 [8], replicated, may hold values from 0 to 7, as said below
- delta: bfloat16 [16, 16384], P('dp', 'tensor'), may hold values from -0.5 to 0.5
- moment1: float32 [16, 16384], P('dp', 'tensor'), may hold values from -4 to 4
- moment2: float32 [16, 16384], P('dp', 'tensor'), may hold values from 0.01 to 1
Outputs:
- projected: bfloat16 [1024, 4096], P('dp', 'tensor')
- input_grad: bfloat16 [1024, 8192], P(('dp', 'tensor'))
- new_delta: bfloat16 [16, 16384], P('dp', 'tensor')
- new_moment1: float32 [16, 16384], P('dp', 'tensor')
- new_moment2: float32 [16, 16384], P('dp', 'tensor')
Inputs may be any that keep to these rules, and one draw needn't show every extreme that they name: `block_owner`: each owner holds at most 2 blocks and some owner exactly 2; some owners hold none.
All inputs are finite; a program needn't handle non-finite values.
Results may differ from a plain program's by a relative error of at most 0.013.
Values may be sent and summed in bfloat16 or wider, within the bound.
No kernel may reach another device: no remote copies, remote signals or barrier semaphores. Data moves between devices by JAX's collectives and lax.ppermute only.
A program may use at most 128 MiB of HBM per device.

v0:
```python
import math

import jax
import jax.numpy as jnp
from jax import lax
from jax.sharding import PartitionSpec as P

D = 8192
HEAD_DIM = 128


CORRECT_ONE = 1.0 - 0.9**10
CORRECT_TWO = 1.0 - 0.999**10


def tables(block_index, block_owner, dp_count, capacity):
    owners = jnp.arange(dp_count, dtype=jnp.int32)
    owner_hit = (block_owner[:, None] == owners[None, :]).astype(jnp.int32)
    before = jnp.cumsum(owner_hit, axis=0) - owner_hit
    slot_rank = jnp.sum(before * owner_hit, axis=1)
    slot_of = block_owner * capacity + slot_rank
    slot_match = (
        slot_of[None, :] == jnp.arange(capacity * dp_count, dtype=jnp.int32)[:, None]
    ).astype(jnp.int32)
    slot_live = jnp.sum(slot_match, axis=1)
    slot_row = jnp.sum(slot_match * block_index[None, :, 0], axis=1)
    slot_head = jnp.sum(slot_match * block_index[None, :, 1], axis=1)
    return (slot_live, slot_row, slot_head)


def on_device(tokens, base_weight, out_grad, block_index, block_owner, delta, moment1, moment2):
    dp_count = lax.axis_size("dp")
    tp_index = lax.axis_index("tensor")
    capacity = delta.shape[0]
    slot_count = capacity * dp_count
    heads_dev = out_grad.shape[1] // HEAD_DIM
    row_blocks = D // HEAD_DIM
    slot_live, slot_row, slot_head = tables(block_index, block_owner, dp_count, capacity)
    owned = slot_live * (slot_head // heads_dev == tp_index).astype(jnp.int32)
    local_head = jnp.clip(slot_head - tp_index * heads_dev, 0, heads_dev - 1)
    gathered = lax.all_gather(tokens, "tensor", axis=0, tiled=True)
    whole_rows = lax.all_gather(delta, "tensor", axis=1, tiled=True)
    all_blocks = lax.all_gather(whole_rows, "dp", axis=0, tiled=True)
    blocks = all_blocks.reshape(slot_count, HEAD_DIM, HEAD_DIM)
    token_count = gathered.shape[0]
    slabs = gathered.reshape(token_count, row_blocks, HEAD_DIM)
    token_pick = jnp.take(slabs, slot_row, axis=1)
    base_part = jnp.dot(gathered, base_weight, preferred_element_type=jnp.float32)
    delta_out = jnp.einsum("tsk,skn->tsn", token_pick, blocks, preferred_element_type=jnp.float32)
    delta_out = delta_out * owned.astype(jnp.float32)[None, :, None]
    delta_sum = (
        jnp.zeros((token_count, heads_dev, HEAD_DIM), jnp.float32)
        .at[:, local_head, :]
        .add(delta_out)
    )
    projected = (base_part + delta_sum.reshape(token_count, heads_dev * HEAD_DIM)).astype(
        jnp.bfloat16
    )
    grad_heads = out_grad.reshape(token_count, heads_dev, HEAD_DIM)
    grad_pick = jnp.take(grad_heads, local_head, axis=1) * owned.astype(jnp.bfloat16)[None, :, None]
    row_count = tokens.shape[0] * lax.axis_size("tensor")
    base_back = lax.dot_general(
        out_grad, base_weight, (((1,), (1,)), ((), ())), preferred_element_type=jnp.float32
    )
    delta_back = jnp.einsum("tsn,skn->tsk", grad_pick, blocks, preferred_element_type=jnp.float32)
    row_spread = (
        jnp.zeros((row_count, row_blocks, HEAD_DIM), jnp.float32).at[:, slot_row, :].add(delta_back)
    )
    input_grad = lax.psum_scatter(
        (base_back + row_spread.reshape(row_count, D)).astype(jnp.bfloat16),
        "tensor",
        scatter_dimension=0,
        tiled=True,
    )
    grad_scale = 1.0 / math.sqrt(token_count * dp_count)
    grad_block = jnp.einsum(
        "tsk,tsn->skn", token_pick, grad_pick, preferred_element_type=jnp.float32
    )
    owned_grad = lax.psum_scatter(
        (grad_block * grad_scale)
        .reshape(capacity * lax.axis_size("dp"), HEAD_DIM * HEAD_DIM)
        .astype(jnp.bfloat16),
        "dp",
        scatter_dimension=0,
        tiled=True,
    )
    block_grad = lax.psum_scatter(owned_grad, "tensor", scatter_dimension=1, tiled=True).astype(
        jnp.float32
    )
    first_new = 0.9 * moment1 + 0.1 * block_grad
    second_new = 0.999 * moment2 + 0.001 * block_grad * block_grad
    update_step = 0.02 * (first_new / CORRECT_ONE) / (jnp.sqrt(second_new / CORRECT_TWO) + 1e-08)
    new_delta = (delta.astype(jnp.float32) - update_step).astype(jnp.bfloat16)
    return (projected, input_grad, new_delta, first_new, second_new)


def solution(mesh):
    placed = (
        P(("dp", "tensor"), None),
        P(None, "tensor"),
        P("dp", "tensor"),
        P(),
        P(),
        P("dp", "tensor"),
        P("dp", "tensor"),
        P("dp", "tensor"),
    )
    return jax.shard_map(
        on_device,
        mesh=mesh,
        in_specs=placed,
        out_specs=(
            P("dp", "tensor"),
            P(("dp", "tensor"), None),
            P("dp", "tensor"),
            P("dp", "tensor"),
            P("dp", "tensor"),
        ),
        check_vma=False,
    )
```

profile of v0, /device:TPU:0, one launch (start us, length us, event | category | flops | bytes accessed | tf_op | source)
XLA Modules:
  0.0 208.1 jit_solution(7862643188654716178)
XLA Ops:
  7.2 0.7 all-gather.3.cloned.1.call-update
  8.0 1.1 copy.38
  9.3 0.7 fusion.10
  10.0 0.8 select_reduce_fusion.2
  10.9 0.7 multiply_add_fusion
  11.5 0.8 slice_bitcast_fusion.1
  12.4 0.6 gather_fusion.1
  13.1 21.8 %all-gather.3.cloned.1.call-done = bf16[128,8192]{1,0:T(8,128)(2,1)} async-done(((bf16[32,8192]{1,0:T(8,128)(2,1)}), bf16[128,8192]{1,0:T(8,128)(2,1)}) %all-gather.3.cloned.1.call-update) | async-done | bytes 2097168 | tf_op jit(solution)/shard_map/all_gather | solution.py:41
  34.9 3.2 %copy.35 = bf16[128,8192]{0,1:T(8,128)(2,1)S(1)} copy(bf16[128,8192]{1,0:T(8,128)(2,1)} %all-gather.3.cloned.1.call-done) | data formatting | bytes 4194304 | tf_op jit(solution)/shard_map/all_gather | solution.py:41
  38.1 2.9 %copy.36 = bf16[128,64,128]{2,0,1:T(8,128)(2,1)} copy(bf16[128,64,128]{0,2,1:T(8,128)(2,1)S(1)} %bitcast.49) | data formatting | bytes 4194304 | tf_op jit(solution)/shard_map/reshape | solution.py:46
  41.0 2.2 %gather_fusion = bf16[16,128,128]{2,1,0:T(8,128)(2,1)S(1)} fusion(bf16[128,64,128]{2,0,1:T(8,128)(2,1)} %copy.36, s32[1024]{0:T(1024)S(1)} %pad_clamp_fusion.1), kind=kCustom, calls=%fused_computation | custom fusion | bytes 1048640 | tf_op jit(solution)/shard_map/jit(_take)/gather | solution.py:47
  43.3 0.4 fusion.1
  43.7 1.1 copy.51
  45.0 5.2 %all_gather.10 = bf16[2,16384]{1,0:T(2,128)(2,1)S(1)} all-gather(bf16[2,4096]{1,0:T(2,128)(2,1)S(1)} %copy-done.2), channel_id=1, replica_groups=mesh['dp'=8,'tensor'=4] {'tensor'}, dimensions={1}, use_global_device_ids=true | all-gather | bytes 81920 | tf_op jit(solution)/shard_map/all_gather | solution.py:42
  50.2 32.1 %all-gather = bf16[8,2,16384]{2,1,0:T(2,128)(2,1)S(1)} all-gather(bf16[1,2,16384]{2,1,0:T(2,128)(2,1)S(1)} %bitcast.54), channel_id=1, replica_groups=mesh['dp'=8,'tensor'=4] {'dp'}, dimensions={0}, use_global_device_ids=true | all-gather | bytes 589824 | tf_op jit(solution)/shard_map/all_gather | solution.py:43
  82.3 0.4 reshape.106
  82.7 0.6 dynamic-slice
  84.0 0.5 fusion.4
  84.5 2.5 %broadcast_in_dim.35 = f32[128,64,128]{2,0,1:T(8,128)} broadcast(f32[]{:T(128)} %constant.39.clone.1), dimensions={} | broadcast | bytes 4194308 | tf_op jit(solution)/shard_map/broadcast_in_dim | solution.py:67
  87.0 3.6 %scatter_fusion.1 = f32[128,64,128]{2,0,1:T(8,128)} fusion(f32[128,64,128]{2,0,1:T(8,128)} %broadcast_in_dim.35, s32[16]{0:T(128)S(1)} %fusion.12, f32[16,128,128]{2,1,0:T(8,128)S(1)} %fusion.4), kind=kCustom, calls=%fused_computation.3 | custom fusion | flops 262144 | bytes 3145792 | tf_op jit(solution)/shard_map/scatter-add | solution.py:67
  90.6 28.1 %all-reduce.3.cloned.1.call-done = bf16[16,16384]{1,0:T(8,128)(2,1)} async-done(((bf16[16,16384]{1,0:T(8,128)(2,1)}), bf16[16,16384]{1,0:T(8,128)(2,1)}) %all-reduce.3.cloned.1.call-update) | async-done | bytes 524304
  118.8 1.0 constant_dynamic-slice_fusion
  119.8 3.4 %copy.43 = bf16[2,16384]{0,1:T(8,128)(2,1)} copy(bf16[2,16384]{1,0:T(2,128)(2,1)S(1)} %constant_dynamic-slice_fusion) | data formatting | bytes 131072
  123.2 0.2 reduce-scatter.5.cloned.1.call-start
  123.4 15.2 %fusion = bf16[128,8192]{1,0:T(8,128)(2,1)} fusion(bf16[128,1024]{1,0:T(8,128)(2,1)S(1)} %copy-done.1, bf16[8192,1024]{1,0:T(8,128)(2,1)} %param.9, f32[128,64,128]{2,0,1:T(8,128)} %scatter_fusion.1), kind=kOutput, calls=%fused_computation.5 | convolution fusion | flops 2149580800 | bytes 23330816 | tf_op jit(solution)/shard_map/dot_general | solution.py:62
  138.7 1.3 convolution_multiply_fusion.1
  140.1 2.9 %scatter_fusion = f32[128,8,128]{2,0,1:T(8,128)S(1)} fusion(f32[128,8,128]{2,0,1:T(8,128)S(1)} %broadcast_in_dim.32, s32[16]{0:T(128)S(1)} %fusion.11, f32[16,128,128]{2,1,0:T(8,128)} %convolution_multiply_fusion.1), kind=kCustom, calls=%fused_computation.2 | custom fusion | flops 262144 | bytes 3145792 | tf_op jit(solution)/shard_map/scatter-add | solution.py:54
  143.0 8.8 %fusion.2 = bf16[128,1024]{1,0:T(8,128)(2,1)} fusion(bf16[128,8192]{1,0:T(8,128)(2,1)S(1)} %copy-done, bf16[8192,1024]{1,0:T(8,128)(2,1)} %param.9, f32[128,8,128]{2,0,1:T(8,128)S(1)} %scatter_fusion), kind=kOutput, calls=%fused_computation.10 | convolution fusion | flops 2147745792 | bytes 19660800 | tf_op jit(solution)/shard_map/dot_general | solution.py:48
  151.8 15.3 %reduce-scatter.7.cloned.1.call-done = bf16[4096,2]{1,0:T(8,128)(2,1)} async-done(((bf16[16384,2]{1,0:T(8,128)(2,1)}), bf16[4096,2]{1,0:T(8,128)(2,1)}) %reduce-scatter.7.cloned.1.call-update) | async-done | bytes 16400
  167.2 1.6 copy.44
  168.8 0.7 subtract_convert_fusion
  169.5 32.1 %reduce-scatter.5.cloned.1.call-done = bf16[32,8192]{1,0:T(8,128)(2,1)} async-done(((bf16[128,8192]{1,0:T(8,128)(2,1)}), bf16[32,8192]{1,0:T(8,128)(2,1)}) %reduce-scatter.5.cloned.1.call-update) | async-done | bytes 524304 | tf_op jit(solution)/shard_map/reduce_scatter | solution.py:69
  (29 shorter events, 0.6 us)
Async XLA Ops:
  7.2 27.7 %all-gather.3.cloned.1.call-start = ((), (), s32[]{:S(2)}) async-start(), calls=%async_computation.2 | async-start | bytes 2621440 | tf_op jit(solution)/shard_map/all_gather | solution.py:41
  7.9 110.9 %all-reduce.3.cloned.1.call-start = ((), (), s32[]{:S(2)}) async-start(), calls=%async_computation.5 | async-start | bytes 1048576
  38.1 6.8 %copy-start.2 = (bf16[2,4096]{1,0:T(2,128)(2,1)S(1)}, bf16[2,4096]{1,0:T(2,128)(2,1)}, u32[]{:S(2)}) copy-start(bf16[2,4096]{1,0:T(2,128)(2,1)} %param.13) | copy-start | bytes 49156
  41.0 41.7 %copy-start.5 = (u32[32]{0:T(128)S(1)}, u32[32]{0:T(128)}, u32[]{:S(2)}) copy-start(u32[32]{0:T(128)} %constant.90) | copy-start | bytes 388
  44.9 122.3 %reduce-scatter.7.cloned.1.call-start = ((), (), s32[]{:S(2)}) async-start(), calls=%async_computation.4 | async-start | bytes 5242880
  119.8 3.6 %copy-start.1 = (bf16[128,1024]{1,0:T(8,128)(2,1)S(1)}, bf16[128,1024]{1,0:T(8,128)(2,1)}, u32[]{:S(2)}) copy-start(bf16[128,1024]{1,0:T(8,128)(2,1)} %param.10) | copy-start | bytes 786436
  123.2 78.4 %reduce-scatter.5.cloned.1.call-start = ((), (), s32[]{:S(2)}) async-start(), calls=%async_computation.3 | async-start | bytes 2621440 | tf_op jit(solution)/shard_map/reduce_scatter | solution.py:69
  138.7 4.3 %copy-start = (bf16[128,8192]{1,0:T(8,128)(2,1)S(1)}, bf16[128,8192]{1,0:T(8,128)(2,1)}, u32[]{:S(2)}) copy-start(bf16[128,8192]{1,0:T(8,128)(2,1)} %all-gather.3.cloned.1.call-done) | copy-start | bytes 6291460
  143.0 25.8 %copy-start.3 = (f32[2,4096]{1,0:T(2,128)S(1)}, f32[2,4096]{1,0:T(2,128)}, u32[]{:S(2)}) copy-start(f32[2,4096]{1,0:T(2,128)} %param.14) | copy-start | bytes 98308
  143.0 25.7 %copy-start.4 = (f32[2,4096]{1,0:T(2,128)S(1)}, f32[2,4096]{1,0:T(2,128)}, u32[]{:S(2)}) copy-start(f32[2,4096]{1,0:T(2,128)} %param.15) | copy-start | bytes 98308
Sparse Core Ops, SparseCore 0:
  9.6 25.2 all-gather.2
  45.0 73.7 all-reduce.2
  123.3 43.7 reduce-scatter.6
  170.1 31.4 reduce-scatter.4
where the time goes:
time: 209 us; the launch traced here: 208 us
  waiting for transfers between devices  98 us (47%)
  blocking collectives  37.4 us (18%)
  matrix products  26.3 us (13%)
  local copies, waits for them, and re-layouts  21.8 us (10%)
  between operations  14.6 us (7%)
  other arithmetic  9.68 us (5%)
    unnamed x6, waiting for transfers between devices  44.2 us
    all_gather x1, blocking collectives, on_device(): all_blocks = lax.all_gather(whole_rows, 'dp', axis=0, tiled=True)  32.1 us
    reduce_scatter x1, waiting for transfers between devices, on_device(): lax.psum_scatter((base_back + row_spread.reshape(row_count, D)).astype(jn...  32.1 us
    all_gather x1, waiting for transfers between devices, on_device(): gathered = lax.all_gather(tokens, 'tensor', axis=0, tiled=True)  21.8 us
    dot_general x1, matrix products, on_device(): lax.dot_general(out_grad, base_weight, (((1,), (1,)), ((), ())), preferre...  15.2 us
    unnamed x18, local copies, waits for them, and re-layouts  8.86 us
    dot_general x1, matrix products, on_device(): jnp.dot(gathered, base_weight, preferred_element_type=jnp.float32)  8.82 us
    all_gather x1, blocking collectives, on_device(): whole_rows = lax.all_gather(delta, 'tensor', axis=1, tiled=True)  5.25 us
  transfers between devices with their start and end apart: 4, of which 4 were waited for; matrix products, arithmetic and copies ran while one was open for 21% of the time, Pallas kernels for 0%

commit v1 on v0

v1 whole, which is shorter than its diff:
```python
import functools
import math

import jax
import jax.numpy as jnp
from jax import lax
from jax.experimental import pallas as pl
from jax.experimental.pallas import tpu as pltpu
from jax.sharding import PartitionSpec as P

HEAD_DIM = 128
LANES = 128
CORRECT_ONE = 1.0 - 0.9**10
CORRECT_TWO = 1.0 - 0.999**10
BF16 = jnp.bfloat16
F32 = jnp.float32
VMEM_LIMIT = 48 * 1024 * 1024
BACK_CHUNKS = 2
TILE = 512


def params():
    return pltpu.CompilerParams(vmem_limit_bytes=VMEM_LIMIT)


def vmem(n=1):
    return [pl.BlockSpec(memory_space=pltpu.VMEM)] * n


def smem(n=1):
    return [pl.BlockSpec(memory_space=pltpu.SMEM)] * n


def bits_of(count):
    return [1 << i for i in range(count.bit_length() - 1)]


def halving_order(count):
    order = [0]
    for bit in reversed(bits_of(count)):
        order = order + [j + bit for j in order]
    width = count.bit_length() - 1
    rev = lambda j: int(format(j, "0%db" % width)[::-1], 2) if width else 0
    return sorted(range(count), key=rev)


def xor_permute(x, axis, bit):
    count = lax.axis_size(axis)
    return lax.ppermute(x, axis, [(i, i ^ bit) for i in range(count)])


def slot_ranks(owner_ref, nb):
    ranks = []
    for b in range(nb):
        rank = jnp.int32(0)
        for before in range(b):
            rank = rank + (owner_ref[before] == owner_ref[b]).astype(jnp.int32)
        ranks.append(rank)
    return ranks


def lane_block(index):
    return pl.ds(pl.multiple_of(index * LANES, LANES), LANES)


def row_block(index, rows):
    return pl.ds(pl.multiple_of(index * rows, rows), rows)


def pick_kernel(nt, nb, index_ref, grad_ref, perm_ref, *piece_refs):
    me = lax.axis_index("tensor")
    rows = grad_ref.shape[0] // nt
    heads = grad_ref.shape[1] // HEAD_DIM
    for p, j in enumerate(halving_order(nt)):
        perm_ref[p * rows : (p + 1) * rows, :] = grad_ref[row_block(me ^ j, rows), :]
    for b in range(nb):
        head = index_ref[b, 1]
        mine = head // heads == me
        local = jnp.where(mine, head - me * heads, 0)
        cols = slice(b * LANES, (b + 1) * LANES)
        for j in range(nt):
            part = grad_ref[row_block(me ^ j, rows), lane_block(local)]
            piece_refs[j][:, cols] = jnp.where(mine, part, jnp.zeros_like(part))


def picks(block_index, out_grad, nt):
    nb = block_index.shape[0]
    rows = out_grad.shape[0] // nt
    return pl.pallas_call(
        functools.partial(pick_kernel, nt, nb),
        out_shape=[jax.ShapeDtypeStruct(out_grad.shape, BF16)]
        + [jax.ShapeDtypeStruct((rows, nb * LANES), BF16)] * nt,
        in_specs=smem() + vmem(),
        out_specs=vmem(1 + nt),
        compiler_params=params(),
        name="picks",
    )(block_index, out_grad)


def grad_kernel(nt, nd, nb, cap, scale, index_ref, owner_ref, tok_ref, *refs):
    piece_refs = refs[:nt]
    picked_ref, keep_ref, send_ref, block_ref = refs[nt:]
    me = lax.axis_index("tensor")
    dp = lax.axis_index("dp")
    part = HEAD_DIM // nt
    total = piece_refs[0][...].astype(F32)
    for j in range(1, nt):
        total = total + piece_refs[j][...].astype(F32)
    picked_ref[...] = total.astype(BF16)
    keep_ref[...] = jnp.zeros_like(keep_ref)
    send_ref[...] = jnp.zeros_like(send_ref)
    ranks = slot_ranks(owner_ref, nb)
    width = nd.bit_length() - 1
    order = halving_order(nt)
    half = nt // 2
    for b in range(nb):
        slab = tok_ref[:, lane_block(index_ref[b, 0])]
        block_ref[b] = (
            lax.dot_general(
                slab,
                picked_ref[:, b * LANES : (b + 1) * LANES],
                (((0,), (0,)), ((), ())),
                preferred_element_type=F32,
            )
            * scale
        ).astype(BF16)
        away = owner_ref[b] ^ dp
        place = jnp.int32(0)
        for i in range(width):
            place = place + ((away >> i) & 1) * (1 << (width - 1 - i))
        for p, j in enumerate(order):
            target = keep_ref if p < half else send_ref
            start = ((place * half + p % half) * cap + ranks[b]) * part
            target[pl.ds(pl.multiple_of(start, part), part), :] = block_ref[b, row_block(me ^ j, part), :]


def block_grads(block_index, block_owner, tokens, pieces, nt, nd, cap):
    nb = block_index.shape[0]
    rows = tokens.shape[0]
    scale = 1.0 / math.sqrt(rows * nt * nd)
    size = nd * (nt // 2) * cap * (HEAD_DIM // nt)
    return pl.pallas_call(
        functools.partial(grad_kernel, nt, nd, nb, cap, scale),
        out_shape=[
            jax.ShapeDtypeStruct((rows, nb * LANES), BF16),
            jax.ShapeDtypeStruct((size, LANES), BF16),
            jax.ShapeDtypeStruct((size, LANES), BF16),
        ],
        in_specs=smem(2) + vmem(1 + nt),
        out_specs=vmem(3),
        scratch_shapes=[pltpu.VMEM((nb, HEAD_DIM, HEAD_DIM), BF16)],
        compiler_params=params(),
        name="block_grads",
    )(block_index, block_owner, tokens, *pieces)


def first_step_kernel(cap, keep_ref, recv_ref, delta_ref, keep_out, send_out):
    half = keep_out.shape[0]
    part = delta_ref.shape[1] // LANES
    total = (keep_ref[...].astype(F32) + recv_ref[...].astype(F32)).astype(BF16)
    keep_out[...] = total[:half]
    send_out[:half, :] = total[half:]
    delta = delta_ref[...].astype(F32)
    for k in range(cap):
        lines = [delta[k : k + 1, i * LANES : (i + 1) * LANES] for i in range(part)]
        send_out[half + k * part : half + (k + 1) * part, :] = jnp.concatenate(lines, 0).astype(BF16)


def first_step(keep, recv, delta):
    cap = delta.shape[0]
    rows = keep.shape[0]
    extra = cap * delta.shape[1] // LANES
    return pl.pallas_call(
        functools.partial(first_step_kernel, cap),
        out_shape=[
            jax.ShapeDtypeStruct((rows // 2, LANES), BF16),
            jax.ShapeDtypeStruct((rows // 2 + extra, LANES), BF16),
        ],
        in_specs=vmem(3),
        out_specs=vmem(2),
        compiler_params=params(),
        name="first_step",
    )(keep, recv, delta)


def step_kernel(keep_ref, sent_ref, recv_ref, keep_out, send_out):
    rows = keep_ref.shape[0]
    half = rows // 2
    extra = sent_ref.shape[0] - rows
    total = (keep_ref[...].astype(F32) + recv_ref[:rows, :].astype(F32)).astype(BF16)
    keep_out[...] = total[:half]
    send_out[:half, :] = total[half:]
    send_out[half : half + extra, :] = sent_ref[rows:, :]
    send_out[half + extra :, :] = recv_ref[rows:, :]


def step(keep, sent, recv):
    rows = keep.shape[0]
    extra = sent.shape[0] - rows
    return pl.pallas_call(
        step_kernel,
        out_shape=[
            jax.ShapeDtypeStruct((rows // 2, LANES), BF16),
            jax.ShapeDtypeStruct((rows // 2 + 2 * extra, LANES), BF16),
        ],
        in_specs=vmem(3),
        out_specs=vmem(2),
        compiler_params=params(),
        name="chain_step",
    )(keep, sent, recv)


def compact_kernel(nb, cap, part, owner_ref, keep_ref, sent_ref, recv_ref, keep_out, send_out, all_ref):
    dp = lax.axis_index("dp")
    rows = keep_ref.shape[0]
    half = rows // 2
    extra = sent_ref.shape[0] - rows
    total = (keep_ref[...].astype(F32) + recv_ref[:rows, :].astype(F32)).astype(BF16)
    keep_out[...] = total[:half]
    send_out[:half, :] = total[half:]
    all_ref[:extra, :] = sent_ref[rows:, :]
    all_ref[extra:, :] = recv_ref[rows:, :]
    ranks = slot_ranks(owner_ref, nb)
    for b in range(nb):
        place = (owner_ref[b] ^ dp) * cap + ranks[b]
        send_out[half + b * part : half + (b + 1) * part, :] = all_ref[row_block(place, part), :]


def compact(block_owner, keep, sent, recv, cap, part):
    nb = block_owner.shape[0]
    rows = keep.shape[0]
    extra = sent.shape[0] - rows
    return pl.pallas_call(
        functools.partial(compact_kernel, nb, cap, part),
        out_shape=[
            jax.ShapeDtypeStruct((rows // 2, LANES), BF16),
            jax.ShapeDtypeStruct((rows // 2 + nb * part, LANES), BF16),
        ],
        in_specs=smem() + vmem(3),
        out_specs=vmem(2),
        scratch_shapes=[pltpu.VMEM((2 * extra, LANES), BF16)],
        compiler_params=params(),
        name="compact_step",
    )(block_owner, keep, sent, recv)


def adam_kernel(
    cap, keep_ref, sent_ref, recv_ref, delta_ref, one_ref, two_ref,
    blocks_out, delta_out, one_out, two_out, grad_ref,
):
    rows = keep_ref.shape[0]
    part = rows // cap
    extra = sent_ref.shape[0] - rows
    blocks_out[:extra, :] = sent_ref[rows:, :]
    blocks_out[extra:, :] = recv_ref[rows:, :]
    total = keep_ref[...].astype(F32) + recv_ref[:rows, :].astype(F32)
    for k in range(cap):
        for i in range(part):
            grad_ref[k : k + 1, i * LANES : (i + 1) * LANES] = total[k * part + i : k * part + i + 1, :]
    grad = grad_ref[...]
    first = 0.9 * one_ref[...] + 0.1 * grad
    second = 0.999 * two_ref[...] + 0.001 * grad * grad
    one_out[...] = first
    two_out[...] = second
    update = 0.02 * (first / CORRECT_ONE) / (jnp.sqrt(second / CORRECT_TWO) + 1e-08)
    delta_out[...] = (delta_ref[...].astype(F32) - update).astype(BF16)


def adam(keep, sent, recv, delta, moment1, moment2):
    rows = keep.shape[0]
    extra = sent.shape[0] - rows
    return pl.pallas_call(
        functools.partial(adam_kernel, delta.shape[0]),
        out_shape=[
            jax.ShapeDtypeStruct((2 * extra, LANES), BF16),
            jax.ShapeDtypeStruct(delta.shape, BF16),
            jax.ShapeDtypeStruct(delta.shape, F32),
            jax.ShapeDtypeStruct(delta.shape, F32),
        ],
        in_specs=vmem(6),
        out_specs=vmem(4),
        scratch_shapes=[pltpu.VMEM(delta.shape, F32)],
        compiler_params=params(),
        name="adam",
    )(keep, sent, recv, delta, moment1, moment2)


def back_kernel(grad_ref, weight_ref, keep_ref, send_ref):
    half = keep_ref.shape[0]
    out = lax.dot_general(
        grad_ref[...], weight_ref[...], (((1,), (1,)), ((), ())), preferred_element_type=F32
    ).astype(BF16)
    keep_ref[...] = out[:half]
    send_ref[...] = out[half:]


def back(grad, weight, chunk):
    rows = grad.shape[0]
    depth, cols = weight.shape
    width = depth // BACK_CHUNKS
    steps = width // TILE
    half = jax.ShapeDtypeStruct((rows // 2, width), BF16)
    return pl.pallas_call(
        back_kernel,
        grid=(steps,),
        out_shape=[half, half],
        in_specs=[
            pl.BlockSpec((rows, cols), lambda i: (0, 0)),
            pl.BlockSpec((TILE, cols), lambda i: (chunk * steps + i, 0)),
        ],
        out_specs=[pl.BlockSpec((rows // 2, TILE), lambda i: (0, i))] * 2,
        compiler_params=params(),
        cost_estimate=pl.CostEstimate(
            flops=2 * rows * width * cols, bytes_accessed=2 * width * cols + 2 * rows * width, transcendentals=0
        ),
        name="back",
    )(grad, weight)


def merge_kernel(keep_ref, recv_ref, keep_out, send_out):
    half = keep_out.shape[0]
    total = (keep_ref[...].astype(F32) + recv_ref[...].astype(F32)).astype(BF16)
    keep_out[...] = total[:half]
    send_out[...] = total[half:]


def merge(keep, recv):
    half = jax.ShapeDtypeStruct((keep.shape[0] // 2, keep.shape[1]), BF16)
    return pl.pallas_call(
        merge_kernel,
        out_shape=[half, half],
        in_specs=vmem(2),
        out_specs=vmem(2),
        compiler_params=params(),
        name="merge",
    )(keep, recv)


def load_block(block_ref, halves, order, b, nb, part, me):
    per = len(order) // 2
    for p, j in enumerate(order):
        source = halves[p // per]
        start = ((p % per) * nb + b) * part
        block_ref[row_block(me ^ j, part), :] = source[start : start + part, :]


def gather_order(nt):
    order = [0]
    for bit in bits_of(nt)[1:] + [1]:
        order = order + [j ^ bit for j in order]
    return order


def forward_kernel(nt, nb, steps, index_ref, *refs):
    token_refs = refs[:nt]
    near_ref, far_ref, weight_ref, out_ref, acc_ref, block_ref = refs[nt:]
    me = lax.axis_index("tensor")
    i = pl.program_id(0)
    order = gather_order(nt)
    rows = token_refs[0].shape[0]
    heads = out_ref.shape[1] // HEAD_DIM
    part = HEAD_DIM // nt

    def slab(cols):
        return jnp.concatenate([ref[:, cols] for ref in token_refs], axis=0)

    tile = slab(pl.ds(pl.multiple_of(i * TILE, TILE), TILE))
    product = jnp.dot(tile, weight_ref[...], preferred_element_type=F32)

    @pl.when(i == 0)
    def _():
        acc_ref[...] = product

    @pl.when(i > 0)
    def _():
        acc_ref[...] += product

    @pl.when(i == steps - 1)
    def _():
        for b in range(nb):
            head = index_ref[b, 1]

            @pl.when(head // heads == me)
            def _():
                load_block(block_ref, (near_ref, far_ref), order, b, nb, part, me)
                cols = lane_block(head - me * heads)
                acc_ref[:, cols] += jnp.dot(
                    slab(lane_block(index_ref[b, 0])), block_ref[...], preferred_element_type=F32
                )

        for p, j in enumerate(order):
            out_ref[row_block(me ^ j, rows), :] = acc_ref[p * rows : (p + 1) * rows, :].astype(BF16)


def forward(block_index, pieces, near, far, weight, nt):
    nb = block_index.shape[0]
    rows = pieces[0].shape[0] * nt
    depth, cols = weight.shape
    steps = depth // TILE
    whole = lambda x: pl.BlockSpec(x.shape, lambda i: (0, 0))
    return pl.pallas_call(
        functools.partial(forward_kernel, nt, nb, steps),
        grid=(steps,),
        out_shape=jax.ShapeDtypeStruct((rows, cols), BF16),
        in_specs=smem()
        + [whole(x) for x in pieces]
        + [whole(near), whole(far)]
        + [pl.BlockSpec((TILE, cols), lambda i: (i, 0))],
        out_specs=pl.BlockSpec((rows, cols), lambda i: (0, 0)),
        scratch_shapes=[pltpu.VMEM((rows, cols), F32), pltpu.VMEM((HEAD_DIM, HEAD_DIM), BF16)],
        compiler_params=params(),
        cost_estimate=pl.CostEstimate(
            flops=2 * rows * depth * cols, bytes_accessed=2 * depth * cols + 2 * rows * depth, transcendentals=0
        ),
        name="forward",
    )(block_index, *pieces, near, far, weight)


def final_kernel(nt, nb, chunks, index_ref, picked_ref, near_ref, far_ref, *refs):
    keeps, recvs = refs[:chunks], refs[chunks : 2 * chunks]
    out_ref, sum_ref, block_ref = refs[2 * chunks :]
    me = lax.axis_index("tensor")
    order = gather_order(nt)
    part = HEAD_DIM // nt
    width = keeps[0].shape[1]
    for c in range(chunks):
        sum_ref[:, c * width : (c + 1) * width] = keeps[c][...].astype(F32) + recvs[c][...].astype(F32)
    for b in range(nb):
        load_block(block_ref.at[b], (near_ref, far_ref), order, b, nb, part, me)
        sum_ref[:, lane_block(index_ref[b, 0])] += lax.dot_general(
            picked_ref[:, b * LANES : (b + 1) * LANES],
            block_ref[b],
            (((1,), (1,)), ((), ())),
            preferred_element_type=F32,
        )
    out_ref[...] = sum_ref[...].astype(BF16)


def final(block_index, picked, near, far, keeps, recvs, nt):
    nb = block_index.shape[0]
    chunks = len(keeps)
    rows, width = keeps[0].shape
    return pl.pallas_call(
        functools.partial(final_kernel, nt, nb, chunks),
        out_shape=jax.ShapeDtypeStruct((rows, width * chunks), BF16),
        in_specs=smem() + vmem(3 + 2 * chunks),
        out_specs=pl.BlockSpec(memory_space=pltpu.VMEM),
        scratch_shapes=[
            pltpu.VMEM((rows, width * chunks), F32),
            pltpu.VMEM((nb, HEAD_DIM, HEAD_DIM), BF16),
        ],
        compiler_params=params(),
        name="final",
    )(block_index, picked, near, far, *keeps, *recvs)


def on_device(tokens, base_weight, out_grad, block_index, block_owner, delta, moment1, moment2):
    nt = lax.axis_size("tensor")
    nd = lax.axis_size("dp")
    cap = delta.shape[0]
    part = HEAD_DIM // nt
    outer = bits_of(nt)[1:]

    gathered = [tokens]
    for bit in outer:
        gathered = gathered + [xor_permute(x, "tensor", bit) for x in gathered]
    gathered = gathered + [xor_permute(x, "tensor", 1) for x in gathered]

    perm, *pieces = picks(block_index, out_grad, nt)
    pieces = [pieces[0]] + [xor_permute(pieces[j], "tensor", j) for j in range(1, nt)]

    picked, keep, send = block_grads(block_index, block_owner, tokens, pieces, nt, nd, cap)
    recv = xor_permute(send, "tensor", 1)
    keep, send = first_step(keep, recv, delta)
    dp_bits = bits_of(nd)
    for bit in dp_bits[:-1]:
        recv = xor_permute(send, "dp", bit)
        keep, send = step(keep, send, recv)
    recv = xor_permute(send, "dp", dp_bits[-1])
    keep, send = compact(block_owner, keep, send, recv, cap, part)
    for bit in outer[:-1]:
        recv = xor_permute(send, "tensor", bit)
        keep, send = step(keep, send, recv)
    recv = xor_permute(send, "tensor", outer[-1])
    near, new_delta, first_new, second_new = adam(keep, send, recv, delta, moment1, moment2)
    far = xor_permute(near, "tensor", 1)

    keeps, recvs = [], []
    for chunk in range(BACK_CHUNKS):
        keep, send = back(perm, base_weight, chunk)
        for bit in bits_of(nt)[:-1]:
            keep, send = merge(keep, xor_permute(send, "tensor", bit))
        keeps.append(keep)
        recvs.append(xor_permute(send, "tensor", bits_of(nt)[-1]))

    projected = forward(block_index, gathered, near, far, base_weight, nt)
    input_grad = final(block_index, picked, near, far, keeps, recvs, nt)
    return (projected, input_grad, new_delta, first_new, second_new)


def solution(mesh):
    placed = (
        P(("dp", "tensor"), None),
        P(None, "tensor"),
        P("dp", "tensor"),
        P(),
        P(),
        P("dp", "tensor"),
        P("dp", "tensor"),
        P("dp", "tensor"),
    )
    return jax.shard_map(
        on_device,
        mesh=mesh,
        in_specs=placed,
        out_specs=(
            P("dp", "tensor"),
            P(("dp", "tensor"), None),
            P("dp", "tensor"),
            P("dp", "tensor"),
            P("dp", "tensor"),
        ),
        check_vma=False,
    )
```

time: 209 us -> 74.8 us (0.36)
  waiting for transfers between devices: 98 us -> 19.2 us
  blocking collectives: 37.4 us -> 0 us
  Pallas kernels: 0 us -> 35.5 us
  matrix products: 26.3 us -> 0 us
  local copies, waits for them, and re-layouts: 21.8 us -> 1.72 us
  starting transfers between devices: 0.34 us -> 17.1 us
  between operations: 14.6 us -> 0.74 us
  other arithmetic: 9.68 us -> 0 us
    unnamed x6 -> x0, waiting for transfers between devices: 44.2 us -> none
    all_gather x2 -> x0, blocking collectives: 37.4 us -> none  [the longest x1 32.1 us: on_device(): all_blocks = lax.all_gather(whole_rows, 'dp', axis=0, tiled=True)]
    pallas_call x0 -> x13, Pallas kernels: none -> 35.5 us  [the longest x2 15.3 us: back(): pl.pallas_call(back_kernel, grid=(steps,), out_shape=[half, half], in_spe...]
    reduce_scatter x1 -> x0, waiting for transfers between devices: 32.1 us -> none  [on_device(): lax.psum_scatter((base_back + row_spread.reshape(row_count, D)).astype(jn...]
    dot_general x5 -> x0, matrix products: 26.3 us -> none  [the longest x1 15.2 us: on_device(): lax.dot_general(out_grad, base_weight, (((1,), (1,)), ((), ())), preferre...]
    all_gather x1 -> x0, waiting for transfers between devices: 21.8 us -> none  [on_device(): gathered = lax.all_gather(tokens, 'tensor', axis=0, tiled=True)]
    ppermute x0 -> x16, waiting for transfers between devices: none -> 19.2 us  [xor_permute(): return lax.ppermute(x, axis, [(i, i ^ bit) for i in range(count)])]
    ppermute x0 -> x16, starting transfers between devices: none -> 17.1 us  [xor_permute(): return lax.ppermute(x, axis, [(i, i ^ bit) for i in range(count)])]
  transfers between devices with their start and end apart: 4 -> 16, of which waited for: 4 -> 6; matrix products, arithmetic and copies ran while one was open for 21% -> 1% of each run, Pallas kernels for 0% -> 27%
where the time goes in v1:
time: 74.8 us; the launch traced here: 74.2 us
  Pallas kernels  35.5 us (47%)
  waiting for transfers between devices  19.2 us (26%)
  starting transfers between devices  17.1 us (23%)
  local copies, waits for them, and re-layouts  1.72 us (2%)
    ppermute x16, waiting for transfers between devices, xor_permute(): return lax.ppermute(x, axis, [(i, i ^ bit) for i in range(count)])  19.2 us
    ppermute x16, starting transfers between devices, xor_permute(): return lax.ppermute(x, axis, [(i, i ^ bit) for i in range(count)])  17.1 us
    pallas_call x2, Pallas kernels, back(): pl.pallas_call(back_kernel, grid=(steps,), out_shape=[half, half], in_spe...  15.3 us
    pallas_call x1, Pallas kernels, forward(): pl.pallas_call(functools.partial(forward_kernel, nt, nb, steps), grid=(st...  15.1 us
    pallas_call x1, Pallas kernels, final(): pl.pallas_call(functools.partial(final_kernel, nt, nb, chunks), out_shape...  1.75 us
    unnamed x13, local copies, waits for them, and re-layouts  1.72 us
  transfers between devices with their start and end apart: 16, of which 6 were waited for; matrix products, arithmetic and copies ran while one was open for 1% of the time, Pallas kernels for 27%

profile of v1, /device:TPU:0, one launch (start us, length us, event | category | flops | bytes accessed | tf_op | source)
XLA Modules:
  0.0 74.2 jit_solution(1255036958165249906)
XLA Ops:
  0.6 3.0 %collective-permute-start = (bf16[32,8192]{1,0:T(8,128)(2,1)}, bf16[32,8192]{1,0:T(8,128)(2,1)S(1)}, u32[]{:S(2)}, u32[]{:S(2)}) collective-permute-start(bf16[32,8192]{1,0:T(8,128)(2,1)} %refs_0_.1), channel_id=1, source_target_pairs={{0,2},{1,3},{2,0},{3,1},{4,6},{5,7},{6,4},{7,5},{8,10},{9,11},{10,... | collective-permute-start | bytes 1572872 | tf_op jit(solution)/shard_map/ppermute | solution.py:49
  3.6 0.8 %copy.15.index_ref = s32[8,2]{1,0:T(8,128)S(1)} copy(s32[8,2]{0,1:T(2,128)} %param.11) | data formatting | bytes 128 | tf_op args[3]
  4.4 0.9 %copy-done.1 = bf16[128,1024]{1,0:T(8,128)(2,1)S(1)} copy-done((bf16[128,1024]{1,0:T(8,128)(2,1)S(1)}, bf16[128,1024]{1,0:T(8,128)(2,1)}, u32[]{:S(2)}) %copy-start.1) | copy-done | bytes 262168
  5.4 0.7 picks.1
  6.1 0.1 collective-permute-start.4
  6.3 1.7 %collective-permute-start.5 = (bf16[32,1024]{1,0:T(8,128)(2,1)S(1)}, bf16[32,1024]{1,0:T(8,128)(2,1)S(1)}, u32[]{:S(2)}, u32[]{:S(2)}) collective-permute-start(bf16[32,1024]{1,0:T(8,128)(2,1)S(1)} %get-tuple-element.36), channel_id=1, source_target_pairs={{0,3},{1,2},{2,1},{3,0},{4,7},{5,6},{6,5},{7,4},{8,11},{9,10},{10,... | collective-permute-start | bytes 196616 | tf_op jit(solution)/shard_map/ppermute | solution.py:49
  8.0 7.7 %back.2 = (bf16[64,4096]{1,0:T(8,128)(2,1)S(1)}, bf16[64,4096]{1,0:T(8,128)(2,1)S(1)}) custom-call(bf16[128,1024]{1,0:T(8,128)(2,1)S(1)} %get-tuple-element.49.grad_ref, bf16[8192,1024]{1,0:T(8,128)(2,1)} %weight_ref.3), custom_call_target="tpu_custom_call" | custom-call | flops 1073741824 | bytes 9437184 | tf_op jit(solution)/shard_map/back/pallas_call | solution.py:303
  15.7 0.4 collective-permute-start.12
  16.1 1.8 %collective-permute-done.4.refs_2_ = bf16[32,1024]{1,0:T(8,128)(2,1)S(1)} collective-permute-done((bf16[32,1024]{1,0:T(8,128)(2,1)S(1)}, bf16[32,1024]{1,0:T(8,128)(2,1)S(1)}, u32[]{:S(2)}, u32[]{:S(2)}) %collective-permute-start.4) | collective-permute-done | bytes 65568 | tf_op jit(solution)/shard_map/ppermute | solution.py:49
  17.9 0.9 %block_grads.1 = (bf16[32,1024]{1,0:T(8,128)(2,1)S(1)}, bf16[1024,128]{1,0:T(8,128)(2,1)S(1)}, bf16[1024,128]{1,0:T(8,128)(2,1)S(1)}) custom-call(s32[8,2]{1,0:T(8,128)S(1)} %copy.15.index_ref, s32[8]{0:T(128)S(1)} %copy-done.5, bf16[32,8192]{1,0:T(8,128)(2,1)S(1)} %copy-done, bf16[32,1024]{1,0:T(8,128)(2,1)S(1)} %get-tuple-element.33.refs_0_, ...), custom_call_target="tpu_custom_call" | custom-call | tf_op jit(solution)/shard_map/block_grads/pallas_call | solution.py:142
  18.8 0.6 collective-permute-start.6
  19.4 7.7 %back.3 = (bf16[64,4096]{1,0:T(8,128)(2,1)S(1)}, bf16[64,4096]{1,0:T(8,128)(2,1)S(1)}) custom-call(bf16[128,1024]{1,0:T(8,128)(2,1)S(1)} %get-tuple-element.49.grad_ref, bf16[8192,1024]{1,0:T(8,128)(2,1)} %weight_ref.3), custom_call_target="tpu_custom_call" | custom-call | flops 1073741824 | bytes 9437184 | tf_op jit(solution)/shard_map/back/pallas_call | solution.py:303
  27.1 0.1 collective-permute-start.13
  27.2 1.8 %collective-permute-start.7 = (bf16[576,128]{1,0:T(8,128)(2,1)S(1)}, bf16[576,128]{1,0:T(8,128)(2,1)S(1)}, u32[]{:S(2)}, u32[]{:S(2)}) collective-permute-start(bf16[576,128]{1,0:T(8,128)(2,1)S(1)} %get-tuple-element.40.sent_ref), channel_id=1, source_target_pairs={{0,4},{4,0},{8,12},{12,8},{16,20},{20,16},{24,28},{28,24},{1,5},{5... | collective-permute-start | bytes 442376 | tf_op jit(solution)/shard_map/ppermute | solution.py:49
  29.1 0.2 collective-permute-start.1
  29.3 0.3 collective-permute-start.2
  29.6 4.0 %collective-permute-done.7.recv_ref = bf16[576,128]{1,0:T(8,128)(2,1)S(1)} collective-permute-done((bf16[576,128]{1,0:T(8,128)(2,1)S(1)}, bf16[576,128]{1,0:T(8,128)(2,1)S(1)}, u32[]{:S(2)}, u32[]{:S(2)}) %collective-permute-start.7) | collective-permute-done | bytes 147488 | tf_op jit(solution)/shard_map/ppermute | solution.py:49
  33.6 1.9 %collective-permute-start.8 = (bf16[384,128]{1,0:T(8,128)(2,1)S(1)}, bf16[384,128]{1,0:T(8,128)(2,1)S(1)}, u32[]{:S(2)}, u32[]{:S(2)}) collective-permute-start(bf16[384,128]{1,0:T(8,128)(2,1)S(1)} %get-tuple-element.42.sent_ref), channel_id=1, source_target_pairs={{0,8},{4,12},{8,0},{12,4},{16,24},{20,28},{24,16},{28,20},{1,9},{5... | collective-permute-start | bytes 294920 | tf_op jit(solution)/shard_map/ppermute | solution.py:49
  35.5 2.8 %collective-permute-done.8.recv_ref = bf16[384,128]{1,0:T(8,128)(2,1)S(1)} collective-permute-done((bf16[384,128]{1,0:T(8,128)(2,1)S(1)}, bf16[384,128]{1,0:T(8,128)(2,1)S(1)}, u32[]{:S(2)}, u32[]{:S(2)}) %collective-permute-start.8) | collective-permute-done | bytes 98336 | tf_op jit(solution)/shard_map/ppermute | solution.py:49
  38.3 2.9 %collective-permute-start.9 = (bf16[384,128]{1,0:T(8,128)(2,1)S(1)}, bf16[384,128]{1,0:T(8,128)(2,1)S(1)}, u32[]{:S(2)}, u32[]{:S(2)}) collective-permute-start(bf16[384,128]{1,0:T(8,128)(2,1)S(1)} %get-tuple-element.44.sent_ref), channel_id=1, source_target_pairs={{0,16},{4,20},{8,24},{12,28},{16,0},{20,4},{24,8},{28,12},{1,17},{... | collective-permute-start | bytes 294920 | tf_op jit(solution)/shard_map/ppermute | solution.py:49
  41.2 0.1 merge.2
  41.3 1.6 %collective-permute-start.14 = (bf16[32,4096]{1,0:T(8,128)(2,1)S(1)}, bf16[32,4096]{1,0:T(8,128)(2,1)S(1)}, u32[]{:S(2)}, u32[]{:S(2)}) collective-permute-start(bf16[32,4096]{1,0:T(8,128)(2,1)S(1)} %get-tuple-element.56), channel_id=1, source_target_pairs={{0,2},{1,3},{2,0},{3,1},{4,6},{5,7},{6,4},{7,5},{8,10},{9,11},{10,... | collective-permute-start | bytes 786440 | tf_op jit(solution)/shard_map/ppermute | solution.py:49
  42.9 0.1 merge.3
  43.0 0.6 collective-permute-start.15
  43.6 0.3 collective-permute-done.9.recv_ref
  43.9 0.6 compact_step.1
  44.5 1.8 %collective-permute-start.10 = (bf16[320,128]{1,0:T(8,128)(2,1)S(1)}, bf16[320,128]{1,0:T(8,128)(2,1)S(1)}, u32[]{:S(2)}, u32[]{:S(2)}) collective-permute-start(bf16[320,128]{1,0:T(8,128)(2,1)S(1)} %get-tuple-element.46.sent_ref), channel_id=1, source_target_pairs={{0,2},{1,3},{2,0},{3,1},{4,6},{5,7},{6,4},{7,5},{8,10},{9,11},{10,... | collective-permute-start | bytes 245768 | tf_op jit(solution)/shard_map/ppermute | solution.py:49
  46.3 8.9 %collective-permute-done.10.recv_ref = bf16[320,128]{1,0:T(8,128)(2,1)S(1)} collective-permute-done((bf16[320,128]{1,0:T(8,128)(2,1)S(1)}, bf16[320,128]{1,0:T(8,128)(2,1)S(1)}, u32[]{:S(2)}, u32[]{:S(2)}) %collective-permute-start.10) | collective-permute-done | bytes 81952 | tf_op jit(solution)/shard_map/ppermute | solution.py:49
  55.2 0.7 adam.1
  55.9 1.3 %collective-permute-done.11.refs_5_.far_ref = bf16[512,128]{1,0:T(8,128)(2,1)S(1)} collective-permute-done((bf16[512,128]{1,0:T(8,128)(2,1)S(1)}, bf16[512,128]{1,0:T(8,128)(2,1)S(1)}, u32[]{:S(2)}, u32[]{:S(2)}) %collective-permute-start.11) | collective-permute-done | bytes 131104 | tf_op jit(solution)/shard_map/ppermute | solution.py:49
  57.3 1.8 %final.1 = bf16[32,8192]{1,0:T(8,128)(2,1)} custom-call(s32[8,2]{1,0:T(8,128)S(1)} %copy.15.index_ref, bf16[32,1024]{1,0:T(8,128)(2,1)S(1)} %get-tuple-element.48.picked_ref, bf16[512,128]{1,0:T(8,128)(2,1)S(1)} %get-tuple-element.47.refs_4_.near_ref, bf16[512,128]{1,0:T(8,128)(2,1)S(1)} %collective-permute-done.11.refs_5_.far_ref, ...), custom_call_target="tpu_custom_call" | custom-call | tf_op jit(solution)/shard_map/final/pallas_call | solution.py:443
  59.0 15.1 %forward.1 = bf16[128,1024]{1,0:T(8,128)(2,1)} custom-call(s32[8,2]{1,0:T(8,128)S(1)} %copy.15.index_ref, bf16[32,8192]{1,0:T(8,128)(2,1)S(1)} %copy-done, bf16[32,8192]{1,0:T(8,128)(2,1)S(1)} %collective-permute-done.refs_1_, bf16[32,8192]{1,0:T(8,128)(2,1)S(1)} %collective-permute-done.1.refs_2_, bf16[32,8192]{1,0:T(8,128)(2,1)S(1)} %collective-permute-done.2.refs_3_, ...), custom_call_target="tpu_custom_call" | custom-call | flops 2147483648 | bytes 18874368 | tf_op jit(solution)/shard_map/forward/pallas_call | solution.py:401
  (26 shorter events, 0.3 us)
Async XLA Ops:
  0.6 17.3 %copy-start = (bf16[32,8192]{1,0:T(8,128)(2,1)S(1)}, bf16[32,8192]{1,0:T(8,128)(2,1)}, u32[]{:S(2)}) copy-start(bf16[32,8192]{1,0:T(8,128)(2,1)} %refs_0_.1) | copy-start | bytes 1572868
  0.6 28.6 %collective-permute-start = (bf16[32,8192]{1,0:T(8,128)(2,1)}, bf16[32,8192]{1,0:T(8,128)(2,1)S(1)}, u32[]{:S(2)}, u32[]{:S(2)}) collective-permute-start(bf16[32,8192]{1,0:T(8,128)(2,1)} %refs_0_.1), channel_id=1, source_target_pairs={{0,2},{1,3},{2,0},{3,1},{4,6},{5,7},{6,4},{7,5},{8,10},{9,11},{10,... | collective-permute-start | bytes 1572872 | tf_op jit(solution)/shard_map/ppermute | solution.py:49
  4.4 0.9 %copy-start.1 = (bf16[128,1024]{1,0:T(8,128)(2,1)S(1)}, bf16[128,1024]{1,0:T(8,128)(2,1)}, u32[]{:S(2)}) copy-start(bf16[128,1024]{1,0:T(8,128)(2,1)} %grad_ref.1) | copy-start | bytes 786436
  5.3 12.5 %copy-start.5 = (s32[8]{0:T(128)S(1)}, s32[8]{0:T(128)}, u32[]{:S(2)}) copy-start(s32[8]{0:T(128)} %owner_ref.3) | copy-start | bytes 100
  6.1 10.0 %collective-permute-start.3 = (bf16[32,1024]{1,0:T(8,128)(2,1)S(1)}, bf16[32,1024]{1,0:T(8,128)(2,1)S(1)}, u32[]{:S(2)}, u32[]{:S(2)}) collective-permute-start(bf16[32,1024]{1,0:T(8,128)(2,1)S(1)} %get-tuple-element.34), channel_id=1, source_target_pairs={{0,1},{1,0},{2,3},{3,2},{4,5},{5,4},{6,7},{7,6},{8,9},{9,8},{10,11... | collective-permute-start | bytes 196616 | tf_op jit(solution)/shard_map/ppermute | solution.py:49
  6.1 11.7 %collective-permute-start.4 = (bf16[32,1024]{1,0:T(8,128)(2,1)S(1)}, bf16[32,1024]{1,0:T(8,128)(2,1)S(1)}, u32[]{:S(2)}, u32[]{:S(2)}) collective-permute-start(bf16[32,1024]{1,0:T(8,128)(2,1)S(1)} %get-tuple-element.35), channel_id=1, source_target_pairs={{0,2},{1,3},{2,0},{3,1},{4,6},{5,7},{6,4},{7,5},{8,10},{9,11},{10,... | collective-permute-start | bytes 196616 | tf_op jit(solution)/shard_map/ppermute | solution.py:49
  6.3 11.6 %collective-permute-start.5 = (bf16[32,1024]{1,0:T(8,128)(2,1)S(1)}, bf16[32,1024]{1,0:T(8,128)(2,1)S(1)}, u32[]{:S(2)}, u32[]{:S(2)}) collective-permute-start(bf16[32,1024]{1,0:T(8,128)(2,1)S(1)} %get-tuple-element.36), channel_id=1, source_target_pairs={{0,3},{1,2},{2,1},{3,0},{4,7},{5,6},{6,5},{7,4},{8,11},{9,10},{10,... | collective-permute-start | bytes 196616 | tf_op jit(solution)/shard_map/ppermute | solution.py:49
  8.0 19.1 %copy-start.2 = (bf16[2,4096]{1,0:T(2,128)(2,1)S(1)}, bf16[2,4096]{1,0:T(2,128)(2,1)}, u32[]{:S(2)}) copy-start(bf16[2,4096]{1,0:T(2,128)(2,1)} %delta_ref.3) | copy-start | bytes 49156
  8.0 47.2 %copy-start.3 = (f32[2,4096]{1,0:T(2,128)S(1)}, f32[2,4096]{1,0:T(2,128)}, u32[]{:S(2)}) copy-start(f32[2,4096]{1,0:T(2,128)} %one_ref.1) | copy-start | bytes 98308
  8.0 47.2 %copy-start.4 = (f32[2,4096]{1,0:T(2,128)S(1)}, f32[2,4096]{1,0:T(2,128)}, u32[]{:S(2)}) copy-start(f32[2,4096]{1,0:T(2,128)} %two_ref.1) | copy-start | bytes 98308
  15.7 25.5 %collective-permute-start.12 = (bf16[64,4096]{1,0:T(8,128)(2,1)S(1)}, bf16[64,4096]{1,0:T(8,128)(2,1)S(1)}, u32[]{:S(2)}, u32[]{:S(2)}) collective-permute-start(bf16[64,4096]{1,0:T(8,128)(2,1)S(1)} %get-tuple-element.51), channel_id=1, source_target_pairs={{0,1},{1,0},{2,3},{3,2},{4,5},{5,4},{6,7},{7,6},{8,9},{9,8},{10,11... | collective-permute-start | bytes 1572872 | tf_op jit(solution)/shard_map/ppermute | solution.py:49
  18.8 8.3 %collective-permute-start.6 = (bf16[1024,128]{1,0:T(8,128)(2,1)S(1)}, bf16[1024,128]{1,0:T(8,128)(2,1)S(1)}, u32[]{:S(2)}, u32[]{:S(2)}) collective-permute-start(bf16[1024,128]{1,0:T(8,128)(2,1)S(1)} %get-tuple-element.38), channel_id=1, source_target_pairs={{0,1},{1,0},{2,3},{3,2},{4,5},{5,4},{6,7},{7,6},{8,9},{9,8},{10,11... | collective-permute-start | bytes 786440 | tf_op jit(solution)/shard_map/ppermute | solution.py:49
  27.1 15.8 %collective-permute-start.13 = (bf16[64,4096]{1,0:T(8,128)(2,1)S(1)}, bf16[64,4096]{1,0:T(8,128)(2,1)S(1)}, u32[]{:S(2)}, u32[]{:S(2)}) collective-permute-start(bf16[64,4096]{1,0:T(8,128)(2,1)S(1)} %get-tuple-element.54), channel_id=1, source_target_pairs={{0,1},{1,0},{2,3},{3,2},{4,5},{5,4},{6,7},{7,6},{8,9},{9,8},{10,11... | collective-permute-start | bytes 1572872 | tf_op jit(solution)/shard_map/ppermute | solution.py:49
  27.2 6.3 %collective-permute-start.7 = (bf16[576,128]{1,0:T(8,128)(2,1)S(1)}, bf16[576,128]{1,0:T(8,128)(2,1)S(1)}, u32[]{:S(2)}, u32[]{:S(2)}) collective-permute-start(bf16[576,128]{1,0:T(8,128)(2,1)S(1)} %get-tuple-element.40.sent_ref), channel_id=1, source_target_pairs={{0,4},{4,0},{8,12},{12,8},{16,20},{20,16},{24,28},{28,24},{1,5},{5... | collective-permute-start | bytes 442376 | tf_op jit(solution)/shard_map/ppermute | solution.py:49
  29.1 29.9 %collective-permute-start.1 = (bf16[32,8192]{1,0:T(8,128)(2,1)S(1)}, bf16[32,8192]{1,0:T(8,128)(2,1)S(1)}, u32[]{:S(2)}, u32[]{:S(2)}) collective-permute-start(bf16[32,8192]{1,0:T(8,128)(2,1)S(1)} %copy-done), channel_id=1, source_target_pairs={{0,1},{1,0},{2,3},{3,2},{4,5},{5,4},{6,7},{7,6},{8,9},{9,8},{10,11... | collective-permute-start | bytes 1572872 | tf_op jit(solution)/shard_map/ppermute | solution.py:49
  29.3 29.7 %collective-permute-start.2 = (bf16[32,8192]{1,0:T(8,128)(2,1)S(1)}, bf16[32,8192]{1,0:T(8,128)(2,1)S(1)}, u32[]{:S(2)}, u32[]{:S(2)}) collective-permute-start(bf16[32,8192]{1,0:T(8,128)(2,1)S(1)} %collective-permute-done.refs_1_), channel_id=1, source_target_pairs={{0,1},{1,0},{2,3},{3,2},{4,5},{5,4},{6,7},{7,6},{8,9},{9,8},{10,11... | collective-permute-start | bytes 1572872 | tf_op jit(solution)/shard_map/ppermute | solution.py:49
  33.6 4.7 %collective-permute-start.8 = (bf16[384,128]{1,0:T(8,128)(2,1)S(1)}, bf16[384,128]{1,0:T(8,128)(2,1)S(1)}, u32[]{:S(2)}, u32[]{:S(2)}) collective-permute-start(bf16[384,128]{1,0:T(8,128)(2,1)S(1)} %get-tuple-element.42.sent_ref), channel_id=1, source_target_pairs={{0,8},{4,12},{8,0},{12,4},{16,24},{20,28},{24,16},{28,20},{1,9},{5... | collective-permute-start | bytes 294920 | tf_op jit(solution)/shard_map/ppermute | solution.py:49
  38.3 5.6 %collective-permute-start.9 = (bf16[384,128]{1,0:T(8,128)(2,1)S(1)}, bf16[384,128]{1,0:T(8,128)(2,1)S(1)}, u32[]{:S(2)}, u32[]{:S(2)}) collective-permute-start(bf16[384,128]{1,0:T(8,128)(2,1)S(1)} %get-tuple-element.44.sent_ref), channel_id=1, source_target_pairs={{0,16},{4,20},{8,24},{12,28},{16,0},{20,4},{24,8},{28,12},{1,17},{... | collective-permute-start | bytes 294920 | tf_op jit(solution)/shard_map/ppermute | solution.py:49
  41.3 14.6 %collective-permute-start.14 = (bf16[32,4096]{1,0:T(8,128)(2,1)S(1)}, bf16[32,4096]{1,0:T(8,128)(2,1)S(1)}, u32[]{:S(2)}, u32[]{:S(2)}) collective-permute-start(bf16[32,4096]{1,0:T(8,128)(2,1)S(1)} %get-tuple-element.56), channel_id=1, source_target_pairs={{0,2},{1,3},{2,0},{3,1},{4,6},{5,7},{6,4},{7,5},{8,10},{9,11},{10,... | collective-permute-start | bytes 786440 | tf_op jit(solution)/shard_map/ppermute | solution.py:49
  43.0 12.9 %collective-permute-start.15 = (bf16[32,4096]{1,0:T(8,128)(2,1)S(1)}, bf16[32,4096]{1,0:T(8,128)(2,1)S(1)}, u32[]{:S(2)}, u32[]{:S(2)}) collective-permute-start(bf16[32,4096]{1,0:T(8,128)(2,1)S(1)} %get-tuple-element.57), channel_id=1, source_target_pairs={{0,2},{1,3},{2,0},{3,1},{4,6},{5,7},{6,4},{7,5},{8,10},{9,11},{10,... | collective-permute-start | bytes 786440 | tf_op jit(solution)/shard_map/ppermute | solution.py:49
  44.5 10.7 %collective-permute-start.10 = (bf16[320,128]{1,0:T(8,128)(2,1)S(1)}, bf16[320,128]{1,0:T(8,128)(2,1)S(1)}, u32[]{:S(2)}, u32[]{:S(2)}) collective-permute-start(bf16[320,128]{1,0:T(8,128)(2,1)S(1)} %get-tuple-element.46.sent_ref), channel_id=1, source_target_pairs={{0,2},{1,3},{2,0},{3,1},{4,6},{5,7},{6,4},{7,5},{8,10},{9,11},{10,... | collective-permute-start | bytes 245768 | tf_op jit(solution)/shard_map/ppermute | solution.py:49
  55.9 1.3 %collective-permute-start.11 = (bf16[512,128]{1,0:T(8,128)(2,1)S(1)}, bf16[512,128]{1,0:T(8,128)(2,1)S(1)}, u32[]{:S(2)}, u32[]{:S(2)}) collective-permute-start(bf16[512,128]{1,0:T(8,128)(2,1)S(1)} %get-tuple-element.47.refs_4_.near_ref), channel_id=1, source_target_pairs={{0,1},{1,0},{2,3},{3,2},{4,5},{5,4},{6,7},{7,6},{8,9},{9,8},{10,11... | collective-permute-start | bytes 393224 | tf_op jit(solution)/shard_map/ppermute | solution.py:49

commit v2 on v0

v2 whole, which is shorter than its diff:
```python
import functools
import math

import jax
import jax.numpy as jnp
from jax import lax
from jax.experimental import pallas as pl
from jax.experimental.pallas import tpu as pltpu
from jax.sharding import PartitionSpec as P

HEAD_DIM = 128
LANES = 128
CORRECT_ONE = 1.0 - 0.9**10
CORRECT_TWO = 1.0 - 0.999**10
BF16 = jnp.bfloat16
F32 = jnp.float32
VMEM_LIMIT = 24 * 1024 * 1024
BACK_PIECES = 4
BACK_CHUNKS = 2
ORDER = (
    ("grad", 0), ("back", 0), ("grad", 1), ("back", 1), ("sum", 0), ("back", 2), ("grad", 2), ("relay", 0), ("back", 3), ("sum", 1), ("forward", 0), ("grad", 3), ("grad", 4), ("project", 0), ("correct", 0), ("adam", 0), ("final", 0),
)


def params():
    return pltpu.CompilerParams(vmem_limit_bytes=VMEM_LIMIT)


def cost(us):
    return pl.CostEstimate(flops=int(us * 1e9), bytes_accessed=int(us * 1e6), transcendentals=0)


def vmem(n=1):
    return [pl.BlockSpec(memory_space=pltpu.VMEM)] * n


def anywhere(deps):
    return [pl.BlockSpec(memory_space=pl.ANY)] * len(deps)


def with_deps(kernel, inputs, deps):
    def run(*refs):
        kernel(*refs[:inputs], *refs[inputs + len(deps) :])

    return run


def bits_of(count):
    return [1 << i for i in range(count.bit_length() - 1)]


def halving_order(count):
    order = [0]
    for bit in reversed(bits_of(count)):
        order = order + [j + bit for j in order]
    width = count.bit_length() - 1
    rev = lambda j: int(format(j, "0%db" % width)[::-1], 2) if width else 0
    return sorted(range(count), key=rev)


def gather_order(nt):
    order = [0]
    for bit in bits_of(nt)[1:] + [1]:
        order = order + [j ^ bit for j in order]
    return order


def xor_permute(x, axis, bit):
    count = lax.axis_size(axis)
    return lax.ppermute(x, axis, [(i, i ^ bit) for i in range(count)])


def slot_ranks(owners):
    ranks = []
    for b, owner in enumerate(owners):
        rank = jnp.int32(0)
        for before in owners[:b]:
            rank = rank + (before == owner).astype(jnp.int32)
        ranks.append(rank)
    return ranks


def scalars(ref, row, nb):
    table = ref[...]
    return [table[row, b] for b in range(nb)]


def place_of(offset, bits):
    place = jnp.int32(0)
    for i, bit in enumerate(bits):
        place = place + jnp.where((offset & bit) != 0, 1 << i, 0)
    return place


def lane_block(index):
    return pl.ds(pl.multiple_of(index * LANES, LANES), LANES)


def row_block(index, rows):
    return pl.ds(pl.multiple_of(index * rows, rows), rows)


def relay_kernel(count, *refs):
    for i in range(count):
        refs[count + i][...] = refs[i][...]


def relay(parts, deps):
    count = len(parts)
    return list(
        pl.pallas_call(
            with_deps(functools.partial(relay_kernel, count), count, deps),
            out_shape=[jax.ShapeDtypeStruct(x.shape, x.dtype) for x in parts],
            in_specs=vmem(count) + anywhere(deps),
            out_specs=vmem(count),
            compiler_params=params(),
            cost_estimate=cost(0.01),
            name="relay",
        )(*parts, *deps)
    )


def begin_kernel(out_ref):
    out_ref[...] = jnp.zeros_like(out_ref)


def begin():
    return pl.pallas_call(
        begin_kernel,
        out_shape=jax.ShapeDtypeStruct((8, LANES), F32),
        out_specs=pl.BlockSpec(memory_space=pltpu.VMEM),
        compiler_params=params(),
        cost_estimate=cost(30),
        name="begin",
    )()


def slab_kernel(nb, index_ref, tok_ref, delta_ref, out_ref):
    rows = tok_ref.shape[0]
    cap = delta_ref.shape[0]
    part = delta_ref.shape[1] // LANES
    delta = delta_ref[...].astype(F32)
    for k in range(cap):
        lines = [delta[k : k + 1, i * LANES : (i + 1) * LANES] for i in range(part)]
        start = nb * rows + k * part
        out_ref[start : start + part, :] = jnp.concatenate(lines, 0).astype(BF16)
    row_of = scalars(index_ref, 0, nb)
    for b in range(nb):
        out_ref[b * rows : (b + 1) * rows, :] = tok_ref[:, lane_block(row_of[b])]


def slabs(index, tokens, delta, deps):
    nb = index.shape[1]
    return pl.pallas_call(
        with_deps(functools.partial(slab_kernel, nb), 3, deps),
        out_shape=jax.ShapeDtypeStruct((nb * tokens.shape[0] + delta.size // LANES, LANES), BF16),
        in_specs=vmem(3) + anywhere(deps),
        out_specs=pl.BlockSpec(memory_space=pltpu.VMEM),
        compiler_params=params(),
        cost_estimate=cost(30),
        name="slabs",
    )(index, tokens, delta, *deps)


def spread_kernel(size, own_ref, recv_ref, slab_out, line_out):
    slab_out[:size, :] = own_ref[:size, :]
    slab_out[size : 2 * size, :] = recv_ref[:size, :]
    extra = own_ref.shape[0] - size
    line_out[:extra, :] = own_ref[size:, :]
    line_out[extra : 2 * extra, :] = recv_ref[size:, :]


def spread(own, recv, size, deps):
    extra = own.shape[0] - size
    return pl.pallas_call(
        with_deps(functools.partial(spread_kernel, size), 2, deps),
        out_shape=[
            jax.ShapeDtypeStruct((2 * size, LANES), BF16),
            jax.ShapeDtypeStruct((2 * extra, LANES), BF16),
        ],
        in_specs=vmem(2) + anywhere(deps),
        out_specs=vmem(2),
        compiler_params=params(),
        cost_estimate=cost(20),
        name="spread",
    )(own, recv, *deps)


def grad_kernel(
    nt, bits, nb, cap, scale, index_ref, owner_ref, near_ref, far_ref, grad_ref, keep_ref, send_ref, slab_ref, block_ref
):
    me = lax.axis_index("tensor")
    dp = lax.axis_index("dp")
    part = HEAD_DIM // nt
    rows = grad_ref.shape[0] // nt
    heads = grad_ref.shape[1] // HEAD_DIM
    half = nt // 2
    keep_ref[...] = jnp.zeros_like(keep_ref)
    send_ref[...] = jnp.zeros_like(send_ref)
    owners = scalars(owner_ref, 0, nb)
    ranks = slot_ranks(owners)
    head_of = scalars(index_ref, 1, nb)
    for b in range(nb):
        head = head_of[b]

        @pl.when(head // heads == me)
        def _():
            for p, j in enumerate(gather_order(nt)):
                source = near_ref if p < half else far_ref
                start = ((p % half) * nb + b) * rows
                slab_ref[row_block(me ^ j, rows), :] = source[start : start + rows, :]
            block_ref[...] = (
                lax.dot_general(
                    slab_ref[...],
                    grad_ref[:, lane_block(head - me * heads)],
                    (((0,), (0,)), ((), ())),
                    preferred_element_type=F32,
                )
                * scale
            ).astype(BF16)
            place = place_of(owners[b] ^ dp, bits[::-1])
            for p, j in enumerate(halving_order(nt)):
                target = keep_ref if p < half else send_ref
                start = ((place * half + p % half) * cap + ranks[b]) * part
                target[pl.ds(pl.multiple_of(start, part), part), :] = block_ref[row_block(me ^ j, part), :]


def block_grads(index, owner, near, far, out_grad, nt, bits, cap, deps):
    nb = index.shape[1]
    rows = out_grad.shape[0]
    nd = 1 << len(bits)
    scale = 1.0 / math.sqrt(rows * nd)
    size = nd * (nt // 2) * cap * (HEAD_DIM // nt)
    half = jax.ShapeDtypeStruct((size, LANES), BF16)
    return pl.pallas_call(
        with_deps(functools.partial(grad_kernel, nt, bits, nb, cap, scale), 5, deps),
        out_shape=[half, half],
        in_specs=vmem(5) + anywhere(deps),
        out_specs=vmem(2),
        scratch_shapes=[pltpu.VMEM((rows, LANES), BF16), pltpu.VMEM((HEAD_DIM, HEAD_DIM), BF16)],
        compiler_params=params(),
        cost_estimate=cost(0.01),
        name="block_grads",
    )(index, owner, near, far, out_grad, *deps)


def halve_kernel(keep_ref, recv_ref, keep_out, send_out):
    half = keep_out.shape[0]
    total = (keep_ref[...].astype(F32) + recv_ref[...].astype(F32)).astype(BF16)
    keep_out[...] = total[:half]
    send_out[...] = total[half:]


def halve(keep, recv, deps):
    rows = keep.shape[0]
    half = jax.ShapeDtypeStruct((rows // 2, LANES), BF16)
    return pl.pallas_call(
        with_deps(halve_kernel, 2, deps),
        out_shape=[half, half],
        in_specs=vmem(2) + anywhere(deps),
        out_specs=vmem(2),
        compiler_params=params(),
        cost_estimate=cost(0.01),
        name="halve",
    )(keep, recv, *deps)


def first_kernel(keep_ref, recv_ref, lines_ref, keep_out, send_out):
    half = keep_out.shape[0]
    total = (keep_ref[...].astype(F32) + recv_ref[...].astype(F32)).astype(BF16)
    keep_out[...] = total[:half]
    send_out[:half, :] = total[half:]
    send_out[half:, :] = lines_ref[...]


def first_step(keep, recv, lines, deps):
    half = keep.shape[0] // 2
    return pl.pallas_call(
        with_deps(first_kernel, 3, deps),
        out_shape=[
            jax.ShapeDtypeStruct((half, LANES), BF16),
            jax.ShapeDtypeStruct((half + lines.shape[0], LANES), BF16),
        ],
        in_specs=vmem(3) + anywhere(deps),
        out_specs=vmem(2),
        compiler_params=params(),
        cost_estimate=cost(0.01),
        name="first_step",
    )(keep, recv, lines, *deps)


def step_kernel(keep_ref, sent_ref, recv_ref, keep_out, send_out):
    rows = keep_ref.shape[0]
    half = rows // 2
    extra = sent_ref.shape[0] - rows
    total = (keep_ref[...].astype(F32) + recv_ref[:rows, :].astype(F32)).astype(BF16)
    keep_out[...] = total[:half]
    send_out[:half, :] = total[half:]
    send_out[half : half + extra, :] = sent_ref[rows:, :]
    send_out[half + extra :, :] = recv_ref[rows:, :]


def step(keep, sent, recv, deps):
    rows = keep.shape[0]
    extra = sent.shape[0] - rows
    return pl.pallas_call(
        with_deps(step_kernel, 3, deps),
        out_shape=[
            jax.ShapeDtypeStruct((rows // 2, LANES), BF16),
            jax.ShapeDtypeStruct((rows // 2 + 2 * extra, LANES), BF16),
        ],
        in_specs=vmem(3) + anywhere(deps),
        out_specs=vmem(2),
        compiler_params=params(),
        cost_estimate=cost(0.01),
        name="chain_step",
    )(keep, sent, recv, *deps)


def compact_kernel(bits, nb, cap, part, tensor, owner_ref, keep_ref, sent_ref, recv_ref, keep_out, send_out, out_ref, all_ref):
    dp = lax.axis_index("dp")
    rows = keep_ref.shape[0]
    half = rows // 2
    extra = sent_ref.shape[0] - rows
    total = (keep_ref[...].astype(F32) + recv_ref[:rows, :].astype(F32)).astype(BF16)
    keep_out[...] = total[:half]
    send_out[...] = total[half:]
    all_ref[:extra, :] = sent_ref[rows:, :]
    all_ref[extra:, :] = recv_ref[rows:, :]
    owners = scalars(owner_ref, 0, nb)
    ranks = slot_ranks(owners)
    for b in range(nb):
        place = place_of(owners[b] ^ dp, bits)
        for t in range(tensor):
            start = ((place * tensor + t) * cap + ranks[b]) * part
            out_ref[(t * nb + b) * part : (t * nb + b + 1) * part, :] = all_ref[
                pl.ds(pl.multiple_of(start, part), part), :
            ]


def compact(owner, keep, sent, recv, bits, cap, part, tensor, deps):
    nb = owner.shape[1]
    rows = keep.shape[0]
    half = jax.ShapeDtypeStruct((rows // 2, LANES), BF16)
    return pl.pallas_call(
        with_deps(functools.partial(compact_kernel, bits, nb, cap, part, tensor), 4, deps),
        out_shape=[half, half, jax.ShapeDtypeStruct((tensor * nb * part, LANES), BF16)],
        in_specs=vmem(4) + anywhere(deps),
        out_specs=vmem(3),
        scratch_shapes=[pltpu.VMEM((2 * (sent.shape[0] - rows), LANES), BF16)],
        compiler_params=params(),
        cost_estimate=cost(0.01),
        name="compact_step",
    )(owner, keep, sent, recv, *deps)


def adam_kernel(
    cap, keep_ref, recv_ref, delta_ref, one_ref, two_ref, delta_out, one_out, two_out, grad_ref
):
    part = keep_ref.shape[0] // cap
    total = keep_ref[...].astype(F32) + recv_ref[...].astype(F32)
    for k in range(cap):
        for i in range(part):
            grad_ref[k : k + 1, i * LANES : (i + 1) * LANES] = total[k * part + i : k * part + i + 1, :]
    grad = grad_ref[...]
    first = 0.9 * one_ref[...] + 0.1 * grad
    second = 0.999 * two_ref[...] + 0.001 * grad * grad
    one_out[...] = first
    two_out[...] = second
    update = 0.02 * (first / CORRECT_ONE) / (jnp.sqrt(second / CORRECT_TWO) + 1e-08)
    delta_out[...] = (delta_ref[...].astype(F32) - update).astype(BF16)


def adam(keep, recv, delta, moment1, moment2, deps):
    return pl.pallas_call(
        with_deps(functools.partial(adam_kernel, delta.shape[0]), 5, deps),
        out_shape=[
            jax.ShapeDtypeStruct(delta.shape, BF16),
            jax.ShapeDtypeStruct(delta.shape, F32),
            jax.ShapeDtypeStruct(delta.shape, F32),
        ],
        in_specs=vmem(5) + anywhere(deps),
        out_specs=vmem(3),
        scratch_shapes=[pltpu.VMEM(delta.shape, F32)],
        compiler_params=params(),
        cost_estimate=cost(0.01),
        name="adam",
    )(keep, recv, delta, moment1, moment2, *deps)


def back_kernel(nt, nb, start, width, index_ref, grad_ref, weight_ref, keep_ref, send_ref, perm_ref):
    me = lax.axis_index("tensor")
    rows = grad_ref.shape[0] // nt
    heads = grad_ref.shape[1] // HEAD_DIM
    half = nt // 2 * rows
    for p, j in enumerate(halving_order(nt)):
        perm_ref[p * rows : (p + 1) * rows, :] = grad_ref[row_block(me ^ j, rows), :]
    out = lax.dot_general(
        weight_ref[start : start + width, :], perm_ref[...], (((1,), (1,)), ((), ())), preferred_element_type=F32
    )
    out = out.astype(BF16).T
    keep_ref[:, :width] = out[:half]
    send_ref[:, :width] = out[half:]
    if keep_ref.shape[1] > width:
        head_of = scalars(index_ref, 1, nb)
        for b in range(nb):
            head = head_of[b]
            mine = head // heads == me
            part = perm_ref[:, lane_block(jnp.where(mine, head - me * heads, 0))]
            part = jnp.where(mine, part, jnp.zeros_like(part))
            cols = slice(width + b * LANES, width + (b + 1) * LANES)
            keep_ref[:, cols] = part[:half]
            send_ref[:, cols] = part[half:]


def back(index, out_grad, weight, piece, riders, nt, deps):
    nb = index.shape[1]
    rows = out_grad.shape[0]
    depth = weight.shape[0]
    width = depth // BACK_PIECES
    half = jax.ShapeDtypeStruct((rows // 2, width + (nb * LANES if riders else 0)), BF16)
    return pl.pallas_call(
        with_deps(functools.partial(back_kernel, nt, nb, piece * width, width), 3, deps),
        out_shape=[half, half],
        in_specs=vmem(3) + anywhere(deps),
        out_specs=vmem(2),
        scratch_shapes=[pltpu.VMEM(out_grad.shape, BF16)],
        compiler_params=params(),
        cost_estimate=cost(0.01),
        name="back",
    )(index, out_grad, weight, *deps)


def merge_kernel(count, *refs):
    keeps, recvs = refs[:count], refs[count : 2 * count]
    keep_out, send_out = refs[2 * count :]
    half = keep_out.shape[0]
    place = 0
    for keep_ref, recv_ref in zip(keeps, recvs):
        cols = slice(place, place + keep_ref.shape[1])
        place += keep_ref.shape[1]
        total = (keep_ref[...].astype(F32) + recv_ref[...].astype(F32)).astype(BF16)
        keep_out[:, cols] = total[:half]
        send_out[:, cols] = total[half:]


def merge(keeps, recvs, deps):
    count = len(keeps)
    half = jax.ShapeDtypeStruct((keeps[0].shape[0] // 2, sum(x.shape[1] for x in keeps)), BF16)
    return pl.pallas_call(
        with_deps(functools.partial(merge_kernel, count), 2 * count, deps),
        out_shape=[half, half],
        in_specs=vmem(2 * count) + anywhere(deps),
        out_specs=vmem(2),
        compiler_params=params(),
        cost_estimate=cost(0.01),
        name="merge",
    )(*keeps, *recvs, *deps)


def load_block(block_ref, halves, order, b, nb, part, me):
    per = len(order) // 2
    for p, j in enumerate(order):
        source = halves[p // per]
        start = ((p % per) * nb + b) * part
        block_ref[row_block(me ^ j, part), :] = source[start : start + part, :]


def forward_kernel(count, *refs):
    weight_ref, out_ref = refs[count:]
    tile = jnp.concatenate([ref[...] for ref in refs[:count]], axis=0)
    out_ref[...] = jnp.dot(tile, weight_ref[...], preferred_element_type=F32)


def forward(pieces, weight, deps):
    count = len(pieces)
    return pl.pallas_call(
        with_deps(functools.partial(forward_kernel, count), count + 1, deps),
        out_shape=jax.ShapeDtypeStruct((pieces[0].shape[0] * count, weight.shape[1]), F32),
        in_specs=vmem(count + 1) + anywhere(deps),
        out_specs=pl.BlockSpec(memory_space=pltpu.VMEM),
        compiler_params=params(),
        cost_estimate=cost(0.01),
        name="forward",
    )(*pieces, weight, *deps)


def project_kernel(nt, nb, index_ref, sum_ref, near_delta, far_delta, near_ref, far_ref, out_ref, acc_ref, block_ref, slab_ref):
    me = lax.axis_index("tensor")
    order = gather_order(nt)
    rows = sum_ref.shape[0] // nt
    heads = out_ref.shape[1] // HEAD_DIM
    part = HEAD_DIM // nt
    half = nt // 2
    acc_ref[...] = sum_ref[...]
    head_of = scalars(index_ref, 1, nb)
    for b in range(nb):
        head = head_of[b]

        @pl.when(head // heads == me)
        def _():
            load_block(block_ref, (near_delta, far_delta), order, b, nb, part, me)
            for p in range(nt):
                source = near_ref if p < half else far_ref
                start = ((p % half) * nb + b) * rows
                slab_ref[p * rows : (p + 1) * rows, :] = source[start : start + rows, :]
            cols = lane_block(head - me * heads)
            acc_ref[:, cols] += jnp.dot(slab_ref[...], block_ref[...], preferred_element_type=F32)

    for p, j in enumerate(order):
        out_ref[row_block(me ^ j, rows), :] = acc_ref[p * rows : (p + 1) * rows, :].astype(BF16)


def project(index, total, near_delta, far_delta, near, far, nt, deps):
    nb = index.shape[1]
    rows, cols = total.shape
    return pl.pallas_call(
        with_deps(functools.partial(project_kernel, nt, nb), 6, deps),
        out_shape=jax.ShapeDtypeStruct((rows, cols), BF16),
        in_specs=vmem(6) + anywhere(deps),
        out_specs=pl.BlockSpec(memory_space=pltpu.VMEM),
        scratch_shapes=[
            pltpu.VMEM((rows, cols), F32),
            pltpu.VMEM((HEAD_DIM, HEAD_DIM), BF16),
            pltpu.VMEM((rows, LANES), BF16),
        ],
        compiler_params=params(),
        cost_estimate=cost(0.01),
        name="project",
    )(index, total, near_delta, far_delta, near, far, *deps)


def correct_kernel(nt, nb, chunks, index_ref, near_ref, far_ref, *refs):
    keeps, recvs = refs[:chunks], refs[chunks : 2 * chunks - 1]
    out_ref, block_ref = refs[2 * chunks - 1 :]
    me = lax.axis_index("tensor")
    order = gather_order(nt)
    part = HEAD_DIM // nt
    width = out_ref.shape[1] // chunks
    for c in range(chunks):
        cols = slice(c * width, (c + 1) * width)
        own = keeps[c][:, :width].astype(F32)
        out_ref[:, cols] = own + recvs[c][:, :width].astype(F32) if c < chunks - 1 else own
    row_of = scalars(index_ref, 0, nb)
    for b in range(nb):
        load_block(block_ref.at[b], (near_ref, far_ref), order, b, nb, part, me)
        ride = slice(width + b * LANES, width + (b + 1) * LANES)
        pick = (keeps[0][:, ride].astype(F32) + recvs[0][:, ride].astype(F32)).astype(BF16)
        out_ref[:, lane_block(row_of[b])] += lax.dot_general(
            pick, block_ref[b], (((1,), (1,)), ((), ())), preferred_element_type=F32
        )


def correct(index, near, far, keeps, recvs, depth, nt, deps):
    nb = index.shape[1]
    chunks = len(keeps)
    rows = keeps[0].shape[0]
    return pl.pallas_call(
        with_deps(functools.partial(correct_kernel, nt, nb, chunks), 2 + 2 * chunks, deps),
        out_shape=jax.ShapeDtypeStruct((rows, depth), F32),
        in_specs=vmem(2 + 2 * chunks) + anywhere(deps),
        out_specs=pl.BlockSpec(memory_space=pltpu.VMEM),
        scratch_shapes=[pltpu.VMEM((nb, HEAD_DIM, HEAD_DIM), BF16)],
        compiler_params=params(),
        cost_estimate=cost(0.01),
        name="correct",
    )(index, near, far, *keeps, *recvs, *deps)


def final_kernel(sum_ref, recv_ref, out_ref):
    width = recv_ref.shape[1]
    done = out_ref.shape[1] - width
    out_ref[:, :done] = sum_ref[:, :done].astype(BF16)
    out_ref[:, done:] = (sum_ref[:, done:] + recv_ref[...].astype(F32)).astype(BF16)


def final(total, recv, deps):
    return pl.pallas_call(
        with_deps(final_kernel, 2, deps),
        out_shape=jax.ShapeDtypeStruct(total.shape, BF16),
        in_specs=vmem(2) + anywhere(deps),
        out_specs=pl.BlockSpec(memory_space=pltpu.VMEM),
        compiler_params=params(),
        cost_estimate=cost(0.01),
        name="final",
    )(total, recv, *deps)


def on_device(tokens, base_weight, out_grad, block_index, block_owner, delta, moment1, moment2):
    nt = lax.axis_size("tensor")
    nd = lax.axis_size("dp")
    cap = delta.shape[0]
    part = HEAD_DIM // nt
    outer = bits_of(nt)[1:]
    dp_bits = bits_of(nd)[:1] + bits_of(nd)[:0:-1]
    index = block_index.T
    owner = block_owner.reshape(1, -1)

    per = BACK_PIECES // BACK_CHUNKS
    steps = len(dp_bits)

    size = index.shape[1] * tokens.shape[0]
    own = slabs(index, tokens, delta, [begin()])
    for bit in outer:
        near_slabs, lines = spread(own, xor_permute(own, "tensor", bit), size, [])
        if bit != outer[-1]:
            own = jnp.concatenate([near_slabs, lines], 0)
            size *= 2
    far_slabs = xor_permute(near_slabs, "tensor", 1)
    crossed = [tokens]
    for bit in outer:
        crossed = crossed + [xor_permute(x, "tensor", bit) for x in crossed]
    far_tokens = xor_permute(tokens, "tensor", 1)

    pieces, sums = {}, {}
    grads = {}
    got = {}
    order = []

    def tie(array):
        order.append(array)

    def deps():
        return order[-1:]

    def task_back(i):
        keep, send = back(index, out_grad, base_weight, i, i == per - 1, nt, deps())
        tie(send)
        pieces[i] = (keep, xor_permute(send, "tensor", 1))

    def task_sum(c):
        group = range(c * per, (c + 1) * per)
        for i in group:
            need("back", i)
        keep, send = merge([pieces[i][0] for i in group], [pieces[i][1] for i in group], deps())
        tie(send)
        for bit in outer[:-1]:
            keep, send = merge([keep], [xor_permute(send, "tensor", bit)], [])
        sums[c] = (keep, xor_permute(send, "tensor", outer[-1]))

    def task_grad(i):
        if i == 0:
            keep, send = block_grads(index, owner, near_slabs, far_slabs, out_grad, nt, dp_bits, cap, deps())
            grads[i] = (keep, xor_permute(send, "tensor", 1))
        else:
            need("grad", i - 1)
            keep, *way = grads[i - 1]
            bit = (dp_bits + outer)[i - 1]
            axis = "dp" if i <= steps else "tensor"
            if i == 1:
                keep, send = first_step(keep, *way, lines, deps())
                grads[i] = (keep, send, xor_permute(send, axis, bit))
            elif i <= steps:
                keep, send = step(keep, *way, deps())
                grads[i] = (keep, send, xor_permute(send, axis, bit))
            elif i == steps + 1:
                keep, send, near = compact(owner, keep, *way, dp_bits, cap, part, nt // 2, deps())
                got["delta"] = (near, xor_permute(near, "tensor", 1))
                grads[i] = (keep, xor_permute(send, axis, bit))
            else:
                keep, send = halve(keep, *way, deps())
                grads[i] = (keep, xor_permute(send, axis, bit))
        tie(send)

    def task_relay(i):
        parts = relay(crossed[1:], deps())
        tie(parts[0])
        got["tokens"] = crossed[:1] + parts + [far_tokens] + [xor_permute(x, "tensor", 1) for x in parts]

    def task_forward(i):
        need("relay", 0)
        got["total"] = forward(got["tokens"], base_weight, deps())
        tie(got["total"])

    def task_project(i):
        need("grad", steps + 1)
        need("forward", 0)
        got["projected"] = project(index, got["total"], *got["delta"], near_slabs, far_slabs, nt, deps())

    def task_correct(i):
        need("grad", steps + 1)
        for c in range(BACK_CHUNKS):
            need("sum", c)
        keeps, recvs = zip(*[sums[c] for c in range(BACK_CHUNKS)])
        got["corrected"] = correct(index, *got["delta"], keeps, recvs[:-1], tokens.shape[1], nt, deps())
        tie(got["corrected"])

    def task_adam(i):
        need("grad", steps + len(outer))
        got["adam"] = adam(*grads[steps + len(outer)], delta, moment1, moment2, deps())

    def task_final(i):
        need("correct", 0)
        got["input_grad"] = final(got["corrected"], sums[BACK_CHUNKS - 1][1], deps())

    tasks = {
        "back": task_back, "sum": task_sum, "grad": task_grad, "relay": task_relay, "project": task_project,
        "forward": task_forward, "correct": task_correct, "adam": task_adam, "final": task_final,
    }
    run = set()

    def need(name, i):
        if (name, i) not in run:
            run.add((name, i))
            tasks[name](i)

    for name, i in ORDER:
        need(name, i)
    new_delta, first_new, second_new = got["adam"]
    return (got["projected"], got["input_grad"], new_delta, first_new, second_new)


def solution(mesh):
    placed = (
        P(("dp", "tensor"), None),
        P(None, "tensor"),
        P("dp", "tensor"),
        P(),
        P(),
        P("dp", "tensor"),
        P("dp", "tensor"),
        P("dp", "tensor"),
    )
    return jax.shard_map(
        on_device,
        mesh=mesh,
        in_specs=placed,
        out_specs=(
            P("dp", "tensor"),
            P(("dp", "tensor"), None),
            P("dp", "tensor"),
            P("dp", "tensor"),
            P("dp", "tensor"),
        ),
        check_vma=False,
    )
```

time: 209 us -> 47.5 us (0.23)
  waiting for transfers between devices: 98 us -> 17.8 us
  blocking collectives: 37.4 us -> 0 us
  matrix products: 26.3 us -> 0 us
  local copies, waits for them, and re-layouts: 21.8 us -> 1.08 us
  starting transfers between devices: 0.34 us -> 14.8 us
  between operations: 14.6 us -> 0.89 us
  Pallas kernels: 0 us -> 12.7 us
  other arithmetic: 9.68 us -> 0.01 us
    unnamed x6 -> x0, waiting for transfers between devices: 44.2 us -> none
    all_gather x2 -> x0, blocking collectives: 37.4 us -> none  [the longest x1 32.1 us: on_device(): all_blocks = lax.all_gather(whole_rows, 'dp', axis=0, tiled=True)]
    reduce_scatter x1 -> x0, waiting for transfers between devices: 32.1 us -> none  [on_device(): lax.psum_scatter((base_back + row_spread.reshape(row_count, D)).astype(jn...]
    dot_general x5 -> x0, matrix products: 26.3 us -> none  [the longest x1 15.2 us: on_device(): lax.dot_general(out_grad, base_weight, (((1,), (1,)), ((), ())), preferre...]
    all_gather x1 -> x0, waiting for transfers between devices: 21.8 us -> none  [on_device(): gathered = lax.all_gather(tokens, 'tensor', axis=0, tiled=True)]
    ppermute x0 -> x17, waiting for transfers between devices: none -> 17.8 us  [xor_permute(): return lax.ppermute(x, axis, [(i, i ^ bit) for i in range(count)])]
    ppermute x0 -> x17, starting transfers between devices: none -> 14.8 us  [xor_permute(): return lax.ppermute(x, axis, [(i, i ^ bit) for i in range(count)])]
    pallas_call x0 -> x20, Pallas kernels: none -> 12.7 us  [the longest x4 5.28 us: back(): pl.pallas_call(with_deps(functools.partial(back_kernel, nt, nb, piece * w...]
  transfers between devices with their start and end apart: 4 -> 17, of which waited for: 4 -> 8; matrix products, arithmetic and copies ran while one was open for 21% -> 0% of each run, Pallas kernels for 0% -> 23%
where the time goes in v2:
time: 47.5 us; the launch traced here: 47.3 us
  waiting for transfers between devices  17.8 us (37%)
  starting transfers between devices  14.8 us (31%)
  Pallas kernels  12.7 us (27%)
  local copies, waits for them, and re-layouts  1.08 us (2%)
  between operations  0.89 us (2%)
    ppermute x17, waiting for transfers between devices, xor_permute(): return lax.ppermute(x, axis, [(i, i ^ bit) for i in range(count)])  17.8 us
    ppermute x17, starting transfers between devices, xor_permute(): return lax.ppermute(x, axis, [(i, i ^ bit) for i in range(count)])  14.8 us
    pallas_call x4, Pallas kernels, back(): pl.pallas_call(with_deps(functools.partial(back_kernel, nt, nb, piece * w...  5.28 us
    pallas_call x1, Pallas kernels, forward(): pl.pallas_call(with_deps(functools.partial(forward_kernel, count), count...  2.33 us
    pallas_call x1, Pallas kernels, project(): pl.pallas_call(with_deps(functools.partial(project_kernel, nt, nb), 6, de...  1.45 us
    unnamed x22, local copies, waits for them, and re-layouts  1.08 us
    pallas_call x1, Pallas kernels, block_grads(): pl.pallas_call(with_deps(functools.partial(grad_kernel, nt, bits, nb, cap...  1.02 us
  transfers between devices with their start and end apart: 17, of which 8 were waited for; matrix products, arithmetic and copies ran while one was open for 0% of the time, Pallas kernels for 23%

profile of v2, /device:TPU:0, one launch (start us, length us, event | category | flops | bytes accessed | tf_op | source)
XLA Modules:
  0.0 47.3 jit_solution(3456894287606452284)
XLA Ops:
  0.7 0.6 %copy-done.2 = s32[8,2]{0,1:T(2,128)S(1)} copy-done((s32[8,2]{0,1:T(2,128)S(1)}, s32[8,2]{0,1:T(2,128)}, u32[]{:S(2)}) %copy-start.2) | copy-done | bytes 88
  1.4 0.3 copy-done.1
  1.9 3.0 %collective-permute-start.1 = (bf16[320,128]{1,0:T(8,128)(2,1)S(1)}, bf16[320,128]{1,0:T(8,128)(2,1)S(1)}, u32[]{:S(2)}, u32[]{:S(2)}) collective-permute-start(bf16[320,128]{1,0:T(8,128)(2,1)S(1)} %slabs.1.refs_0_), channel_id=1, source_target_pairs={{0,2},{1,3},{2,0},{3,1},{4,6},{5,7},{6,4},{7,5},{8,10},{9,11},{10,... | collective-permute-start | bytes 245768 | tf_op jit(solution)/shard_map/ppermute | solution.py:70
  4.9 2.4 %collective-permute-done.1.refs_1_ = bf16[320,128]{1,0:T(8,128)(2,1)S(1)} collective-permute-done((bf16[320,128]{1,0:T(8,128)(2,1)S(1)}, bf16[320,128]{1,0:T(8,128)(2,1)S(1)}, u32[]{:S(2)}, u32[]{:S(2)}) %collective-permute-start.1) | collective-permute-done | bytes 81952 | tf_op jit(solution)/shard_map/ppermute | solution.py:70
  7.4 1.3 %collective-permute-done.2.refs_3_.refs_5_ = bf16[512,128]{1,0:T(8,128)(2,1)S(1)} collective-permute-done((bf16[512,128]{1,0:T(8,128)(2,1)S(1)}, bf16[512,128]{1,0:T(8,128)(2,1)S(1)}, u32[]{:S(2)}, u32[]{:S(2)}) %collective-permute-start.2) | collective-permute-done | bytes 131104 | tf_op jit(solution)/shard_map/ppermute | solution.py:70
  8.8 1.0 %block_grads.1 = (bf16[1024,128]{1,0:T(8,128)(2,1)S(1)}, bf16[1024,128]{1,0:T(8,128)(2,1)S(1)}) custom-call(s32[2,8]{1,0:T(2,128)S(1)} %bitcast.5, s32[1,8]{1,0:T(1,128)S(1)} %bitcast.12, bf16[512,128]{1,0:T(8,128)(2,1)S(1)} %get-tuple-element.33.refs_2_.refs_4_, bf16[512,128]{1,0:T(8,128)(2,1)S(1)} %collective-permute-done.2.refs_3_.refs_5_, ...), custom_call_target="tpu_custom_call" | custom-call | flops 10000000 | bytes 10000 | tf_op jit(solution)/shard_map/block_grads/pallas_call | solution.py:235
  9.9 1.9 %collective-permute-start = (bf16[32,8192]{1,0:T(8,128)(2,1)S(1)}, bf16[32,8192]{1,0:T(8,128)(2,1)S(1)}, u32[]{:S(2)}, u32[]{:S(2)}) collective-permute-start(bf16[32,8192]{1,0:T(8,128)(2,1)S(1)} %copy-done.1), channel_id=1, source_target_pairs={{0,2},{1,3},{2,0},{3,1},{4,6},{5,7},{6,4},{7,5},{8,10},{9,11},{10,... | collective-permute-start | bytes 1572872 | tf_op jit(solution)/shard_map/ppermute | solution.py:70
  11.8 1.3 %back.4 = (bf16[64,2048]{1,0:T(8,128)(2,1)S(1)}, bf16[64,2048]{1,0:T(8,128)(2,1)S(1)}) custom-call(s32[2,8]{1,0:T(2,128)S(1)} %bitcast.6, bf16[128,1024]{1,0:T(8,128)(2,1)S(1)} %copy-done, bf16[8192,1024]{1,0:T(8,128)(2,1)S(1)} %bitcast.3, bf16[1024,128]{1,0:T(8,128)(2,1)S(1)} %get-tuple-element.35.refs_3_), custom_call_target="tpu_custom_call" | custom-call | flops 10000000 | bytes 10000 | tf_op jit(solution)/shard_map/back/pallas_call | solution.py:422
  13.2 1.3 %back.5 = (bf16[64,3072]{1,0:T(8,128)(2,1)S(1)}, bf16[64,3072]{1,0:T(8,128)(2,1)S(1)}) custom-call(s32[2,8]{1,0:T(2,128)S(1)} %bitcast.7, bf16[128,1024]{1,0:T(8,128)(2,1)S(1)} %copy-done, bf16[8192,1024]{1,0:T(8,128)(2,1)S(1)} %bitcast.3, bf16[640,128]{1,0:T(8,128)(2,1)S(1)} %get-tuple-element.39.refs_3_.refs_1_), custom_call_target="tpu_custom_call" | custom-call | flops 10000000 | bytes 10000 | tf_op jit(solution)/shard_map/back/pallas_call | solution.py:422
  14.7 0.5 %collective-permute-start.5 = (bf16[64,2048]{1,0:T(8,128)(2,1)S(1)}, bf16[64,2048]{1,0:T(8,128)(2,1)S(1)}, u32[]{:S(2)}, u32[]{:S(2)}) collective-permute-start(bf16[64,2048]{1,0:T(8,128)(2,1)S(1)} %get-tuple-element.37.refs_3_), channel_id=1, source_target_pairs={{0,1},{1,0},{2,3},{3,2},{4,5},{5,4},{6,7},{7,6},{8,9},{9,8},{10,11... | collective-permute-start | bytes 786440 | tf_op jit(solution)/shard_map/ppermute | solution.py:70
  15.2 1.5 %collective-permute-start.4 = (bf16[640,128]{1,0:T(8,128)(2,1)S(1)}, bf16[640,128]{1,0:T(8,128)(2,1)S(1)}, u32[]{:S(2)}, u32[]{:S(2)}) collective-permute-start(bf16[640,128]{1,0:T(8,128)(2,1)S(1)} %get-tuple-element.39.refs_3_.refs_1_), channel_id=1, source_target_pairs={{0,4},{4,0},{8,12},{12,8},{16,20},{20,16},{24,28},{28,24},{1,5},{5... | collective-permute-start | bytes 491528 | tf_op jit(solution)/shard_map/ppermute | solution.py:70
  16.8 0.2 merge.2
  16.9 1.3 %back.6 = (bf16[64,2048]{1,0:T(8,128)(2,1)S(1)}, bf16[64,2048]{1,0:T(8,128)(2,1)S(1)}) custom-call(s32[2,8]{1,0:T(2,128)S(1)} %bitcast.8, bf16[128,1024]{1,0:T(8,128)(2,1)S(1)} %copy-done, bf16[8192,1024]{1,0:T(8,128)(2,1)S(1)} %bitcast.3, bf16[32,5120]{1,0:T(8,128)(2,1)S(1)} %get-tuple-element.43.refs_3_), custom_call_target="tpu_custom_call" | custom-call | flops 10000000 | bytes 10000 | tf_op jit(solution)/shard_map/back/pallas_call | solution.py:422
  18.2 3.1 %collective-permute-done.4.refs_2_ = bf16[640,128]{1,0:T(8,128)(2,1)S(1)} collective-permute-done((bf16[640,128]{1,0:T(8,128)(2,1)S(1)}, bf16[640,128]{1,0:T(8,128)(2,1)S(1)}, u32[]{:S(2)}, u32[]{:S(2)}) %collective-permute-start.4) | collective-permute-done | bytes 163872 | tf_op jit(solution)/shard_map/ppermute | solution.py:70
  21.4 2.8 %collective-permute-done.refs_0_ = bf16[32,8192]{1,0:T(8,128)(2,1)S(1)} collective-permute-done((bf16[32,8192]{1,0:T(8,128)(2,1)S(1)}, bf16[32,8192]{1,0:T(8,128)(2,1)S(1)}, u32[]{:S(2)}, u32[]{:S(2)}) %collective-permute-start) | collective-permute-done | bytes 524320 | tf_op jit(solution)/shard_map/ppermute | solution.py:70
  24.3 1.3 %back.7 = (bf16[64,2048]{1,0:T(8,128)(2,1)S(1)}, bf16[64,2048]{1,0:T(8,128)(2,1)S(1)}) custom-call(s32[2,8]{1,0:T(2,128)S(1)} %bitcast.9, bf16[128,1024]{1,0:T(8,128)(2,1)S(1)} %copy-done, bf16[8192,1024]{1,0:T(8,128)(2,1)S(1)} %bitcast.3, bf16[32,8192]{1,0:T(8,128)(2,1)S(1)} %relay.1.refs_3_.refs_1_), custom_call_target="tpu_custom_call" | custom-call | flops 10000000 | bytes 10000 | tf_op jit(solution)/shard_map/back/pallas_call | solution.py:422
  25.7 0.6 %collective-permute-start.10 = (bf16[64,2048]{1,0:T(8,128)(2,1)S(1)}, bf16[64,2048]{1,0:T(8,128)(2,1)S(1)}, u32[]{:S(2)}, u32[]{:S(2)}) collective-permute-start(bf16[64,2048]{1,0:T(8,128)(2,1)S(1)} %get-tuple-element.48.refs_4_), channel_id=1, source_target_pairs={{0,1},{1,0},{2,3},{3,2},{4,5},{5,4},{6,7},{7,6},{8,9},{9,8},{10,11... | collective-permute-start | bytes 786440 | tf_op jit(solution)/shard_map/ppermute | solution.py:70
  26.3 3.1 %collective-permute-start.11 = (bf16[512,128]{1,0:T(8,128)(2,1)S(1)}, bf16[512,128]{1,0:T(8,128)(2,1)S(1)}, u32[]{:S(2)}, u32[]{:S(2)}) collective-permute-start(bf16[512,128]{1,0:T(8,128)(2,1)S(1)} %get-tuple-element.45.refs_1_), channel_id=1, source_target_pairs={{0,16},{4,20},{8,24},{12,28},{16,0},{20,4},{24,8},{28,12},{1,17},{... | collective-permute-start | bytes 393224 | tf_op jit(solution)/shard_map/ppermute | solution.py:70
  29.4 1.0 %collective-permute-start.14 = (bf16[32,5120]{1,0:T(8,128)(2,1)S(1)}, bf16[32,5120]{1,0:T(8,128)(2,1)S(1)}, u32[]{:S(2)}, u32[]{:S(2)}) collective-permute-start(bf16[32,5120]{1,0:T(8,128)(2,1)S(1)} %get-tuple-element.43.refs_3_), channel_id=1, source_target_pairs={{0,2},{1,3},{2,0},{3,1},{4,6},{5,7},{6,4},{7,5},{8,10},{9,11},{10,... | collective-permute-start | bytes 983048 | tf_op jit(solution)/shard_map/ppermute | solution.py:70
  30.4 0.1 merge.3
  30.6 2.3 %forward.1.refs_3_.refs_1_ = f32[128,1024]{1,0:T(8,128)S(1)} custom-call(bf16[32,8192]{1,0:T(8,128)(2,1)S(1)} %copy-done.1, bf16[32,8192]{1,0:T(8,128)(2,1)S(1)} %relay.1.refs_3_.refs_1_, bf16[32,8192]{1,0:T(8,128)(2,1)S(1)} %collective-permute-done.7.refs_2_, bf16[32,8192]{1,0:T(8,128)(2,1)S(1)} %collective-permute-done.8.refs_3_, ...), custom_call_target="tpu_custom_call" | custom-call | flops 10000000 | bytes 10000 | tf_op jit(solution)/shard_map/forward/pallas_call | solution.py:477
  32.9 3.4 %collective-permute-done.11.refs_2_ = bf16[512,128]{1,0:T(8,128)(2,1)S(1)} collective-permute-done((bf16[512,128]{1,0:T(8,128)(2,1)S(1)}, bf16[512,128]{1,0:T(8,128)(2,1)S(1)}, u32[]{:S(2)}, u32[]{:S(2)}) %collective-permute-start.11) | collective-permute-done | bytes 131104 | tf_op jit(solution)/shard_map/ppermute | solution.py:70
  36.3 0.8 %collective-permute-start.12 = (bf16[640,128]{1,0:T(8,128)(2,1)S(1)}, bf16[640,128]{1,0:T(8,128)(2,1)S(1)}, u32[]{:S(2)}, u32[]{:S(2)}) collective-permute-start(bf16[640,128]{1,0:T(8,128)(2,1)S(1)} %get-tuple-element.52.refs_2_.refs_4_), channel_id=1, source_target_pairs={{0,8},{4,12},{8,0},{12,4},{16,24},{20,28},{24,16},{28,20},{1,9},{5... | collective-permute-start | bytes 491528 | tf_op jit(solution)/shard_map/ppermute | solution.py:70
  37.1 1.0 %collective-permute-start.15 = (bf16[32,4096]{1,0:T(8,128)(2,1)S(1)}, bf16[32,4096]{1,0:T(8,128)(2,1)S(1)}, u32[]{:S(2)}, u32[]{:S(2)}) collective-permute-start(bf16[32,4096]{1,0:T(8,128)(2,1)S(1)} %get-tuple-element.49.refs_5_), channel_id=1, source_target_pairs={{0,2},{1,3},{2,0},{3,1},{4,6},{5,7},{6,4},{7,5},{8,10},{9,11},{10,... | collective-permute-start | bytes 786440 | tf_op jit(solution)/shard_map/ppermute | solution.py:70
  38.1 4.2 %collective-permute-done.12.refs_3_ = bf16[640,128]{1,0:T(8,128)(2,1)S(1)} collective-permute-done((bf16[640,128]{1,0:T(8,128)(2,1)S(1)}, bf16[640,128]{1,0:T(8,128)(2,1)S(1)}, u32[]{:S(2)}, u32[]{:S(2)}) %collective-permute-start.12) | collective-permute-done | bytes 163872 | tf_op jit(solution)/shard_map/ppermute | solution.py:70
  42.3 0.2 compact_step.1
  42.6 0.9 %collective-permute-start.16 = (bf16[64,128]{1,0:T(8,128)(2,1)S(1)}, bf16[64,128]{1,0:T(8,128)(2,1)S(1)}, u32[]{:S(2)}, u32[]{:S(2)}) collective-permute-start(bf16[64,128]{1,0:T(8,128)(2,1)S(1)} %get-tuple-element.54.refs_6_), channel_id=1, source_target_pairs={{0,2},{1,3},{2,0},{3,1},{4,6},{5,7},{6,4},{7,5},{8,10},{9,11},{10,... | collective-permute-start | bytes 49160 | tf_op jit(solution)/shard_map/ppermute | solution.py:70
  43.5 0.4 collective-permute-done.13.refs_3_.refs_2_
  43.9 1.5 %project.1 = bf16[128,1024]{1,0:T(8,128)(2,1)} custom-call(s32[2,8]{1,0:T(2,128)S(1)} %bitcast.10, f32[128,1024]{1,0:T(8,128)S(1)} %forward.1.refs_3_.refs_1_, bf16[512,128]{1,0:T(8,128)(2,1)S(1)} %get-tuple-element.53.refs_2_.refs_1_, bf16[512,128]{1,0:T(8,128)(2,1)S(1)} %collective-permute-done.13.refs_3_.refs_2_, ...), custom_call_target="tpu_custom_call" | custom-call | flops 10000000 | bytes 10000 | tf_op jit(solution)/shard_map/project/pallas_call | solution.py:517
  45.4 0.3 correct.1.refs_0_.refs_2_.refs_5_
  45.7 0.9 %final.1 = bf16[32,8192]{1,0:T(8,128)(2,1)} custom-call(f32[32,8192]{1,0:T(8,128)S(1)} %correct.1.refs_0_.refs_2_.refs_5_, bf16[32,4096]{1,0:T(8,128)(2,1)S(1)} %collective-permute-done.15.refs_1_, f32[32,8192]{1,0:T(8,128)S(1)} %correct.1.refs_0_.refs_2_.refs_5_), custom_call_target="tpu_custom_call" | custom-call | flops 10000000 | bytes 10000 | tf_op jit(solution)/shard_map/final/pallas_call | solution.py:578
  46.6 0.7 %adam.1 = (bf16[2,4096]{1,0:T(2,128)(2,1)}, f32[2,4096]{1,0:T(2,128)}, f32[2,4096]{1,0:T(2,128)}) custom-call(bf16[64,128]{1,0:T(8,128)(2,1)S(1)} %get-tuple-element.57.refs_0_, bf16[64,128]{1,0:T(8,128)(2,1)S(1)} %collective-permute-done.16.refs_1_, bf16[2,4096]{1,0:T(2,128)(2,1)S(1)} %copy-done.5, f32[2,4096]{1,0:T(2,128)S(1)} %copy-done.3, ...), custom_call_target="tpu_custom_call" | custom-call | flops 10000000 | bytes 10000 | tf_op jit(solution)/shard_map/adam/pallas_call | solution.py:375
  (45 shorter events, 0.9 us)
Async XLA Ops:
  0.6 0.7 %copy-start.2 = (s32[8,2]{0,1:T(2,128)S(1)}, s32[8,2]{0,1:T(2,128)}, u32[]{:S(2)}) copy-start(s32[8,2]{0,1:T(2,128)} %param.11) | copy-start | bytes 196
  0.6 0.7 %copy-start.5 = (bf16[2,4096]{1,0:T(2,128)(2,1)S(1)}, bf16[2,4096]{1,0:T(2,128)(2,1)}, u32[]{:S(2)}) copy-start(bf16[2,4096]{1,0:T(2,128)(2,1)} %refs_2_.11) | copy-start | bytes 49156
  0.7 1.1 %copy-start.1 = (bf16[32,8192]{1,0:T(8,128)(2,1)S(1)}, bf16[32,8192]{1,0:T(8,128)(2,1)}, u32[]{:S(2)}) copy-start(bf16[32,8192]{1,0:T(8,128)(2,1)} %refs_0_.1) | copy-start | bytes 1572868
  1.7 10.1 %slice-start = ((s8[16777216]{0:T(1024)(128)(4,1)}), s8[4194304]{0:T(1024)(128)(4,1)S(1)}, s32[]{:S(2)}) async-start(s8[16777216]{0:T(1024)(128)(4,1)} %bitcast.2), calls=%async_computation | async-start | bytes 8388608
  1.7 10.1 %slice-start.1 = ((s8[16777216]{0:T(1024)(128)(4,1)}), s8[4194304]{0:T(1024)(128)(4,1)S(1)}, s32[]{:S(2)}) async-start(s8[16777216]{0:T(1024)(128)(4,1)} %bitcast.2), calls=%async_computation.1 | async-start | bytes 8388608
  1.7 10.1 %slice-start.2 = ((s8[16777216]{0:T(1024)(128)(4,1)}), s8[4194304]{0:T(1024)(128)(4,1)S(1)}, s32[]{:S(2)}) async-start(s8[16777216]{0:T(1024)(128)(4,1)} %bitcast.2), calls=%async_computation.2 | async-start | bytes 8388608
  1.8 6.9 %copy-start = (bf16[128,1024]{1,0:T(8,128)(2,1)S(1)}, bf16[128,1024]{1,0:T(8,128)(2,1)}, u32[]{:S(2)}) copy-start(bf16[128,1024]{1,0:T(8,128)(2,1)} %refs_1_.9) | copy-start | bytes 786436
  1.9 6.9 %copy-start.6 = (s32[8]{0:T(128)S(1)}, s32[8]{0:T(128)}, u32[]{:S(2)}) copy-start(s32[8]{0:T(128)} %param.12) | copy-start | bytes 100
  1.9 10.0 %slice-start.3 = ((s8[16777216]{0:T(1024)(128)(4,1)}), s8[4194304]{0:T(1024)(128)(4,1)S(1)}, s32[]{:S(2)}) async-start(s8[16777216]{0:T(1024)(128)(4,1)} %bitcast.2), calls=%async_computation.3 | async-start | bytes 8388608
  1.9 5.4 %collective-permute-start.1 = (bf16[320,128]{1,0:T(8,128)(2,1)S(1)}, bf16[320,128]{1,0:T(8,128)(2,1)S(1)}, u32[]{:S(2)}, u32[]{:S(2)}) collective-permute-start(bf16[320,128]{1,0:T(8,128)(2,1)S(1)} %slabs.1.refs_0_), channel_id=1, source_target_pairs={{0,2},{1,3},{2,0},{3,1},{4,6},{5,7},{6,4},{7,5},{8,10},{9,11},{10,... | collective-permute-start | bytes 245768 | tf_op jit(solution)/shard_map/ppermute | solution.py:70
  7.3 1.4 %collective-permute-start.2 = (bf16[512,128]{1,0:T(8,128)(2,1)S(1)}, bf16[512,128]{1,0:T(8,128)(2,1)S(1)}, u32[]{:S(2)}, u32[]{:S(2)}) collective-permute-start(bf16[512,128]{1,0:T(8,128)(2,1)S(1)} %get-tuple-element.33.refs_2_.refs_4_), channel_id=1, source_target_pairs={{0,1},{1,0},{2,3},{3,2},{4,5},{5,4},{6,7},{7,6},{8,9},{9,8},{10,11... | collective-permute-start | bytes 393224 | tf_op jit(solution)/shard_map/ppermute | solution.py:70
  9.8 3.4 %collective-permute-start.3 = (bf16[1024,128]{1,0:T(8,128)(2,1)S(1)}, bf16[1024,128]{1,0:T(8,128)(2,1)S(1)}, u32[]{:S(2)}, u32[]{:S(2)}) collective-permute-start(bf16[1024,128]{1,0:T(8,128)(2,1)S(1)} %get-tuple-element.35.refs_3_), channel_id=1, source_target_pairs={{0,1},{1,0},{2,3},{3,2},{4,5},{5,4},{6,7},{7,6},{8,9},{9,8},{10,11... | collective-permute-start | bytes 786440 | tf_op jit(solution)/shard_map/ppermute | solution.py:70
  9.9 14.3 %collective-permute-start = (bf16[32,8192]{1,0:T(8,128)(2,1)S(1)}, bf16[32,8192]{1,0:T(8,128)(2,1)S(1)}, u32[]{:S(2)}, u32[]{:S(2)}) collective-permute-start(bf16[32,8192]{1,0:T(8,128)(2,1)S(1)} %copy-done.1), channel_id=1, source_target_pairs={{0,2},{1,3},{2,0},{3,1},{4,6},{5,7},{6,4},{7,5},{8,10},{9,11},{10,... | collective-permute-start | bytes 1572872 | tf_op jit(solution)/shard_map/ppermute | solution.py:70
  14.6 2.2 %collective-permute-start.6 = (bf16[64,3072]{1,0:T(8,128)(2,1)S(1)}, bf16[64,3072]{1,0:T(8,128)(2,1)S(1)}, u32[]{:S(2)}, u32[]{:S(2)}) collective-permute-start(bf16[64,3072]{1,0:T(8,128)(2,1)S(1)} %get-tuple-element.42.refs_4_), channel_id=1, source_target_pairs={{0,1},{1,0},{2,3},{3,2},{4,5},{5,4},{6,7},{7,6},{8,9},{9,8},{10,11... | collective-permute-start | bytes 1179656 | tf_op jit(solution)/shard_map/ppermute | solution.py:70
  14.7 2.1 %collective-permute-start.5 = (bf16[64,2048]{1,0:T(8,128)(2,1)S(1)}, bf16[64,2048]{1,0:T(8,128)(2,1)S(1)}, u32[]{:S(2)}, u32[]{:S(2)}) collective-permute-start(bf16[64,2048]{1,0:T(8,128)(2,1)S(1)} %get-tuple-element.37.refs_3_), channel_id=1, source_target_pairs={{0,1},{1,0},{2,3},{3,2},{4,5},{5,4},{6,7},{7,6},{8,9},{9,8},{10,11... | collective-permute-start | bytes 786440 | tf_op jit(solution)/shard_map/ppermute | solution.py:70
  15.2 6.2 %collective-permute-start.4 = (bf16[640,128]{1,0:T(8,128)(2,1)S(1)}, bf16[640,128]{1,0:T(8,128)(2,1)S(1)}, u32[]{:S(2)}, u32[]{:S(2)}) collective-permute-start(bf16[640,128]{1,0:T(8,128)(2,1)S(1)} %get-tuple-element.39.refs_3_.refs_1_), channel_id=1, source_target_pairs={{0,4},{4,0},{8,12},{12,8},{16,20},{20,16},{24,28},{28,24},{1,5},{5... | collective-permute-start | bytes 491528 | tf_op jit(solution)/shard_map/ppermute | solution.py:70
  16.7 13.8 %collective-permute-start.7 = (bf16[32,8192]{1,0:T(8,128)(2,1)S(1)}, bf16[32,8192]{1,0:T(8,128)(2,1)S(1)}, u32[]{:S(2)}, u32[]{:S(2)}) collective-permute-start(bf16[32,8192]{1,0:T(8,128)(2,1)S(1)} %copy-done.1), channel_id=1, source_target_pairs={{0,1},{1,0},{2,3},{3,2},{4,5},{5,4},{6,7},{7,6},{8,9},{9,8},{10,11... | collective-permute-start | bytes 1572872 | tf_op jit(solution)/shard_map/ppermute | solution.py:70
  24.2 6.3 %collective-permute-start.8 = (bf16[32,8192]{1,0:T(8,128)(2,1)S(1)}, bf16[32,8192]{1,0:T(8,128)(2,1)S(1)}, u32[]{:S(2)}, u32[]{:S(2)}) collective-permute-start(bf16[32,8192]{1,0:T(8,128)(2,1)S(1)} %relay.1.refs_3_.refs_1_), channel_id=1, source_target_pairs={{0,1},{1,0},{2,3},{3,2},{4,5},{5,4},{6,7},{7,6},{8,9},{9,8},{10,11... | collective-permute-start | bytes 1572872 | tf_op jit(solution)/shard_map/ppermute | solution.py:70
  25.6 21.0 %copy-start.3 = (f32[2,4096]{1,0:T(2,128)S(1)}, f32[2,4096]{1,0:T(2,128)}, u32[]{:S(2)}) copy-start(f32[2,4096]{1,0:T(2,128)} %refs_3_.1) | copy-start | bytes 98308
  25.7 21.0 %copy-start.4 = (f32[2,4096]{1,0:T(2,128)S(1)}, f32[2,4096]{1,0:T(2,128)}, u32[]{:S(2)}) copy-start(f32[2,4096]{1,0:T(2,128)} %refs_4_.5) | copy-start | bytes 98308
  25.7 3.7 %collective-permute-start.10 = (bf16[64,2048]{1,0:T(8,128)(2,1)S(1)}, bf16[64,2048]{1,0:T(8,128)(2,1)S(1)}, u32[]{:S(2)}, u32[]{:S(2)}) collective-permute-start(bf16[64,2048]{1,0:T(8,128)(2,1)S(1)} %get-tuple-element.48.refs_4_), channel_id=1, source_target_pairs={{0,1},{1,0},{2,3},{3,2},{4,5},{5,4},{6,7},{7,6},{8,9},{9,8},{10,11... | collective-permute-start | bytes 786440 | tf_op jit(solution)/shard_map/ppermute | solution.py:70
  26.2 4.2 %collective-permute-start.9 = (bf16[64,2048]{1,0:T(8,128)(2,1)S(1)}, bf16[64,2048]{1,0:T(8,128)(2,1)S(1)}, u32[]{:S(2)}, u32[]{:S(2)}) collective-permute-start(bf16[64,2048]{1,0:T(8,128)(2,1)S(1)} %get-tuple-element.44.refs_3_), channel_id=1, source_target_pairs={{0,1},{1,0},{2,3},{3,2},{4,5},{5,4},{6,7},{7,6},{8,9},{9,8},{10,11... | collective-permute-start | bytes 786440 | tf_op jit(solution)/shard_map/ppermute | solution.py:70
  26.3 10.0 %collective-permute-start.11 = (bf16[512,128]{1,0:T(8,128)(2,1)S(1)}, bf16[512,128]{1,0:T(8,128)(2,1)S(1)}, u32[]{:S(2)}, u32[]{:S(2)}) collective-permute-start(bf16[512,128]{1,0:T(8,128)(2,1)S(1)} %get-tuple-element.45.refs_1_), channel_id=1, source_target_pairs={{0,16},{4,20},{8,24},{12,28},{16,0},{20,4},{24,8},{28,12},{1,17},{... | collective-permute-start | bytes 393224 | tf_op jit(solution)/shard_map/ppermute | solution.py:70
  29.4 16.0 %collective-permute-start.14 = (bf16[32,5120]{1,0:T(8,128)(2,1)S(1)}, bf16[32,5120]{1,0:T(8,128)(2,1)S(1)}, u32[]{:S(2)}, u32[]{:S(2)}) collective-permute-start(bf16[32,5120]{1,0:T(8,128)(2,1)S(1)} %get-tuple-element.43.refs_3_), channel_id=1, source_target_pairs={{0,2},{1,3},{2,0},{3,1},{4,6},{5,7},{6,4},{7,5},{8,10},{9,11},{10,... | collective-permute-start | bytes 983048 | tf_op jit(solution)/shard_map/ppermute | solution.py:70
  36.3 6.0 %collective-permute-start.12 = (bf16[640,128]{1,0:T(8,128)(2,1)S(1)}, bf16[640,128]{1,0:T(8,128)(2,1)S(1)}, u32[]{:S(2)}, u32[]{:S(2)}) collective-permute-start(bf16[640,128]{1,0:T(8,128)(2,1)S(1)} %get-tuple-element.52.refs_2_.refs_4_), channel_id=1, source_target_pairs={{0,8},{4,12},{8,0},{12,4},{16,24},{20,28},{24,16},{28,20},{1,9},{5... | collective-permute-start | bytes 491528 | tf_op jit(solution)/shard_map/ppermute | solution.py:70
  37.1 8.6 %collective-permute-start.15 = (bf16[32,4096]{1,0:T(8,128)(2,1)S(1)}, bf16[32,4096]{1,0:T(8,128)(2,1)S(1)}, u32[]{:S(2)}, u32[]{:S(2)}) collective-permute-start(bf16[32,4096]{1,0:T(8,128)(2,1)S(1)} %get-tuple-element.49.refs_5_), channel_id=1, source_target_pairs={{0,2},{1,3},{2,0},{3,1},{4,6},{5,7},{6,4},{7,5},{8,10},{9,11},{10,... | collective-permute-start | bytes 786440 | tf_op jit(solution)/shard_map/ppermute | solution.py:70
  42.5 1.4 %collective-permute-start.13 = (bf16[512,128]{1,0:T(8,128)(2,1)S(1)}, bf16[512,128]{1,0:T(8,128)(2,1)S(1)}, u32[]{:S(2)}, u32[]{:S(2)}) collective-permute-start(bf16[512,128]{1,0:T(8,128)(2,1)S(1)} %get-tuple-element.53.refs_2_.refs_1_), channel_id=1, source_target_pairs={{0,1},{1,0},{2,3},{3,2},{4,5},{5,4},{6,7},{7,6},{8,9},{9,8},{10,11... | collective-permute-start | bytes 393224 | tf_op jit(solution)/shard_map/ppermute | solution.py:70
  42.6 4.0 %collective-permute-start.16 = (bf16[64,128]{1,0:T(8,128)(2,1)S(1)}, bf16[64,128]{1,0:T(8,128)(2,1)S(1)}, u32[]{:S(2)}, u32[]{:S(2)}) collective-permute-start(bf16[64,128]{1,0:T(8,128)(2,1)S(1)} %get-tuple-element.54.refs_6_), channel_id=1, source_target_pairs={{0,2},{1,3},{2,0},{3,1},{4,6},{5,7},{6,4},{7,5},{8,10},{9,11},{10,... | collective-permute-start | bytes 49160 | tf_op jit(solution)/shard_map/ppermute | solution.py:70

commit v3 on v2

v3 whole, which is shorter than its diff:
```python
import functools
import math

import jax
import jax.numpy as jnp
from jax import lax
from jax.experimental import pallas as pl
from jax.experimental.pallas import tpu as pltpu
from jax.sharding import PartitionSpec as P

HEAD_DIM = 128
LANES = 128
CORRECT_ONE = 1.0 - 0.9**10
CORRECT_TWO = 1.0 - 0.999**10
BF16 = jnp.bfloat16
F32 = jnp.float32
VMEM_LIMIT = 24 * 1024 * 1024
BACK_PIECES = 4
BACK_CHUNKS = 2
ORDER = (
    ("delta", 0), ("back", 0), ("delta", 1), ("back", 1), ("delta", 2), ("sum", 0), ("relay", 0), ("back", 2), ("grad", 0), ("back", 3), ("grad", 1), ("sum", 1), ("grad", 2), ("forward", 0), ("delta", 3), ("grad", 3), ("correct", 0), ("project", 0), ("grad", 4), ("final", 0), ("adam", 0),
)


def params():
    return pltpu.CompilerParams(vmem_limit_bytes=VMEM_LIMIT)


def cost(us):
    return pl.CostEstimate(flops=int(us * 1e9), bytes_accessed=int(us * 1e6), transcendentals=0)


def vmem(n=1):
    return [pl.BlockSpec(memory_space=pltpu.VMEM)] * n


def anywhere(deps):
    return [pl.BlockSpec(memory_space=pl.ANY)] * len(deps)


def with_deps(kernel, inputs, deps):
    def run(*refs):
        kernel(*refs[:inputs], *refs[inputs + len(deps) :])

    return run


def bits_of(count):
    return [1 << i for i in range(count.bit_length() - 1)]


def halving_order(count):
    order = [0]
    for bit in reversed(bits_of(count)):
        order = order + [j + bit for j in order]
    width = count.bit_length() - 1
    rev = lambda j: int(format(j, "0%db" % width)[::-1], 2) if width else 0
    return sorted(range(count), key=rev)


def gather_order(nt):
    order = [0]
    for bit in bits_of(nt)[1:] + [1]:
        order = order + [j ^ bit for j in order]
    return order


def xor_permute(x, axis, bit):
    count = lax.axis_size(axis)
    return lax.ppermute(x, axis, [(i, i ^ bit) for i in range(count)])


def slot_ranks(owners):
    ranks = []
    for b, owner in enumerate(owners):
        rank = jnp.int32(0)
        for before in owners[:b]:
            rank = rank + (before == owner).astype(jnp.int32)
        ranks.append(rank)
    return ranks


def scalars(ref, row, nb):
    table = ref[...]
    return [table[row, b] for b in range(nb)]


def place_of(offset, bits):
    place = jnp.int32(0)
    for i, bit in enumerate(bits):
        place = place + jnp.where((offset & bit) != 0, 1 << i, 0)
    return place


def lane_block(index):
    return pl.ds(pl.multiple_of(index * LANES, LANES), LANES)


def row_block(index, rows):
    return pl.ds(pl.multiple_of(index * rows, rows), rows)


def relay_kernel(count, *refs):
    for i in range(count):
        refs[count + i][...] = refs[i][...]


def relay(parts, deps):
    count = len(parts)
    return list(
        pl.pallas_call(
            with_deps(functools.partial(relay_kernel, count), count, deps),
            out_shape=[jax.ShapeDtypeStruct(x.shape, x.dtype) for x in parts],
            in_specs=vmem(count) + anywhere(deps),
            out_specs=vmem(count),
            compiler_params=params(),
            cost_estimate=cost(10),
            name="relay",
        )(*parts, *deps)
    )


def begin_kernel(out_ref):
    out_ref[...] = jnp.zeros_like(out_ref)


def begin():
    return pl.pallas_call(
        begin_kernel,
        out_shape=jax.ShapeDtypeStruct((8, LANES), F32),
        out_specs=pl.BlockSpec(memory_space=pltpu.VMEM),
        compiler_params=params(),
        cost_estimate=cost(30),
        name="begin",
    )()


def line_kernel(delta_ref, out_ref):
    cap = delta_ref.shape[0]
    part = delta_ref.shape[1] // LANES
    delta = delta_ref[...].astype(F32)
    for k in range(cap):
        lines = [delta[k : k + 1, i * LANES : (i + 1) * LANES] for i in range(part)]
        out_ref[k * part : (k + 1) * part, :] = jnp.concatenate(lines, 0).astype(BF16)


def lines_of(delta, deps):
    return pl.pallas_call(
        with_deps(line_kernel, 1, deps),
        out_shape=jax.ShapeDtypeStruct((delta.size // LANES, LANES), BF16),
        in_specs=vmem() + anywhere(deps),
        out_specs=pl.BlockSpec(memory_space=pltpu.VMEM),
        compiler_params=params(),
        cost_estimate=cost(30),
        name="lines",
    )(delta, *deps)


def double_kernel(own_ref, recv_ref, out_ref):
    rows = own_ref.shape[0]
    out_ref[:rows, :] = own_ref[...]
    out_ref[rows:, :] = recv_ref[...]


def double(own, recv, deps):
    rows = own.shape[0]
    return pl.pallas_call(
        with_deps(double_kernel, 2, deps),
        out_shape=jax.ShapeDtypeStruct((2 * rows, LANES), BF16),
        in_specs=vmem(2) + anywhere(deps),
        out_specs=pl.BlockSpec(memory_space=pltpu.VMEM),
        compiler_params=params(),
        cost_estimate=cost(10),
        name="double",
    )(own, recv, *deps)


def compact_kernel(bits, nb, cap, part, owner_ref, own_ref, recv_ref, out_ref, all_ref):
    dp = lax.axis_index("dp")
    rows = own_ref.shape[0]
    all_ref[:rows, :] = own_ref[...]
    all_ref[rows:, :] = recv_ref[...]
    owners = scalars(owner_ref, 0, nb)
    ranks = slot_ranks(owners)
    for b in range(nb):
        start = (place_of(owners[b] ^ dp, bits) * cap + ranks[b]) * part
        out_ref[b * part : (b + 1) * part, :] = all_ref[pl.ds(pl.multiple_of(start, part), part), :]


def compact(owner, own, recv, bits, cap, part, deps):
    nb = owner.shape[1]
    return pl.pallas_call(
        with_deps(functools.partial(compact_kernel, bits, nb, cap, part), 3, deps),
        out_shape=jax.ShapeDtypeStruct((nb * part, LANES), BF16),
        in_specs=vmem(3) + anywhere(deps),
        out_specs=pl.BlockSpec(memory_space=pltpu.VMEM),
        scratch_shapes=[pltpu.VMEM((2 * own.shape[0], LANES), BF16)],
        compiler_params=params(),
        cost_estimate=cost(10),
        name="compact_step",
    )(owner, own, recv, *deps)


def unride_kernel(part, width, own_ref, recv_ref, out_ref):
    rows = own_ref.shape[0]
    out_ref[:rows, :] = own_ref[...]
    for b in range(rows // part):
        cols = slice(width + b * LANES, width + (b + 1) * LANES)
        out_ref[rows + b * part : rows + (b + 1) * part, :] = recv_ref[:part, cols]


def unride(own, recv, part, deps):
    rows = own.shape[0]
    width = recv.shape[1] - rows // part * LANES
    return pl.pallas_call(
        with_deps(functools.partial(unride_kernel, part, width), 2, deps),
        out_shape=jax.ShapeDtypeStruct((2 * rows, LANES), BF16),
        in_specs=vmem(2) + anywhere(deps),
        out_specs=pl.BlockSpec(memory_space=pltpu.VMEM),
        compiler_params=params(),
        cost_estimate=cost(10),
        name="unride",
    )(own, recv, *deps)


def grad_kernel(nt, bits, nb, cap, scale, index_ref, owner_ref, grad_ref, *refs):
    token_refs = refs[:nt]
    keep_ref, send_ref, slab_ref, block_ref = refs[nt:]
    me = lax.axis_index("tensor")
    dp = lax.axis_index("dp")
    part = HEAD_DIM // nt
    rows = grad_ref.shape[0] // nt
    heads = grad_ref.shape[1] // HEAD_DIM
    half = nt // 2
    keep_ref[...] = jnp.zeros_like(keep_ref)
    send_ref[...] = jnp.zeros_like(send_ref)
    owners = scalars(owner_ref, 0, nb)
    ranks = slot_ranks(owners)
    row_of = scalars(index_ref, 0, nb)
    head_of = scalars(index_ref, 1, nb)
    for b in range(nb):
        head = head_of[b]

        @pl.when(head // heads == me)
        def _():
            for ref, j in zip(token_refs, gather_order(nt)):
                slab_ref[row_block(me ^ j, rows), :] = ref[:, lane_block(row_of[b])]
            block_ref[...] = (
                lax.dot_general(
                    slab_ref[...],
                    grad_ref[:, lane_block(head - me * heads)],
                    (((0,), (0,)), ((), ())),
                    preferred_element_type=F32,
                )
                * scale
            ).astype(BF16)
            place = place_of(owners[b] ^ dp, bits[::-1])
            for p, j in enumerate(halving_order(nt)):
                target = keep_ref if p < half else send_ref
                start = ((place * half + p % half) * cap + ranks[b]) * part
                target[pl.ds(pl.multiple_of(start, part), part), :] = block_ref[row_block(me ^ j, part), :]


def block_grads(index, owner, out_grad, pieces, nt, bits, cap, deps):
    nb = index.shape[1]
    rows = out_grad.shape[0]
    nd = 1 << len(bits)
    scale = 1.0 / math.sqrt(rows * nd)
    size = nd * (nt // 2) * cap * (HEAD_DIM // nt)
    half = jax.ShapeDtypeStruct((size, LANES), BF16)
    return pl.pallas_call(
        with_deps(functools.partial(grad_kernel, nt, bits, nb, cap, scale), 3 + nt, deps),
        out_shape=[half, half],
        in_specs=vmem(3 + nt) + anywhere(deps),
        out_specs=vmem(2),
        scratch_shapes=[pltpu.VMEM((rows, LANES), BF16), pltpu.VMEM((HEAD_DIM, HEAD_DIM), BF16)],
        compiler_params=params(),
        cost_estimate=cost(10),
        name="block_grads",
    )(index, owner, out_grad, *pieces, *deps)


def halve_kernel(keep_ref, recv_ref, keep_out, send_out):
    half = keep_out.shape[0]
    total = (keep_ref[...].astype(F32) + recv_ref[...].astype(F32)).astype(BF16)
    keep_out[...] = total[:half]
    send_out[...] = total[half:]


def halve(keep, recv, deps):
    rows = keep.shape[0]
    half = jax.ShapeDtypeStruct((rows // 2, LANES), BF16)
    return pl.pallas_call(
        with_deps(halve_kernel, 2, deps),
        out_shape=[half, half],
        in_specs=vmem(2) + anywhere(deps),
        out_specs=vmem(2),
        compiler_params=params(),
        cost_estimate=cost(10),
        name="halve",
    )(keep, recv, *deps)


def adam_kernel(
    cap, keep_ref, recv_ref, delta_ref, one_ref, two_ref, delta_out, one_out, two_out, grad_ref
):
    part = keep_ref.shape[0] // cap
    total = keep_ref[...].astype(F32) + recv_ref[...].astype(F32)
    for k in range(cap):
        for i in range(part):
            grad_ref[k : k + 1, i * LANES : (i + 1) * LANES] = total[k * part + i : k * part + i + 1, :]
    grad = grad_ref[...]
    first = 0.9 * one_ref[...] + 0.1 * grad
    second = 0.999 * two_ref[...] + 0.001 * grad * grad
    one_out[...] = first
    two_out[...] = second
    update = 0.02 * (first / CORRECT_ONE) / (jnp.sqrt(second / CORRECT_TWO) + 1e-08)
    delta_out[...] = (delta_ref[...].astype(F32) - update).astype(BF16)


def adam(keep, recv, delta, moment1, moment2, deps):
    return pl.pallas_call(
        with_deps(functools.partial(adam_kernel, delta.shape[0]), 5, deps),
        out_shape=[
            jax.ShapeDtypeStruct(delta.shape, BF16),
            jax.ShapeDtypeStruct(delta.shape, F32),
            jax.ShapeDtypeStruct(delta.shape, F32),
        ],
        in_specs=vmem(5) + anywhere(deps),
        out_specs=vmem(3),
        scratch_shapes=[pltpu.VMEM(delta.shape, F32)],
        compiler_params=params(),
        cost_estimate=cost(10),
        name="adam",
    )(keep, recv, delta, moment1, moment2, *deps)


def back_kernel(nt, nb, start, width, index_ref, grad_ref, weight_ref, keep_ref, send_ref, perm_ref):
    me = lax.axis_index("tensor")
    rows = grad_ref.shape[0] // nt
    heads = grad_ref.shape[1] // HEAD_DIM
    half = nt // 2 * rows
    for p, j in enumerate(halving_order(nt)):
        perm_ref[p * rows : (p + 1) * rows, :] = grad_ref[row_block(me ^ j, rows), :]
    out = lax.dot_general(
        weight_ref[start : start + width, :], perm_ref[...], (((1,), (1,)), ((), ())), preferred_element_type=F32
    )
    out = out.astype(BF16).T
    keep_ref[:, :width] = out[:half]
    send_ref[:, :width] = out[half:]
    if keep_ref.shape[1] > width:
        head_of = scalars(index_ref, 1, nb)
        for b in range(nb):
            head = head_of[b]
            mine = head // heads == me
            part = perm_ref[:, lane_block(jnp.where(mine, head - me * heads, 0))]
            part = jnp.where(mine, part, jnp.zeros_like(part))
            cols = slice(width + b * LANES, width + (b + 1) * LANES)
            keep_ref[:, cols] = part[:half]
            send_ref[:, cols] = part[half:]


def back(index, out_grad, weight, piece, riders, nt, deps):
    nb = index.shape[1]
    rows = out_grad.shape[0]
    depth = weight.shape[0]
    width = depth // BACK_PIECES
    half = jax.ShapeDtypeStruct((rows // 2, width + (nb * LANES if riders else 0)), BF16)
    return pl.pallas_call(
        with_deps(functools.partial(back_kernel, nt, nb, piece * width, width), 3, deps),
        out_shape=[half, half],
        in_specs=vmem(3) + anywhere(deps),
        out_specs=vmem(2),
        scratch_shapes=[pltpu.VMEM(out_grad.shape, BF16)],
        compiler_params=params(),
        cost_estimate=cost(10),
        name="back",
    )(index, out_grad, weight, *deps)


def merge_kernel(count, part, *refs):
    keeps, recvs = refs[:count], refs[count : 2 * count]
    keep_out, send_out = refs[-2:]
    half = keep_out.shape[0]
    place = 0
    for keep_ref, recv_ref in zip(keeps, recvs):
        cols = slice(place, place + keep_ref.shape[1])
        place += keep_ref.shape[1]
        total = (keep_ref[...].astype(F32) + recv_ref[...].astype(F32)).astype(BF16)
        keep_out[:, cols] = total[:half]
        send_out[:, cols] = total[half:]
    for rider_ref in refs[2 * count : -2]:
        for b in range(rider_ref.shape[0] // part):
            cols = slice(place + b * LANES, place + (b + 1) * LANES)
            send_out[:part, cols] = rider_ref[b * part : (b + 1) * part, :]
            if part < half:
                send_out[part:, cols] = jnp.zeros((half - part, LANES), BF16)


def merge(keeps, recvs, riders, part, deps):
    count = len(keeps)
    rows = keeps[0].shape[0] // 2
    width = sum(x.shape[1] for x in keeps)
    extra = sum(x.shape[0] for x in riders) // part * LANES
    return pl.pallas_call(
        with_deps(functools.partial(merge_kernel, count, part), 2 * count + len(riders), deps),
        out_shape=[jax.ShapeDtypeStruct((rows, width), BF16), jax.ShapeDtypeStruct((rows, width + extra), BF16)],
        in_specs=vmem(2 * count + len(riders)) + anywhere(deps),
        out_specs=vmem(2),
        compiler_params=params(),
        cost_estimate=cost(10),
        name="merge",
    )(*keeps, *recvs, *riders, *deps)


def load_block(block_ref, halves, order, b, nb, part, me):
    per = len(order) // 2
    for p, j in enumerate(order):
        source = halves[p // per]
        start = ((p % per) * nb + b) * part
        block_ref[row_block(me ^ j, part), :] = source[start : start + part, :]


def forward_kernel(count, *refs):
    weight_ref, out_ref = refs[count:]
    tile = jnp.concatenate([ref[...] for ref in refs[:count]], axis=0)
    out_ref[...] = jnp.dot(tile, weight_ref[...], preferred_element_type=F32)


def forward(pieces, weight, deps):
    count = len(pieces)
    return pl.pallas_call(
        with_deps(functools.partial(forward_kernel, count), count + 1, deps),
        out_shape=jax.ShapeDtypeStruct((pieces[0].shape[0] * count, weight.shape[1]), F32),
        in_specs=vmem(count + 1) + anywhere(deps),
        out_specs=pl.BlockSpec(memory_space=pltpu.VMEM),
        compiler_params=params(),
        cost_estimate=cost(10),
        name="forward",
    )(*pieces, weight, *deps)


def project_kernel(nt, nb, index_ref, sum_ref, near_delta, far_delta, *refs):
    token_refs = refs[:nt]
    out_ref, acc_ref, block_ref = refs[nt:]
    me = lax.axis_index("tensor")
    order = gather_order(nt)
    rows = sum_ref.shape[0] // nt
    heads = out_ref.shape[1] // HEAD_DIM
    part = HEAD_DIM // nt
    acc_ref[...] = sum_ref[...]
    row_of = scalars(index_ref, 0, nb)
    head_of = scalars(index_ref, 1, nb)
    for b in range(nb):
        head = head_of[b]

        @pl.when(head // heads == me)
        def _():
            load_block(block_ref, (near_delta, far_delta), order, b, nb, part, me)
            slab = jnp.concatenate([ref[:, lane_block(row_of[b])] for ref in token_refs], axis=0)
            cols = lane_block(head - me * heads)
            acc_ref[:, cols] += jnp.dot(slab, block_ref[...], preferred_element_type=F32)

    for p, j in enumerate(order):
        out_ref[row_block(me ^ j, rows), :] = acc_ref[p * rows : (p + 1) * rows, :].astype(BF16)


def project(index, total, near_delta, far_delta, pieces, nt, deps):
    nb = index.shape[1]
    rows, cols = total.shape
    return pl.pallas_call(
        with_deps(functools.partial(project_kernel, nt, nb), 4 + nt, deps),
        out_shape=jax.ShapeDtypeStruct((rows, cols), BF16),
        in_specs=vmem(4 + nt) + anywhere(deps),
        out_specs=pl.BlockSpec(memory_space=pltpu.VMEM),
        scratch_shapes=[pltpu.VMEM((rows, cols), F32), pltpu.VMEM((HEAD_DIM, HEAD_DIM), BF16)],
        compiler_params=params(),
        cost_estimate=cost(10),
        name="project",
    )(index, total, near_delta, far_delta, *pieces, *deps)


def correct_kernel(nt, nb, chunks, index_ref, near_ref, far_ref, *refs):
    keeps, recvs = refs[:chunks], refs[chunks : 2 * chunks - 1]
    out_ref, block_ref = refs[2 * chunks - 1 :]
    me = lax.axis_index("tensor")
    order = gather_order(nt)
    part = HEAD_DIM // nt
    width = out_ref.shape[1] // chunks
    for c in range(chunks):
        cols = slice(c * width, (c + 1) * width)
        own = keeps[c][:, :width].astype(F32)
        out_ref[:, cols] = own + recvs[c][:, :width].astype(F32) if c < chunks - 1 else own
    row_of = scalars(index_ref, 0, nb)
    for b in range(nb):
        load_block(block_ref.at[b], (near_ref, far_ref), order, b, nb, part, me)
        ride = slice(width + b * LANES, width + (b + 1) * LANES)
        pick = (keeps[0][:, ride].astype(F32) + recvs[0][:, ride].astype(F32)).astype(BF16)
        out_ref[:, lane_block(row_of[b])] += lax.dot_general(
            pick, block_ref[b], (((1,), (1,)), ((), ())), preferred_element_type=F32
        )


def correct(index, near, far, keeps, recvs, depth, nt, deps):
    nb = index.shape[1]
    chunks = len(keeps)
    rows = keeps[0].shape[0]
    return pl.pallas_call(
        with_deps(functools.partial(correct_kernel, nt, nb, chunks), 2 + 2 * chunks, deps),
        out_shape=jax.ShapeDtypeStruct((rows, depth), F32),
        in_specs=vmem(2 + 2 * chunks) + anywhere(deps),
        out_specs=pl.BlockSpec(memory_space=pltpu.VMEM),
        scratch_shapes=[pltpu.VMEM((nb, HEAD_DIM, HEAD_DIM), BF16)],
        compiler_params=params(),
        cost_estimate=cost(10),
        name="correct",
    )(index, near, far, *keeps, *recvs, *deps)


def final_kernel(sum_ref, recv_ref, out_ref):
    width = out_ref.shape[1] // BACK_CHUNKS
    done = out_ref.shape[1] - width
    out_ref[:, :done] = sum_ref[:, :done].astype(BF16)
    out_ref[:, done:] = (sum_ref[:, done:] + recv_ref[:, :width].astype(F32)).astype(BF16)


def final(total, recv, deps):
    return pl.pallas_call(
        with_deps(final_kernel, 2, deps),
        out_shape=jax.ShapeDtypeStruct(total.shape, BF16),
        in_specs=vmem(2) + anywhere(deps),
        out_specs=pl.BlockSpec(memory_space=pltpu.VMEM),
        compiler_params=params(),
        cost_estimate=cost(10),
        name="final",
    )(total, recv, *deps)


def on_device(tokens, base_weight, out_grad, block_index, block_owner, delta, moment1, moment2):
    nt = lax.axis_size("tensor")
    nd = lax.axis_size("dp")
    cap = delta.shape[0]
    part = HEAD_DIM // nt
    outer = bits_of(nt)[1:]
    grad_bits = bits_of(nd)
    delta_bits = grad_bits[:1] + grad_bits[:0:-1]
    grad_ways = [("tensor", 1)] + [("dp", bit) for bit in grad_bits] + [("tensor", bit) for bit in outer]
    index = block_index.T
    owner = block_owner.reshape(1, -1)
    per = BACK_PIECES // BACK_CHUNKS
    last_chunk = BACK_CHUNKS - 1

    crossed = [tokens]
    for bit in outer:
        crossed = crossed + [xor_permute(x, "tensor", bit) for x in crossed]
    far_tokens = xor_permute(tokens, "tensor", 1)

    lines = lines_of(delta, [begin()])
    order = [lines]
    pieces, sums, grads, got = {}, {}, {}, {}
    deltas = {0: (lines, xor_permute(lines, "dp", delta_bits[0]))}

    def tie(array):
        order.append(array)

    def deps():
        return order[-1:]

    def task_delta(i):
        if i > 0:
            need("delta", i - 1)
        if i < len(delta_bits) - 1:
            lines = double(*deltas[i], deps())
            tie(lines)
            deltas[i + 1] = (lines, xor_permute(lines, "dp", delta_bits[i + 1]))
        elif i == len(delta_bits) - 1:
            blocks = compact(owner, *deltas[i], delta_bits, cap, part, deps())
            tie(blocks)
            for bit in outer[:-1]:
                blocks = double(blocks, xor_permute(blocks, "tensor", bit), [])
            got["blocks"] = blocks
        else:
            need("sum", 0)
            near = unride(got["blocks"], sums[0][1], part, deps())
            tie(near)
            got["delta"] = (near, xor_permute(near, "tensor", 1))

    def task_back(i):
        keep, send = back(index, out_grad, base_weight, i, i == per - 1, nt, deps())
        tie(send)
        pieces[i] = (keep, xor_permute(send, "tensor", 1))

    def task_sum(c):
        group = range(c * per, (c + 1) * per)
        for i in group:
            need("back", i)
        riders = []
        if c == 0:
            need("delta", len(delta_bits) - 1)
            riders = [got["blocks"]]
        keeps, recvs = [pieces[i][0] for i in group], [pieces[i][1] for i in group]
        for i, bit in enumerate(outer):
            early = deps() if i == 0 else []
            keep, send = merge(keeps, recvs, riders if bit == outer[-1] else [], part, early)
            keeps, recvs = [keep], [xor_permute(send, "tensor", bit)]
        tie(keep)
        sums[c] = (keep, recvs[0])

    def task_grad(i):
        if i == 0:
            need("relay", 0)
            keep, send = block_grads(index, owner, out_grad, got["tokens"], nt, grad_bits, cap, deps())
        else:
            need("grad", i - 1)
            keep, send = halve(*grads[i - 1], deps())
        tie(send)
        grads[i] = (keep, xor_permute(send, *grad_ways[i]))

    def task_relay(i):
        parts = relay(crossed[1:], deps())
        tie(parts[0])
        got["tokens"] = crossed[:1] + parts + [far_tokens] + [xor_permute(x, "tensor", 1) for x in parts]

    def task_forward(i):
        need("relay", 0)
        got["total"] = forward(got["tokens"], base_weight, deps())
        tie(got["total"])

    def task_project(i):
        need("delta", len(delta_bits))
        need("forward", 0)
        got["projected"] = project(index, got["total"], *got["delta"], got["tokens"], nt, deps())

    def task_correct(i):
        need("delta", len(delta_bits))
        for c in range(BACK_CHUNKS):
            need("sum", c)
        keeps, recvs = zip(*[sums[c] for c in range(BACK_CHUNKS)])
        got["corrected"] = correct(index, *got["delta"], keeps, recvs[:-1], tokens.shape[1], nt, deps())
        tie(got["corrected"])

    def task_adam(i):
        need("grad", len(grad_ways) - 1)
        got["adam"] = adam(*grads[len(grad_ways) - 1], delta, moment1, moment2, deps())

    def task_final(i):
        need("correct", 0)
        got["input_grad"] = final(got["corrected"], sums[last_chunk][1], deps())

    tasks = {
        "delta": task_delta, "back": task_back, "sum": task_sum, "grad": task_grad, "relay": task_relay,
        "forward": task_forward, "project": task_project, "correct": task_correct, "adam": task_adam, "final": task_final,
    }
    run = set()

    def need(name, i):
        if (name, i) not in run:
            run.add((name, i))
            tasks[name](i)

    for name, i in ORDER:
        need(name, i)
    new_delta, first_new, second_new = got["adam"]
    return (got["projected"], got["input_grad"], new_delta, first_new, second_new)


def solution(mesh):
    placed = (
        P(("dp", "tensor"), None),
        P(None, "tensor"),
        P("dp", "tensor"),
        P(),
        P(),
        P("dp", "tensor"),
        P("dp", "tensor"),
        P("dp", "tensor"),
    )
    return jax.shard_map(
        on_device,
        mesh=mesh,
        in_specs=placed,
        out_specs=(
            P("dp", "tensor"),
            P(("dp", "tensor"), None),
            P("dp", "tensor"),
            P("dp", "tensor"),
            P("dp", "tensor"),
        ),
        check_vma=False,
    )
```

time: 47.5 us -> 42.3 us (0.89)
  waiting for transfers between devices: 17.8 us -> 6.87 us
  starting transfers between devices: 14.8 us -> 21.5 us
  Pallas kernels: 12.7 us -> 12 us
    ppermute x17 -> x18, waiting for transfers between devices: 17.8 us -> 6.87 us  [xor_permute(): return lax.ppermute(x, axis, [(i, i ^ bit) for i in range(count)])]
    ppermute x17 -> x18, starting transfers between devices: 14.8 us -> 21.5 us  [xor_permute(): return lax.ppermute(x, axis, [(i, i ^ bit) for i in range(count)])]
    pallas_call x8 -> x11, Pallas kernels: 1.98 us -> 1.61 us  [the longest x1 1.16 us: project(): pl.pallas_call(with_deps(functools.partial(project_kernel, nt, nb), 4 + n...]
    unnamed x22 -> x24, local copies, waits for them, and re-layouts: 1.08 us -> 0.75 us
  transfers between devices with their start and end apart: 17 -> 18, of which waited for: 8 -> 7; matrix products, arithmetic and copies ran while one was open for 0% -> 0% of each run, Pallas kernels for 23% -> 27%
where the time goes in v3:
time: 42.3 us; the launch traced here: 42 us
  starting transfers between devices  21.5 us (51%)
  Pallas kernels  12 us (28%)
  waiting for transfers between devices  6.87 us (16%)
  between operations  0.89 us (2%)
  local copies, waits for them, and re-layouts  0.75 us (2%)
    ppermute x18, starting transfers between devices, xor_permute(): return lax.ppermute(x, axis, [(i, i ^ bit) for i in range(count)])  21.5 us
    ppermute x18, waiting for transfers between devices, xor_permute(): return lax.ppermute(x, axis, [(i, i ^ bit) for i in range(count)])  6.87 us
    pallas_call x4, Pallas kernels, back(): pl.pallas_call(with_deps(functools.partial(back_kernel, nt, nb, piece * w...  5.25 us
    pallas_call x1, Pallas kernels, forward(): pl.pallas_call(with_deps(functools.partial(forward_kernel, count), count...  2.42 us
    pallas_call x1, Pallas kernels, project(): pl.pallas_call(with_deps(functools.partial(project_kernel, nt, nb), 4 + n...  1.16 us
    pallas_call x1, Pallas kernels, final(): pl.pallas_call(with_deps(final_kernel, 2, deps), out_shape=jax.ShapeDtype...  0.87 us
  transfers between devices with their start and end apart: 18, of which 7 were waited for; matrix products, arithmetic and copies ran while one was open for 0% of the time, Pallas kernels for 27%

profile of v3, /device:TPU:0, one launch (start us, length us, event | category | flops | bytes accessed | tf_op | source)
XLA Modules:
  0.0 42.0 jit_solution(2527389634473278645)
XLA Ops:
  0.7 0.7 %copy-done.4 = bf16[2,4096]{1,0:T(2,128)(2,1)S(1)} copy-done((bf16[2,4096]{1,0:T(2,128)(2,1)S(1)}, bf16[2,4096]{1,0:T(2,128)(2,1)}, u32[]{:S(2)}) %copy-start.4) | copy-done | bytes 16408
  1.4 3.0 %collective-permute-start.1 = (bf16[64,128]{1,0:T(8,128)(2,1)S(1)}, bf16[64,128]{1,0:T(8,128)(2,1)S(1)}, u32[]{:S(2)}, u32[]{:S(2)}) collective-permute-start(bf16[64,128]{1,0:T(8,128)(2,1)S(1)} %lines.1.refs_0_.refs_2_), channel_id=1, source_target_pairs={{0,4},{4,0},{8,12},{12,8},{16,20},{20,16},{24,28},{28,24},{1,5},{5... | collective-permute-start | bytes 49160 | tf_op jit(solution)/shard_map/ppermute | solution.py:70
  4.5 1.5 %collective-permute-start = (bf16[32,8192]{1,0:T(8,128)(2,1)S(1)}, bf16[32,8192]{1,0:T(8,128)(2,1)S(1)}, u32[]{:S(2)}, u32[]{:S(2)}) collective-permute-start(bf16[32,8192]{1,0:T(8,128)(2,1)S(1)} %copy-done), channel_id=1, source_target_pairs={{0,2},{1,3},{2,0},{3,1},{4,6},{5,7},{6,4},{7,5},{8,10},{9,11},{10,... | collective-permute-start | bytes 1572872 | tf_op jit(solution)/shard_map/ppermute | solution.py:70
  6.0 0.2 collective-permute-done.1.refs_1_
  6.2 3.1 %collective-permute-start.2 = (bf16[128,128]{1,0:T(8,128)(2,1)S(1)}, bf16[128,128]{1,0:T(8,128)(2,1)S(1)}, u32[]{:S(2)}, u32[]{:S(2)}) collective-permute-start(bf16[128,128]{1,0:T(8,128)(2,1)S(1)} %double.2.refs_3_.refs_0_), channel_id=1, source_target_pairs={{0,16},{4,20},{8,24},{12,28},{16,0},{20,4},{24,8},{28,12},{1,17},{... | collective-permute-start | bytes 98312 | tf_op jit(solution)/shard_map/ppermute | solution.py:70
  9.3 1.3 %back.4 = (bf16[64,2048]{1,0:T(8,128)(2,1)S(1)}, bf16[64,2048]{1,0:T(8,128)(2,1)S(1)}) custom-call(s32[2,8]{1,0:T(2,128)S(1)} %bitcast.4, bf16[128,1024]{1,0:T(8,128)(2,1)S(1)} %copy-done.1, bf16[8192,1024]{1,0:T(8,128)(2,1)S(1)} %bitcast.3, bf16[128,128]{1,0:T(8,128)(2,1)S(1)} %double.2.refs_3_.refs_0_), custom_call_target="tpu_custom_call" | custom-call | flops 10000000000 | bytes 10000000 | tf_op jit(solution)/shard_map/back/pallas_call | solution.py:369
  10.7 0.8 %collective-permute-done.2.refs_1_ = bf16[128,128]{1,0:T(8,128)(2,1)S(1)} collective-permute-done((bf16[128,128]{1,0:T(8,128)(2,1)S(1)}, bf16[128,128]{1,0:T(8,128)(2,1)S(1)}, u32[]{:S(2)}, u32[]{:S(2)}) %collective-permute-start.2) | collective-permute-done | bytes 32800 | tf_op jit(solution)/shard_map/ppermute | solution.py:70
  11.5 1.6 %collective-permute-start.5 = (bf16[256,128]{1,0:T(8,128)(2,1)S(1)}, bf16[256,128]{1,0:T(8,128)(2,1)S(1)}, u32[]{:S(2)}, u32[]{:S(2)}) collective-permute-start(bf16[256,128]{1,0:T(8,128)(2,1)S(1)} %double.3.refs_3_.refs_1_), channel_id=1, source_target_pairs={{0,8},{4,12},{8,0},{12,4},{16,24},{20,28},{24,16},{28,20},{1,9},{5... | collective-permute-start | bytes 196616 | tf_op jit(solution)/shard_map/ppermute | solution.py:70
  13.2 1.3 %back.5 = (bf16[64,3072]{1,0:T(8,128)(2,1)S(1)}, bf16[64,3072]{1,0:T(8,128)(2,1)S(1)}) custom-call(s32[2,8]{1,0:T(2,128)S(1)} %bitcast.5, bf16[128,1024]{1,0:T(8,128)(2,1)S(1)} %copy-done.1, bf16[8192,1024]{1,0:T(8,128)(2,1)S(1)} %bitcast.3, bf16[256,128]{1,0:T(8,128)(2,1)S(1)} %double.3.refs_3_.refs_1_), custom_call_target="tpu_custom_call" | custom-call | flops 10000000000 | bytes 10000000 | tf_op jit(solution)/shard_map/back/pallas_call | solution.py:369
  14.6 1.3 %collective-permute-done.5.refs_2_ = bf16[256,128]{1,0:T(8,128)(2,1)S(1)} collective-permute-done((bf16[256,128]{1,0:T(8,128)(2,1)S(1)}, bf16[256,128]{1,0:T(8,128)(2,1)S(1)}, u32[]{:S(2)}, u32[]{:S(2)}) %collective-permute-start.5) | collective-permute-done | bytes 65568 | tf_op jit(solution)/shard_map/ppermute | solution.py:70
  15.9 0.2 compact_step.1.refs_4_.refs_5_.refs_0_
  16.0 0.2 collective-permute-done.4.refs_3_
  16.3 0.2 merge.2
  16.4 1.6 %collective-permute-start.12 = (bf16[32,6144]{1,0:T(8,128)(2,1)S(1)}, bf16[32,6144]{1,0:T(8,128)(2,1)S(1)}, u32[]{:S(2)}, u32[]{:S(2)}) collective-permute-start(bf16[32,6144]{1,0:T(8,128)(2,1)S(1)} %get-tuple-element.45), channel_id=1, source_target_pairs={{0,2},{1,3},{2,0},{3,1},{4,6},{5,7},{6,4},{7,5},{8,10},{9,11},{10,... | collective-permute-start | bytes 1179656 | tf_op jit(solution)/shard_map/ppermute | solution.py:70
  18.1 1.3 %back.6 = (bf16[64,2048]{1,0:T(8,128)(2,1)S(1)}, bf16[64,2048]{1,0:T(8,128)(2,1)S(1)}) custom-call(s32[2,8]{1,0:T(2,128)S(1)} %bitcast.6, bf16[128,1024]{1,0:T(8,128)(2,1)S(1)} %copy-done.1, bf16[8192,1024]{1,0:T(8,128)(2,1)S(1)} %bitcast.3, bf16[32,8192]{1,0:T(8,128)(2,1)S(1)} %relay.1.refs_3_.refs_4_.refs_1_.refs_5_), custom_call_target="tpu_custom_call" | custom-call | flops 10000000000 | bytes 10000000 | tf_op jit(solution)/shard_map/back/pallas_call | solution.py:369
  19.4 0.6 %collective-permute-start.10 = (bf16[64,2048]{1,0:T(8,128)(2,1)S(1)}, bf16[64,2048]{1,0:T(8,128)(2,1)S(1)}, u32[]{:S(2)}, u32[]{:S(2)}) collective-permute-start(bf16[64,2048]{1,0:T(8,128)(2,1)S(1)} %get-tuple-element.35.refs_7_), channel_id=1, source_target_pairs={{0,1},{1,0},{2,3},{3,2},{4,5},{5,4},{6,7},{7,6},{8,9},{9,8},{10,11... | collective-permute-start | bytes 786440 | tf_op jit(solution)/shard_map/ppermute | solution.py:70
  20.0 0.7 %block_grads.1 = (bf16[1024,128]{1,0:T(8,128)(2,1)S(1)}, bf16[1024,128]{1,0:T(8,128)(2,1)S(1)}) custom-call(s32[2,8]{1,0:T(2,128)S(1)} %bitcast.7, s32[1,8]{1,0:T(1,128)S(1)} %bitcast.12, bf16[128,1024]{1,0:T(8,128)(2,1)S(1)} %copy-done.1, bf16[32,8192]{1,0:T(8,128)(2,1)S(1)} %copy-done, bf16[32,8192]{1,0:T(8,128)(2,1)S(1)} %relay.1.refs_3_.refs_4_.refs_1_.refs_5_, ...), custom_call_target="tpu_custom_call" | custom-call | flops 10000000000 | bytes 10000000 | tf_op jit(solution)/shard_map/block_grads/pallas_call | solution.py:271
  20.7 1.3 %back.7 = (bf16[64,2048]{1,0:T(8,128)(2,1)S(1)}, bf16[64,2048]{1,0:T(8,128)(2,1)S(1)}) custom-call(s32[2,8]{1,0:T(2,128)S(1)} %bitcast.8, bf16[128,1024]{1,0:T(8,128)(2,1)S(1)} %copy-done.1, bf16[8192,1024]{1,0:T(8,128)(2,1)S(1)} %bitcast.3, bf16[1024,128]{1,0:T(8,128)(2,1)S(1)} %get-tuple-element.37.refs_3_), custom_call_target="tpu_custom_call" | custom-call | flops 10000000000 | bytes 10000000 | tf_op jit(solution)/shard_map/back/pallas_call | solution.py:369
  22.1 0.6 %collective-permute-start.11 = (bf16[64,2048]{1,0:T(8,128)(2,1)S(1)}, bf16[64,2048]{1,0:T(8,128)(2,1)S(1)}, u32[]{:S(2)}, u32[]{:S(2)}) collective-permute-start(bf16[64,2048]{1,0:T(8,128)(2,1)S(1)} %get-tuple-element.38.refs_2_), channel_id=1, source_target_pairs={{0,1},{1,0},{2,3},{3,2},{4,5},{5,4},{6,7},{7,6},{8,9},{9,8},{10,11... | collective-permute-start | bytes 786440 | tf_op jit(solution)/shard_map/ppermute | solution.py:70
  22.7 1.6 %collective-permute-start.9 = (bf16[512,128]{1,0:T(8,128)(2,1)S(1)}, bf16[512,128]{1,0:T(8,128)(2,1)S(1)}, u32[]{:S(2)}, u32[]{:S(2)}) collective-permute-start(bf16[512,128]{1,0:T(8,128)(2,1)S(1)} %get-tuple-element.40.refs_4_), channel_id=1, source_target_pairs={{0,4},{4,0},{8,12},{12,8},{16,20},{20,16},{24,28},{28,24},{1,5},{5... | collective-permute-start | bytes 393224 | tf_op jit(solution)/shard_map/ppermute | solution.py:70
  24.4 1.5 %collective-permute-start.15 = (bf16[32,4096]{1,0:T(8,128)(2,1)S(1)}, bf16[32,4096]{1,0:T(8,128)(2,1)S(1)}, u32[]{:S(2)}, u32[]{:S(2)}) collective-permute-start(bf16[32,4096]{1,0:T(8,128)(2,1)S(1)} %get-tuple-element.48), channel_id=1, source_target_pairs={{0,2},{1,3},{2,0},{3,1},{4,6},{5,7},{6,4},{7,5},{8,10},{9,11},{10,... | collective-permute-start | bytes 786440 | tf_op jit(solution)/shard_map/ppermute | solution.py:70
  25.9 2.3 %collective-permute-done.9.refs_1_ = bf16[512,128]{1,0:T(8,128)(2,1)S(1)} collective-permute-done((bf16[512,128]{1,0:T(8,128)(2,1)S(1)}, bf16[512,128]{1,0:T(8,128)(2,1)S(1)}, u32[]{:S(2)}, u32[]{:S(2)}) %collective-permute-start.9) | collective-permute-done | bytes 131104 | tf_op jit(solution)/shard_map/ppermute | solution.py:70
  28.2 1.5 %collective-permute-start.14 = (bf16[256,128]{1,0:T(8,128)(2,1)S(1)}, bf16[256,128]{1,0:T(8,128)(2,1)S(1)}, u32[]{:S(2)}, u32[]{:S(2)}) collective-permute-start(bf16[256,128]{1,0:T(8,128)(2,1)S(1)} %get-tuple-element.44.refs_5_), channel_id=1, source_target_pairs={{0,8},{4,12},{8,0},{12,4},{16,24},{20,28},{24,16},{28,20},{1,9},{5... | collective-permute-start | bytes 196616 | tf_op jit(solution)/shard_map/ppermute | solution.py:70
  29.7 2.4 %forward.1.refs_2_.refs_1_ = f32[128,1024]{1,0:T(8,128)S(1)} custom-call(bf16[32,8192]{1,0:T(8,128)(2,1)S(1)} %copy-done, bf16[32,8192]{1,0:T(8,128)(2,1)S(1)} %relay.1.refs_3_.refs_4_.refs_1_.refs_5_, bf16[32,8192]{1,0:T(8,128)(2,1)S(1)} %collective-permute-done.6.refs_5_.refs_2_.refs_6_, ...), custom_call_target="tpu_custom_call" | custom-call | flops 10000000000 | bytes 10000000 | tf_op jit(solution)/shard_map/forward/pallas_call | solution.py:432
  32.3 0.3 collective-permute-done.14.refs_1_
  32.6 2.9 %collective-permute-start.16 = (bf16[128,128]{1,0:T(8,128)(2,1)S(1)}, bf16[128,128]{1,0:T(8,128)(2,1)S(1)}, u32[]{:S(2)}, u32[]{:S(2)}) collective-permute-start(bf16[128,128]{1,0:T(8,128)(2,1)S(1)} %get-tuple-element.47.refs_6_), channel_id=1, source_target_pairs={{0,16},{4,20},{8,24},{12,28},{16,0},{20,4},{24,8},{28,12},{1,17},{... | collective-permute-start | bytes 98312 | tf_op jit(solution)/shard_map/ppermute | solution.py:70
  35.5 0.3 correct.1.refs_8_.refs_2_.refs_0_
  35.8 1.7 %collective-permute-done.16.refs_1_ = bf16[128,128]{1,0:T(8,128)(2,1)S(1)} collective-permute-done((bf16[128,128]{1,0:T(8,128)(2,1)S(1)}, bf16[128,128]{1,0:T(8,128)(2,1)S(1)}, u32[]{:S(2)}, u32[]{:S(2)}) %collective-permute-start.16) | collective-permute-done | bytes 32800 | tf_op jit(solution)/shard_map/ppermute | solution.py:70
  37.5 1.8 %collective-permute-start.17 = (bf16[64,128]{1,0:T(8,128)(2,1)S(1)}, bf16[64,128]{1,0:T(8,128)(2,1)S(1)}, u32[]{:S(2)}, u32[]{:S(2)}) collective-permute-start(bf16[64,128]{1,0:T(8,128)(2,1)S(1)} %get-tuple-element.50.refs_2_.refs_5_), channel_id=1, source_target_pairs={{0,2},{1,3},{2,0},{3,1},{4,6},{5,7},{6,4},{7,5},{8,10},{9,11},{10,... | collective-permute-start | bytes 49160 | tf_op jit(solution)/shard_map/ppermute | solution.py:70
  39.3 1.2 %project.1 = bf16[128,1024]{1,0:T(8,128)(2,1)} custom-call(s32[2,8]{1,0:T(2,128)S(1)} %bitcast.10, f32[128,1024]{1,0:T(8,128)S(1)} %forward.1.refs_2_.refs_1_, bf16[512,128]{1,0:T(8,128)(2,1)S(1)} %unride.1.refs_2_.refs_1_, bf16[512,128]{1,0:T(8,128)(2,1)S(1)} %collective-permute-done.13.refs_2_.refs_3_, bf16[32,8192]{1,0:T(8,128)(2,1)S(1)} %copy-done, ...), custom_call_target="tpu_custom_call" | custom-call | flops 10000000000 | bytes 10000000 | tf_op jit(solution)/shard_map/project/pallas_call | solution.py:471
  40.4 0.9 %final.1 = bf16[32,8192]{1,0:T(8,128)(2,1)} custom-call(f32[32,8192]{1,0:T(8,128)S(1)} %correct.1.refs_8_.refs_2_.refs_0_, bf16[32,4096]{1,0:T(8,128)(2,1)S(1)} %collective-permute-done.15.refs_1_, bf16[64,128]{1,0:T(8,128)(2,1)S(1)} %get-tuple-element.50.refs_2_.refs_5_), custom_call_target="tpu_custom_call" | custom-call | flops 10000000000 | bytes 10000000 | tf_op jit(solution)/shard_map/final/pallas_call | solution.py:528
  41.3 0.7 %adam.1 = (bf16[2,4096]{1,0:T(2,128)(2,1)}, f32[2,4096]{1,0:T(2,128)}, f32[2,4096]{1,0:T(2,128)}) custom-call(bf16[64,128]{1,0:T(8,128)(2,1)S(1)} %get-tuple-element.51.refs_0_, bf16[64,128]{1,0:T(8,128)(2,1)S(1)} %collective-permute-done.17.refs_1_, bf16[2,4096]{1,0:T(2,128)(2,1)S(1)} %copy-done.5, f32[2,4096]{1,0:T(2,128)S(1)} %copy-done.2, ...), custom_call_target="tpu_custom_call" | custom-call | flops 10000000000 | bytes 10000000 | tf_op jit(solution)/shard_map/adam/pallas_call | solution.py:322
  (52 shorter events, 0.8 us)
Async XLA Ops:
  0.6 0.7 %copy-start.4 = (bf16[2,4096]{1,0:T(2,128)(2,1)S(1)}, bf16[2,4096]{1,0:T(2,128)(2,1)}, u32[]{:S(2)}) copy-start(bf16[2,4096]{1,0:T(2,128)(2,1)} %refs_2_.11) | copy-start | bytes 49156
  1.4 3.1 %copy-start = (bf16[32,8192]{1,0:T(8,128)(2,1)S(1)}, bf16[32,8192]{1,0:T(8,128)(2,1)}, u32[]{:S(2)}) copy-start(bf16[32,8192]{1,0:T(8,128)(2,1)} %refs_4_.4) | copy-start | bytes 1572868
  1.4 7.9 %slice-start = ((s8[16777216]{0:T(1024)(128)(4,1)}), s8[4194304]{0:T(1024)(128)(4,1)S(1)}, s32[]{:S(2)}) async-start(s8[16777216]{0:T(1024)(128)(4,1)} %bitcast.2), calls=%async_computation | async-start | bytes 8388608
  1.4 7.9 %slice-start.1 = ((s8[16777216]{0:T(1024)(128)(4,1)}), s8[4194304]{0:T(1024)(128)(4,1)S(1)}, s32[]{:S(2)}) async-start(s8[16777216]{0:T(1024)(128)(4,1)} %bitcast.2), calls=%async_computation.1 | async-start | bytes 8388608
  1.4 7.9 %slice-start.2 = ((s8[16777216]{0:T(1024)(128)(4,1)}), s8[4194304]{0:T(1024)(128)(4,1)S(1)}, s32[]{:S(2)}) async-start(s8[16777216]{0:T(1024)(128)(4,1)} %bitcast.2), calls=%async_computation.2 | async-start | bytes 8388608
  1.4 7.9 %slice-start.3 = ((s8[16777216]{0:T(1024)(128)(4,1)}), s8[4194304]{0:T(1024)(128)(4,1)S(1)}, s32[]{:S(2)}) async-start(s8[16777216]{0:T(1024)(128)(4,1)} %bitcast.2), calls=%async_computation.3 | async-start | bytes 8388608
  1.4 7.9 %copy-start.1 = (bf16[128,1024]{1,0:T(8,128)(2,1)S(1)}, bf16[128,1024]{1,0:T(8,128)(2,1)}, u32[]{:S(2)}) copy-start(bf16[128,1024]{1,0:T(8,128)(2,1)} %refs_1_.7) | copy-start | bytes 786436
  1.4 7.9 %copy-start.6 = (s32[8,2]{0,1:T(2,128)S(1)}, s32[8,2]{0,1:T(2,128)}, u32[]{:S(2)}) copy-start(s32[8,2]{0,1:T(2,128)} %param.11) | copy-start | bytes 196
  1.4 4.8 %collective-permute-start.1 = (bf16[64,128]{1,0:T(8,128)(2,1)S(1)}, bf16[64,128]{1,0:T(8,128)(2,1)S(1)}, u32[]{:S(2)}, u32[]{:S(2)}) collective-permute-start(bf16[64,128]{1,0:T(8,128)(2,1)S(1)} %lines.1.refs_0_.refs_2_), channel_id=1, source_target_pairs={{0,4},{4,0},{8,12},{12,8},{16,20},{20,16},{24,28},{28,24},{1,5},{5... | collective-permute-start | bytes 49160 | tf_op jit(solution)/shard_map/ppermute | solution.py:70
  4.5 13.5 %collective-permute-start = (bf16[32,8192]{1,0:T(8,128)(2,1)S(1)}, bf16[32,8192]{1,0:T(8,128)(2,1)S(1)}, u32[]{:S(2)}, u32[]{:S(2)}) collective-permute-start(bf16[32,8192]{1,0:T(8,128)(2,1)S(1)} %copy-done), channel_id=1, source_target_pairs={{0,2},{1,3},{2,0},{3,1},{4,6},{5,7},{6,4},{7,5},{8,10},{9,11},{10,... | collective-permute-start | bytes 1572872 | tf_op jit(solution)/shard_map/ppermute | solution.py:70
  6.0 14.0 %collective-permute-start.6 = (bf16[32,8192]{1,0:T(8,128)(2,1)S(1)}, bf16[32,8192]{1,0:T(8,128)(2,1)S(1)}, u32[]{:S(2)}, u32[]{:S(2)}) collective-permute-start(bf16[32,8192]{1,0:T(8,128)(2,1)S(1)} %copy-done), channel_id=1, source_target_pairs={{0,1},{1,0},{2,3},{3,2},{4,5},{5,4},{6,7},{7,6},{8,9},{9,8},{10,11... | collective-permute-start | bytes 1572872 | tf_op jit(solution)/shard_map/ppermute | solution.py:70
  6.2 5.3 %collective-permute-start.2 = (bf16[128,128]{1,0:T(8,128)(2,1)S(1)}, bf16[128,128]{1,0:T(8,128)(2,1)S(1)}, u32[]{:S(2)}, u32[]{:S(2)}) collective-permute-start(bf16[128,128]{1,0:T(8,128)(2,1)S(1)} %double.2.refs_3_.refs_0_), channel_id=1, source_target_pairs={{0,16},{4,20},{8,24},{12,28},{16,0},{20,4},{24,8},{28,12},{1,17},{... | collective-permute-start | bytes 98312 | tf_op jit(solution)/shard_map/ppermute | solution.py:70
  10.6 5.4 %collective-permute-start.3 = (bf16[64,2048]{1,0:T(8,128)(2,1)S(1)}, bf16[64,2048]{1,0:T(8,128)(2,1)S(1)}, u32[]{:S(2)}, u32[]{:S(2)}) collective-permute-start(bf16[64,2048]{1,0:T(8,128)(2,1)S(1)} %get-tuple-element.31.refs_2_), channel_id=1, source_target_pairs={{0,1},{1,0},{2,3},{3,2},{4,5},{5,4},{6,7},{7,6},{8,9},{9,8},{10,11... | collective-permute-start | bytes 786440 | tf_op jit(solution)/shard_map/ppermute | solution.py:70
  11.5 4.3 %copy-start.7 = (s32[8]{0:T(128)S(1)}, s32[8]{0:T(128)}, u32[]{:S(2)}) copy-start(s32[8]{0:T(128)} %param.12) | copy-start | bytes 100
  11.5 4.3 %collective-permute-start.5 = (bf16[256,128]{1,0:T(8,128)(2,1)S(1)}, bf16[256,128]{1,0:T(8,128)(2,1)S(1)}, u32[]{:S(2)}, u32[]{:S(2)}) collective-permute-start(bf16[256,128]{1,0:T(8,128)(2,1)S(1)} %double.3.refs_3_.refs_1_), channel_id=1, source_target_pairs={{0,8},{4,12},{8,0},{12,4},{16,24},{20,28},{24,16},{28,20},{1,9},{5... | collective-permute-start | bytes 196616 | tf_op jit(solution)/shard_map/ppermute | solution.py:70
  14.5 1.8 %collective-permute-start.4 = (bf16[64,3072]{1,0:T(8,128)(2,1)S(1)}, bf16[64,3072]{1,0:T(8,128)(2,1)S(1)}, u32[]{:S(2)}, u32[]{:S(2)}) collective-permute-start(bf16[64,3072]{1,0:T(8,128)(2,1)S(1)} %get-tuple-element.33.refs_3_), channel_id=1, source_target_pairs={{0,1},{1,0},{2,3},{3,2},{4,5},{5,4},{6,7},{7,6},{8,9},{9,8},{10,11... | collective-permute-start | bytes 1179656 | tf_op jit(solution)/shard_map/ppermute | solution.py:70
  16.4 15.7 %collective-permute-start.12 = (bf16[32,6144]{1,0:T(8,128)(2,1)S(1)}, bf16[32,6144]{1,0:T(8,128)(2,1)S(1)}, u32[]{:S(2)}, u32[]{:S(2)}) collective-permute-start(bf16[32,6144]{1,0:T(8,128)(2,1)S(1)} %get-tuple-element.45), channel_id=1, source_target_pairs={{0,2},{1,3},{2,0},{3,1},{4,6},{5,7},{6,4},{7,5},{8,10},{9,11},{10,... | collective-permute-start | bytes 1179656 | tf_op jit(solution)/shard_map/ppermute | solution.py:70
  18.0 2.0 %collective-permute-start.7 = (bf16[32,8192]{1,0:T(8,128)(2,1)S(1)}, bf16[32,8192]{1,0:T(8,128)(2,1)S(1)}, u32[]{:S(2)}, u32[]{:S(2)}) collective-permute-start(bf16[32,8192]{1,0:T(8,128)(2,1)S(1)} %relay.1.refs_3_.refs_4_.refs_1_.refs_5_), channel_id=1, source_target_pairs={{0,1},{1,0},{2,3},{3,2},{4,5},{5,4},{6,7},{7,6},{8,9},{9,8},{10,11... | collective-permute-start | bytes 1572872 | tf_op jit(solution)/shard_map/ppermute | solution.py:70
  19.4 4.9 %collective-permute-start.10 = (bf16[64,2048]{1,0:T(8,128)(2,1)S(1)}, bf16[64,2048]{1,0:T(8,128)(2,1)S(1)}, u32[]{:S(2)}, u32[]{:S(2)}) collective-permute-start(bf16[64,2048]{1,0:T(8,128)(2,1)S(1)} %get-tuple-element.35.refs_7_), channel_id=1, source_target_pairs={{0,1},{1,0},{2,3},{3,2},{4,5},{5,4},{6,7},{7,6},{8,9},{9,8},{10,11... | collective-permute-start | bytes 786440 | tf_op jit(solution)/shard_map/ppermute | solution.py:70
  20.7 2.0 %collective-permute-start.8 = (bf16[1024,128]{1,0:T(8,128)(2,1)S(1)}, bf16[1024,128]{1,0:T(8,128)(2,1)S(1)}, u32[]{:S(2)}, u32[]{:S(2)}) collective-permute-start(bf16[1024,128]{1,0:T(8,128)(2,1)S(1)} %get-tuple-element.37.refs_3_), channel_id=1, source_target_pairs={{0,1},{1,0},{2,3},{3,2},{4,5},{5,4},{6,7},{7,6},{8,9},{9,8},{10,11... | collective-permute-start | bytes 786440 | tf_op jit(solution)/shard_map/ppermute | solution.py:70
  22.1 2.2 %collective-permute-start.11 = (bf16[64,2048]{1,0:T(8,128)(2,1)S(1)}, bf16[64,2048]{1,0:T(8,128)(2,1)S(1)}, u32[]{:S(2)}, u32[]{:S(2)}) collective-permute-start(bf16[64,2048]{1,0:T(8,128)(2,1)S(1)} %get-tuple-element.38.refs_2_), channel_id=1, source_target_pairs={{0,1},{1,0},{2,3},{3,2},{4,5},{5,4},{6,7},{7,6},{8,9},{9,8},{10,11... | collective-permute-start | bytes 786440 | tf_op jit(solution)/shard_map/ppermute | solution.py:70
  22.7 5.5 %collective-permute-start.9 = (bf16[512,128]{1,0:T(8,128)(2,1)S(1)}, bf16[512,128]{1,0:T(8,128)(2,1)S(1)}, u32[]{:S(2)}, u32[]{:S(2)}) collective-permute-start(bf16[512,128]{1,0:T(8,128)(2,1)S(1)} %get-tuple-element.40.refs_4_), channel_id=1, source_target_pairs={{0,4},{4,0},{8,12},{12,8},{16,20},{20,16},{24,28},{28,24},{1,5},{5... | collective-permute-start | bytes 393224 | tf_op jit(solution)/shard_map/ppermute | solution.py:70
  24.4 16.0 %collective-permute-start.15 = (bf16[32,4096]{1,0:T(8,128)(2,1)S(1)}, bf16[32,4096]{1,0:T(8,128)(2,1)S(1)}, u32[]{:S(2)}, u32[]{:S(2)}) collective-permute-start(bf16[32,4096]{1,0:T(8,128)(2,1)S(1)} %get-tuple-element.48), channel_id=1, source_target_pairs={{0,2},{1,3},{2,0},{3,1},{4,6},{5,7},{6,4},{7,5},{8,10},{9,11},{10,... | collective-permute-start | bytes 786440 | tf_op jit(solution)/shard_map/ppermute | solution.py:70
  28.2 4.3 %collective-permute-start.14 = (bf16[256,128]{1,0:T(8,128)(2,1)S(1)}, bf16[256,128]{1,0:T(8,128)(2,1)S(1)}, u32[]{:S(2)}, u32[]{:S(2)}) collective-permute-start(bf16[256,128]{1,0:T(8,128)(2,1)S(1)} %get-tuple-element.44.refs_5_), channel_id=1, source_target_pairs={{0,8},{4,12},{8,0},{12,4},{16,24},{20,28},{24,16},{28,20},{1,9},{5... | collective-permute-start | bytes 196616 | tf_op jit(solution)/shard_map/ppermute | solution.py:70
  32.2 3.3 %collective-permute-start.13 = (bf16[512,128]{1,0:T(8,128)(2,1)S(1)}, bf16[512,128]{1,0:T(8,128)(2,1)S(1)}, u32[]{:S(2)}, u32[]{:S(2)}) collective-permute-start(bf16[512,128]{1,0:T(8,128)(2,1)S(1)} %unride.1.refs_2_.refs_1_), channel_id=1, source_target_pairs={{0,1},{1,0},{2,3},{3,2},{4,5},{5,4},{6,7},{7,6},{8,9},{9,8},{10,11... | collective-permute-start | bytes 393224 | tf_op jit(solution)/shard_map/ppermute | solution.py:70
  32.6 4.9 %collective-permute-start.16 = (bf16[128,128]{1,0:T(8,128)(2,1)S(1)}, bf16[128,128]{1,0:T(8,128)(2,1)S(1)}, u32[]{:S(2)}, u32[]{:S(2)}) collective-permute-start(bf16[128,128]{1,0:T(8,128)(2,1)S(1)} %get-tuple-element.47.refs_6_), channel_id=1, source_target_pairs={{0,16},{4,20},{8,24},{12,28},{16,0},{20,4},{24,8},{28,12},{1,17},{... | collective-permute-start | bytes 98312 | tf_op jit(solution)/shard_map/ppermute | solution.py:70
  37.5 3.8 %collective-permute-start.17 = (bf16[64,128]{1,0:T(8,128)(2,1)S(1)}, bf16[64,128]{1,0:T(8,128)(2,1)S(1)}, u32[]{:S(2)}, u32[]{:S(2)}) collective-permute-start(bf16[64,128]{1,0:T(8,128)(2,1)S(1)} %get-tuple-element.50.refs_2_.refs_5_), channel_id=1, source_target_pairs={{0,2},{1,3},{2,0},{3,1},{4,6},{5,7},{6,4},{7,5},{8,10},{9,11},{10,... | collective-permute-start | bytes 49160 | tf_op jit(solution)/shard_map/ppermute | solution.py:70
  40.4 0.9 %copy-start.2 = (f32[2,4096]{1,0:T(2,128)S(1)}, f32[2,4096]{1,0:T(2,128)}, u32[]{:S(2)}) copy-start(f32[2,4096]{1,0:T(2,128)} %refs_3_.3) | copy-start | bytes 98308
  40.4 0.9 %copy-start.3 = (f32[2,4096]{1,0:T(2,128)S(1)}, f32[2,4096]{1,0:T(2,128)}, u32[]{:S(2)}) copy-start(f32[2,4096]{1,0:T(2,128)} %refs_4_.5) | copy-start | bytes 98308
  40.4 0.9 %copy-start.5 = (bf16[2,4096]{1,0:T(2,128)(2,1)S(1)}, bf16[2,4096]{1,0:T(2,128)(2,1)}, u32[]{:S(2)}) copy-start(bf16[2,4096]{1,0:T(2,128)(2,1)} %refs_2_.11) | copy-start | bytes 49156

commit v4 on v3

--- a/solution.py
+++ b/solution.py
@@ -17,8 +17,10 @@
 VMEM_LIMIT = 24 * 1024 * 1024
 BACK_PIECES = 4
 BACK_CHUNKS = 2
+PAUSE = 30
+FIRST = 30
 ORDER = (
-    ("delta", 0), ("back", 0), ("delta", 1), ("back", 1), ("delta", 2), ("sum", 0), ("relay", 0), ("back", 2), ("grad", 0), ("back", 3), ("grad", 1), ("sum", 1), ("grad", 2), ("forward", 0), ("delta", 3), ("grad", 3), ("correct", 0), ("project", 0), ("grad", 4), ("final", 0), ("adam", 0),
+    ("back", 0), ("delta", 0), ("back", 1), ("back", 2), ("sum", 0), ("relay", 0), ("back", 3), ("grad", 0), ("delta", 1), ("grad", 1), ("sum", 1), ("grad", 2), ("forward", 0), ("grad", 3), ("delta", 3), ("grad", 4), ("correct", 0), ("project", 0), ("final", 0), ("adam", 0),
 )
 
 
@@ -105,7 +107,7 @@
         refs[count + i][...] = refs[i][...]
 
 
-def relay(parts, deps):
+def relay(parts, deps, us=10):
     count = len(parts)
     return list(
         pl.pallas_call(
@@ -114,25 +116,26 @@
             in_specs=vmem(count) + anywhere(deps),
             out_specs=vmem(count),
             compiler_params=params(),
-            cost_estimate=cost(10),
+            cost_estimate=cost(us),
             name="relay",
         )(*parts, *deps)
     )
 
 
-def begin_kernel(out_ref):
+def pause_kernel(out_ref):
     out_ref[...] = jnp.zeros_like(out_ref)
 
 
-def begin():
-    return pl.pallas_call(
-        begin_kernel,
+def pause(deps, us):
+    return pl.pallas_call(
+        with_deps(pause_kernel, 0, deps),
         out_shape=jax.ShapeDtypeStruct((8, LANES), F32),
-        out_specs=pl.BlockSpec(memory_space=pltpu.VMEM),
-        compiler_params=params(),
-        cost_estimate=cost(30),
-        name="begin",
-    )()
+        in_specs=anywhere(deps),
+        out_specs=pl.BlockSpec(memory_space=pltpu.VMEM),
+        compiler_params=params(),
+        cost_estimate=cost(us),
+        name="pause",
+    )(*deps)
 
 
 def line_kernel(delta_ref, out_ref):
@@ -550,13 +553,14 @@
     per = BACK_PIECES // BACK_CHUNKS
     last_chunk = BACK_CHUNKS - 1
 
-    crossed = [tokens]
+    (own,) = relay([tokens], [pause([], PAUSE)], FIRST)
+    crossed = [own]
     for bit in outer:
         crossed = crossed + [xor_permute(x, "tensor", bit) for x in crossed]
-    far_tokens = xor_permute(tokens, "tensor", 1)
-
-    lines = lines_of(delta, [begin()])
-    order = [lines]
+    far_tokens = xor_permute(own, "tensor", 1)
+
+    lines = lines_of(delta, [own])
+    order = [pause([lines], 3)]
     pieces, sums, grads, got = {}, {}, {}, {}
     deltas = {0: (lines, xor_permute(lines, "dp", delta_bits[0]))}
 
@@ -580,8 +584,8 @@
                 blocks = double(blocks, xor_permute(blocks, "tensor", bit), [])
             got["blocks"] = blocks
         else:
-            need("sum", 0)
-            near = unride(got["blocks"], sums[0][1], part, deps())
+            need("sum", last_chunk)
+            near = unride(got["blocks"], sums[last_chunk][1], part, deps())
             tie(near)
             got["delta"] = (near, xor_permute(near, "tensor", 1))
 
@@ -595,7 +599,7 @@
         for i in group:
             need("back", i)
         riders = []
-        if c == 0:
+        if c == last_chunk:
             need("delta", len(delta_bits) - 1)
             riders = [got["blocks"]]
         keeps, recvs = [pieces[i][0] for i in group], [pieces[i][1] for i in group]

time: 42.3 us -> 42.2 us (level)
  starting transfers between devices: 21.5 us -> 19.4 us
  local copies, waits for them, and re-layouts: 0.75 us -> 2.23 us
  waiting for transfers between devices: 6.87 us -> 7.44 us
    ppermute x18, starting transfers between devices: 21.5 us -> 19.4 us  [xor_permute(): return lax.ppermute(x, axis, [(i, i ^ bit) for i in range(count)])]
    unnamed x24, local copies, waits for them, and re-layouts: 0.75 us -> 2.23 us
    ppermute x18, waiting for transfers between devices: 6.87 us -> 7.44 us  [xor_permute(): return lax.ppermute(x, axis, [(i, i ^ bit) for i in range(count)])]
  transfers between devices with their start and end apart: 18 -> 18, of which waited for: 7 -> 6; matrix products, arithmetic and copies ran while one was open for 0% -> 0% of each run, Pallas kernels for 27% -> 27%
where the time goes in v4:
time: 42.2 us; the launch traced here: 42 us
  starting transfers between devices  19.4 us (46%)
  Pallas kernels  12.1 us (29%)
  waiting for transfers between devices  7.44 us (18%)
  local copies, waits for them, and re-layouts  2.23 us (5%)
  between operations  0.85 us (2%)
    ppermute x18, starting transfers between devices, xor_permute(): return lax.ppermute(x, axis, [(i, i ^ bit) for i in range(count)])  19.4 us
    ppermute x18, waiting for transfers between devices, xor_permute(): return lax.ppermute(x, axis, [(i, i ^ bit) for i in range(count)])  7.44 us
    pallas_call x4, Pallas kernels, back(): pl.pallas_call(with_deps(functools.partial(back_kernel, nt, nb, piece * w...  5.24 us
    pallas_call x1, Pallas kernels, forward(): pl.pallas_call(with_deps(functools.partial(forward_kernel, count), count...  2.42 us
    unnamed x24, local copies, waits for them, and re-layouts  2.23 us
    pallas_call x1, Pallas kernels, project(): pl.pallas_call(with_deps(functools.partial(project_kernel, nt, nb), 4 + n...  1.16 us
    pallas_call x1, Pallas kernels, final(): pl.pallas_call(with_deps(final_kernel, 2, deps), out_shape=jax.ShapeDtype...  0.89 us
  transfers between devices with their start and end apart: 18, of which 6 were waited for; matrix products, arithmetic and copies ran while one was open for 0% of the time, Pallas kernels for 27%

profile of v4, /device:TPU:0, one launch (start us, length us, event | category | flops | bytes accessed | tf_op | source)
XLA Modules:
  0.0 42.0 jit_solution(7216452178674041030)
XLA Ops:
  0.7 1.0 %copy-done = bf16[32,8192]{1,0:T(8,128)(2,1)S(1)} copy-done((bf16[32,8192]{1,0:T(8,128)(2,1)S(1)}, bf16[32,8192]{1,0:T(8,128)(2,1)}, u32[]{:S(2)}) %copy-start) | copy-done | bytes 524312
  1.8 3.0 %collective-permute-start = (bf16[32,8192]{1,0:T(8,128)(2,1)S(1)}, bf16[32,8192]{1,0:T(8,128)(2,1)S(1)}, u32[]{:S(2)}, u32[]{:S(2)}) collective-permute-start(bf16[32,8192]{1,0:T(8,128)(2,1)S(1)} %relay.2.refs_1_.refs_3_.refs_0_.refs_4_), channel_id=1, source_target_pairs={{0,2},{1,3},{2,0},{3,1},{4,6},{5,7},{6,4},{7,5},{8,10},{9,11},{10,... | collective-permute-start | bytes 1572872 | tf_op jit(solution)/shard_map/ppermute | solution.py:72
  4.8 1.6 %collective-permute-start.1 = (bf16[64,128]{1,0:T(8,128)(2,1)S(1)}, bf16[64,128]{1,0:T(8,128)(2,1)S(1)}, u32[]{:S(2)}, u32[]{:S(2)}) collective-permute-start(bf16[64,128]{1,0:T(8,128)(2,1)S(1)} %lines.1.refs_0_), channel_id=1, source_target_pairs={{0,4},{4,0},{8,12},{12,8},{16,20},{20,16},{24,28},{28,24},{1,5},{5... | collective-permute-start | bytes 49160 | tf_op jit(solution)/shard_map/ppermute | solution.py:72
  6.4 1.2 %slice-done.3 = s8[4194304]{0:T(1024)(128)(4,1)S(1)} async-done(((s8[16777216]{0:T(1024)(128)(4,1)}), s8[4194304]{0:T(1024)(128)(4,1)S(1)}, s32[]{:S(2)}) %slice-start.3) | async-done | bytes 4194328
  7.6 1.3 %back.4 = (bf16[64,2048]{1,0:T(8,128)(2,1)S(1)}, bf16[64,2048]{1,0:T(8,128)(2,1)S(1)}) custom-call(s32[2,8]{1,0:T(2,128)S(1)} %bitcast.4, bf16[128,1024]{1,0:T(8,128)(2,1)S(1)} %copy-done.1, bf16[8192,1024]{1,0:T(8,128)(2,1)S(1)} %bitcast.3, f32[8,128]{1,0:T(8,128)S(1)} %pause.3.refs_3_), custom_call_target="tpu_custom_call" | custom-call | flops 10000000000 | bytes 10000000 | tf_op jit(solution)/shard_map/back/pallas_call | solution.py:372
  8.9 0.5 %collective-permute-start.2 = (bf16[64,2048]{1,0:T(8,128)(2,1)S(1)}, bf16[64,2048]{1,0:T(8,128)(2,1)S(1)}, u32[]{:S(2)}, u32[]{:S(2)}) collective-permute-start(bf16[64,2048]{1,0:T(8,128)(2,1)S(1)} %get-tuple-element.31.refs_2_), channel_id=1, source_target_pairs={{0,1},{1,0},{2,3},{3,2},{4,5},{5,4},{6,7},{7,6},{8,9},{9,8},{10,11... | collective-permute-start | bytes 786440 | tf_op jit(solution)/shard_map/ppermute | solution.py:72
  9.4 1.3 %back.5 = (bf16[64,3072]{1,0:T(8,128)(2,1)S(1)}, bf16[64,3072]{1,0:T(8,128)(2,1)S(1)}) custom-call(s32[2,8]{1,0:T(2,128)S(1)} %bitcast.5, bf16[128,1024]{1,0:T(8,128)(2,1)S(1)} %copy-done.1, bf16[8192,1024]{1,0:T(8,128)(2,1)S(1)} %bitcast.3, bf16[128,128]{1,0:T(8,128)(2,1)S(1)} %double.2.refs_3_.refs_0_), custom_call_target="tpu_custom_call" | custom-call | flops 10000000000 | bytes 10000000 | tf_op jit(solution)/shard_map/back/pallas_call | solution.py:372
  10.9 1.3 %back.6 = (bf16[64,2048]{1,0:T(8,128)(2,1)S(1)}, bf16[64,2048]{1,0:T(8,128)(2,1)S(1)}) custom-call(s32[2,8]{1,0:T(2,128)S(1)} %bitcast.6, bf16[128,1024]{1,0:T(8,128)(2,1)S(1)} %copy-done.1, bf16[8192,1024]{1,0:T(8,128)(2,1)S(1)} %bitcast.3, bf16[64,3072]{1,0:T(8,128)(2,1)S(1)} %get-tuple-element.33.refs_3_), custom_call_target="tpu_custom_call" | custom-call | flops 10000000000 | bytes 10000000 | tf_op jit(solution)/shard_map/back/pallas_call | solution.py:372
  12.2 4.1 %collective-permute-start.7 = (bf16[128,128]{1,0:T(8,128)(2,1)S(1)}, bf16[128,128]{1,0:T(8,128)(2,1)S(1)}, u32[]{:S(2)}, u32[]{:S(2)}) collective-permute-start(bf16[128,128]{1,0:T(8,128)(2,1)S(1)} %double.2.refs_3_.refs_0_), channel_id=1, source_target_pairs={{0,16},{4,20},{8,24},{12,28},{16,0},{20,4},{24,8},{28,12},{1,17},{... | collective-permute-start | bytes 98312 | tf_op jit(solution)/shard_map/ppermute | solution.py:72
  16.5 1.5 %collective-permute-start.15 = (bf16[32,5120]{1,0:T(8,128)(2,1)S(1)}, bf16[32,5120]{1,0:T(8,128)(2,1)S(1)}, u32[]{:S(2)}, u32[]{:S(2)}) collective-permute-start(bf16[32,5120]{1,0:T(8,128)(2,1)S(1)} %get-tuple-element.48), channel_id=1, source_target_pairs={{0,2},{1,3},{2,0},{3,1},{4,6},{5,7},{6,4},{7,5},{8,10},{9,11},{10,... | collective-permute-start | bytes 983048 | tf_op jit(solution)/shard_map/ppermute | solution.py:72
  18.1 0.3 collective-permute-start.5
  18.3 1.3 %back.7 = (bf16[64,2048]{1,0:T(8,128)(2,1)S(1)}, bf16[64,2048]{1,0:T(8,128)(2,1)S(1)}) custom-call(s32[2,8]{1,0:T(2,128)S(1)} %bitcast.7, bf16[128,1024]{1,0:T(8,128)(2,1)S(1)} %copy-done.1, bf16[8192,1024]{1,0:T(8,128)(2,1)S(1)} %bitcast.3, bf16[32,8192]{1,0:T(8,128)(2,1)S(1)} %relay.3.refs_3_.refs_4_.refs_1_.refs_5_), custom_call_target="tpu_custom_call" | custom-call | flops 10000000000 | bytes 10000000 | tf_op jit(solution)/shard_map/back/pallas_call | solution.py:372
  19.7 0.4 collective-permute-start.10
  20.0 0.7 %block_grads.1 = (bf16[1024,128]{1,0:T(8,128)(2,1)S(1)}, bf16[1024,128]{1,0:T(8,128)(2,1)S(1)}) custom-call(s32[2,8]{1,0:T(2,128)S(1)} %bitcast.8, s32[1,8]{1,0:T(1,128)S(1)} %bitcast.11, bf16[128,1024]{1,0:T(8,128)(2,1)S(1)} %copy-done.1, bf16[32,8192]{1,0:T(8,128)(2,1)S(1)} %relay.2.refs_1_.refs_3_.refs_0_.refs_4_, ...), custom_call_target="tpu_custom_call" | custom-call | flops 10000000000 | bytes 10000000 | tf_op jit(solution)/shard_map/block_grads/pallas_call | solution.py:274
  20.7 0.5 %collective-permute-start.6 = (bf16[1024,128]{1,0:T(8,128)(2,1)S(1)}, bf16[1024,128]{1,0:T(8,128)(2,1)S(1)}, u32[]{:S(2)}, u32[]{:S(2)}) collective-permute-start(bf16[1024,128]{1,0:T(8,128)(2,1)S(1)} %get-tuple-element.38.refs_2_), channel_id=1, source_target_pairs={{0,1},{1,0},{2,3},{3,2},{4,5},{5,4},{6,7},{7,6},{8,9},{9,8},{10,11... | collective-permute-start | bytes 786440 | tf_op jit(solution)/shard_map/ppermute | solution.py:72
  21.2 1.7 %collective-permute-start.11 = (bf16[256,128]{1,0:T(8,128)(2,1)S(1)}, bf16[256,128]{1,0:T(8,128)(2,1)S(1)}, u32[]{:S(2)}, u32[]{:S(2)}) collective-permute-start(bf16[256,128]{1,0:T(8,128)(2,1)S(1)} %double.3.refs_2_.refs_1_), channel_id=1, source_target_pairs={{0,8},{4,12},{8,0},{12,4},{16,24},{20,28},{24,16},{28,20},{1,9},{5... | collective-permute-start | bytes 196616 | tf_op jit(solution)/shard_map/ppermute | solution.py:72
  22.9 1.6 %collective-permute-start.8 = (bf16[512,128]{1,0:T(8,128)(2,1)S(1)}, bf16[512,128]{1,0:T(8,128)(2,1)S(1)}, u32[]{:S(2)}, u32[]{:S(2)}) collective-permute-start(bf16[512,128]{1,0:T(8,128)(2,1)S(1)} %get-tuple-element.40.refs_3_), channel_id=1, source_target_pairs={{0,4},{4,0},{8,12},{12,8},{16,20},{20,16},{24,28},{28,24},{1,5},{5... | collective-permute-start | bytes 393224 | tf_op jit(solution)/shard_map/ppermute | solution.py:72
  24.5 1.0 %collective-permute-done.11.refs_2_ = bf16[256,128]{1,0:T(8,128)(2,1)S(1)} collective-permute-done((bf16[256,128]{1,0:T(8,128)(2,1)S(1)}, bf16[256,128]{1,0:T(8,128)(2,1)S(1)}, u32[]{:S(2)}, u32[]{:S(2)}) %collective-permute-start.11) | collective-permute-done | bytes 65568 | tf_op jit(solution)/shard_map/ppermute | solution.py:72
  25.9 0.4 %collective-permute-start.12 = (bf16[32,5120]{1,0:T(8,128)(2,1)S(1)}, bf16[32,5120]{1,0:T(8,128)(2,1)S(1)}, u32[]{:S(2)}, u32[]{:S(2)}) collective-permute-start(bf16[32,5120]{1,0:T(8,128)(2,1)S(1)} %get-tuple-element.45), channel_id=1, source_target_pairs={{0,2},{1,3},{2,0},{3,1},{4,6},{5,7},{6,4},{7,5},{8,10},{9,11},{10,... | collective-permute-start | bytes 983048 | tf_op jit(solution)/shard_map/ppermute | solution.py:72
  26.3 2.0 %collective-permute-done.8.refs_1_ = bf16[512,128]{1,0:T(8,128)(2,1)S(1)} collective-permute-done((bf16[512,128]{1,0:T(8,128)(2,1)S(1)}, bf16[512,128]{1,0:T(8,128)(2,1)S(1)}, u32[]{:S(2)}, u32[]{:S(2)}) %collective-permute-start.8) | collective-permute-done | bytes 131104 | tf_op jit(solution)/shard_map/ppermute | solution.py:72
  28.3 1.7 %collective-permute-start.13 = (bf16[256,128]{1,0:T(8,128)(2,1)S(1)}, bf16[256,128]{1,0:T(8,128)(2,1)S(1)}, u32[]{:S(2)}, u32[]{:S(2)}) collective-permute-start(bf16[256,128]{1,0:T(8,128)(2,1)S(1)} %get-tuple-element.44.refs_5_), channel_id=1, source_target_pairs={{0,8},{4,12},{8,0},{12,4},{16,24},{20,28},{24,16},{28,20},{1,9},{5... | collective-permute-start | bytes 196616 | tf_op jit(solution)/shard_map/ppermute | solution.py:72
  29.9 2.4 %forward.1.refs_2_.refs_1_ = f32[128,1024]{1,0:T(8,128)S(1)} custom-call(bf16[32,8192]{1,0:T(8,128)(2,1)S(1)} %relay.2.refs_1_.refs_3_.refs_0_.refs_4_, bf16[32,8192]{1,0:T(8,128)(2,1)S(1)} %relay.3.refs_3_.refs_4_.refs_1_.refs_5_, bf16[32,8192]{1,0:T(8,128)(2,1)S(1)} %collective-permute-done.4.refs_5_.refs_2_.refs_6_, ...), custom_call_target="tpu_custom_call" | custom-call | flops 10000000000 | bytes 10000000 | tf_op jit(solution)/shard_map/forward/pallas_call | solution.py:435
  32.4 0.3 collective-permute-done.13.refs_1_
  32.6 1.5 %collective-permute-start.16 = (bf16[128,128]{1,0:T(8,128)(2,1)S(1)}, bf16[128,128]{1,0:T(8,128)(2,1)S(1)}, u32[]{:S(2)}, u32[]{:S(2)}) collective-permute-start(bf16[128,128]{1,0:T(8,128)(2,1)S(1)} %get-tuple-element.47.refs_2_), channel_id=1, source_target_pairs={{0,16},{4,20},{8,24},{12,28},{16,0},{20,4},{24,8},{28,12},{1,17},{... | collective-permute-start | bytes 98312 | tf_op jit(solution)/shard_map/ppermute | solution.py:72
  34.2 0.6 %collective-permute-done.12.refs_1_ = bf16[32,5120]{1,0:T(8,128)(2,1)S(1)} collective-permute-done((bf16[32,5120]{1,0:T(8,128)(2,1)S(1)}, bf16[32,5120]{1,0:T(8,128)(2,1)S(1)}, u32[]{:S(2)}, u32[]{:S(2)}) %collective-permute-start.12) | collective-permute-done | bytes 327712 | tf_op jit(solution)/shard_map/ppermute | solution.py:72
  34.9 2.7 %collective-permute-done.16.refs_1_ = bf16[128,128]{1,0:T(8,128)(2,1)S(1)} collective-permute-done((bf16[128,128]{1,0:T(8,128)(2,1)S(1)}, bf16[128,128]{1,0:T(8,128)(2,1)S(1)}, u32[]{:S(2)}, u32[]{:S(2)}) %collective-permute-start.16) | collective-permute-done | bytes 32800 | tf_op jit(solution)/shard_map/ppermute | solution.py:72
  37.5 0.5 %collective-permute-start.17 = (bf16[64,128]{1,0:T(8,128)(2,1)S(1)}, bf16[64,128]{1,0:T(8,128)(2,1)S(1)}, u32[]{:S(2)}, u32[]{:S(2)}) collective-permute-start(bf16[64,128]{1,0:T(8,128)(2,1)S(1)} %get-tuple-element.50.refs_6_), channel_id=1, source_target_pairs={{0,2},{1,3},{2,0},{3,1},{4,6},{5,7},{6,4},{7,5},{8,10},{9,11},{10,... | collective-permute-start | bytes 49160 | tf_op jit(solution)/shard_map/ppermute | solution.py:72
  38.1 0.3 correct.1.refs_8_.refs_0_.refs_2_.refs_5_
  38.4 0.9 %final.1 = bf16[32,8192]{1,0:T(8,128)(2,1)} custom-call(f32[32,8192]{1,0:T(8,128)S(1)} %correct.1.refs_8_.refs_0_.refs_2_.refs_5_, bf16[32,5120]{1,0:T(8,128)(2,1)S(1)} %collective-permute-done.12.refs_1_, f32[32,8192]{1,0:T(8,128)S(1)} %correct.1.refs_8_.refs_0_.refs_2_.refs_5_), custom_call_target="tpu_custom_call" | custom-call | flops 10000000000 | bytes 10000000 | tf_op jit(solution)/shard_map/final/pallas_call | solution.py:531
  39.3 1.2 %project.1 = bf16[128,1024]{1,0:T(8,128)(2,1)} custom-call(s32[2,8]{1,0:T(2,128)S(1)} %bitcast.10, f32[128,1024]{1,0:T(8,128)S(1)} %forward.1.refs_2_.refs_1_, bf16[512,128]{1,0:T(8,128)(2,1)S(1)} %unride.1.refs_2_.refs_1_, bf16[512,128]{1,0:T(8,128)(2,1)S(1)} %collective-permute-done.14.refs_2_.refs_3_, ...), custom_call_target="tpu_custom_call" | custom-call | flops 10000000000 | bytes 10000000 | tf_op jit(solution)/shard_map/project/pallas_call | solution.py:474
  40.5 0.9 %collective-permute-done.17.refs_1_ = bf16[64,128]{1,0:T(8,128)(2,1)S(1)} collective-permute-done((bf16[64,128]{1,0:T(8,128)(2,1)S(1)}, bf16[64,128]{1,0:T(8,128)(2,1)S(1)}, u32[]{:S(2)}, u32[]{:S(2)}) %collective-permute-start.17) | collective-permute-done | bytes 16416 | tf_op jit(solution)/shard_map/ppermute | solution.py:72
  41.4 0.7 %adam.1 = (bf16[2,4096]{1,0:T(2,128)(2,1)}, f32[2,4096]{1,0:T(2,128)}, f32[2,4096]{1,0:T(2,128)}) custom-call(bf16[64,128]{1,0:T(8,128)(2,1)S(1)} %get-tuple-element.51.refs_0_, bf16[64,128]{1,0:T(8,128)(2,1)S(1)} %collective-permute-done.17.refs_1_, bf16[2,4096]{1,0:T(2,128)(2,1)S(1)} %copy-done.5, f32[2,4096]{1,0:T(2,128)S(1)} %copy-done.2, ...), custom_call_target="tpu_custom_call" | custom-call | flops 10000000000 | bytes 10000000 | tf_op jit(solution)/shard_map/adam/pallas_call | solution.py:325
  (54 shorter events, 1.0 us)
Async XLA Ops:
  0.6 1.0 %copy-start = (bf16[32,8192]{1,0:T(8,128)(2,1)S(1)}, bf16[32,8192]{1,0:T(8,128)(2,1)}, u32[]{:S(2)}) copy-start(bf16[32,8192]{1,0:T(8,128)(2,1)} %refs_0_.2) | copy-start | bytes 1572868
  1.7 3.1 %copy-start.4 = (bf16[2,4096]{1,0:T(2,128)(2,1)S(1)}, bf16[2,4096]{1,0:T(2,128)(2,1)}, u32[]{:S(2)}) copy-start(bf16[2,4096]{1,0:T(2,128)(2,1)} %refs_2_.11) | copy-start | bytes 49156
  1.7 4.7 %slice-start = ((s8[16777216]{0:T(1024)(128)(4,1)}), s8[4194304]{0:T(1024)(128)(4,1)S(1)}, s32[]{:S(2)}) async-start(s8[16777216]{0:T(1024)(128)(4,1)} %bitcast.2), calls=%async_computation | async-start | bytes 8388608
  1.7 4.7 %slice-start.1 = ((s8[16777216]{0:T(1024)(128)(4,1)}), s8[4194304]{0:T(1024)(128)(4,1)S(1)}, s32[]{:S(2)}) async-start(s8[16777216]{0:T(1024)(128)(4,1)} %bitcast.2), calls=%async_computation.1 | async-start | bytes 8388608
  1.7 4.7 %slice-start.2 = ((s8[16777216]{0:T(1024)(128)(4,1)}), s8[4194304]{0:T(1024)(128)(4,1)S(1)}, s32[]{:S(2)}) async-start(s8[16777216]{0:T(1024)(128)(4,1)} %bitcast.2), calls=%async_computation.2 | async-start | bytes 8388608
  1.7 5.8 %slice-start.3 = ((s8[16777216]{0:T(1024)(128)(4,1)}), s8[4194304]{0:T(1024)(128)(4,1)S(1)}, s32[]{:S(2)}) async-start(s8[16777216]{0:T(1024)(128)(4,1)} %bitcast.2), calls=%async_computation.3 | async-start | bytes 8388608
  1.7 5.8 %copy-start.1 = (bf16[128,1024]{1,0:T(8,128)(2,1)S(1)}, bf16[128,1024]{1,0:T(8,128)(2,1)}, u32[]{:S(2)}) copy-start(bf16[128,1024]{1,0:T(8,128)(2,1)} %refs_2_.10) | copy-start | bytes 786436
  1.8 5.8 %copy-start.6 = (s32[8,2]{0,1:T(2,128)S(1)}, s32[8,2]{0,1:T(2,128)}, u32[]{:S(2)}) copy-start(s32[8,2]{0,1:T(2,128)} %param.11) | copy-start | bytes 196
  1.8 16.2 %collective-permute-start = (bf16[32,8192]{1,0:T(8,128)(2,1)S(1)}, bf16[32,8192]{1,0:T(8,128)(2,1)S(1)}, u32[]{:S(2)}, u32[]{:S(2)}) collective-permute-start(bf16[32,8192]{1,0:T(8,128)(2,1)S(1)} %relay.2.refs_1_.refs_3_.refs_0_.refs_4_), channel_id=1, source_target_pairs={{0,2},{1,3},{2,0},{3,1},{4,6},{5,7},{6,4},{7,5},{8,10},{9,11},{10,... | collective-permute-start | bytes 1572872 | tf_op jit(solution)/shard_map/ppermute | solution.py:72
  4.8 14.9 %collective-permute-start.4 = (bf16[32,8192]{1,0:T(8,128)(2,1)S(1)}, bf16[32,8192]{1,0:T(8,128)(2,1)S(1)}, u32[]{:S(2)}, u32[]{:S(2)}) collective-permute-start(bf16[32,8192]{1,0:T(8,128)(2,1)S(1)} %relay.2.refs_1_.refs_3_.refs_0_.refs_4_), channel_id=1, source_target_pairs={{0,1},{1,0},{2,3},{3,2},{4,5},{5,4},{6,7},{7,6},{8,9},{9,8},{10,11... | collective-permute-start | bytes 1572872 | tf_op jit(solution)/shard_map/ppermute | solution.py:72
  4.8 4.6 %collective-permute-start.1 = (bf16[64,128]{1,0:T(8,128)(2,1)S(1)}, bf16[64,128]{1,0:T(8,128)(2,1)S(1)}, u32[]{:S(2)}, u32[]{:S(2)}) collective-permute-start(bf16[64,128]{1,0:T(8,128)(2,1)S(1)} %lines.1.refs_0_), channel_id=1, source_target_pairs={{0,4},{4,0},{8,12},{12,8},{16,20},{20,16},{24,28},{28,24},{1,5},{5... | collective-permute-start | bytes 49160 | tf_op jit(solution)/shard_map/ppermute | solution.py:72
  8.9 7.4 %collective-permute-start.2 = (bf16[64,2048]{1,0:T(8,128)(2,1)S(1)}, bf16[64,2048]{1,0:T(8,128)(2,1)S(1)}, u32[]{:S(2)}, u32[]{:S(2)}) collective-permute-start(bf16[64,2048]{1,0:T(8,128)(2,1)S(1)} %get-tuple-element.31.refs_2_), channel_id=1, source_target_pairs={{0,1},{1,0},{2,3},{3,2},{4,5},{5,4},{6,7},{7,6},{8,9},{9,8},{10,11... | collective-permute-start | bytes 786440 | tf_op jit(solution)/shard_map/ppermute | solution.py:72
  10.7 5.6 %collective-permute-start.3 = (bf16[64,3072]{1,0:T(8,128)(2,1)S(1)}, bf16[64,3072]{1,0:T(8,128)(2,1)S(1)}, u32[]{:S(2)}, u32[]{:S(2)}) collective-permute-start(bf16[64,3072]{1,0:T(8,128)(2,1)S(1)} %get-tuple-element.33.refs_3_), channel_id=1, source_target_pairs={{0,1},{1,0},{2,3},{3,2},{4,5},{5,4},{6,7},{7,6},{8,9},{9,8},{10,11... | collective-permute-start | bytes 1179656 | tf_op jit(solution)/shard_map/ppermute | solution.py:72
  12.2 9.0 %collective-permute-start.7 = (bf16[128,128]{1,0:T(8,128)(2,1)S(1)}, bf16[128,128]{1,0:T(8,128)(2,1)S(1)}, u32[]{:S(2)}, u32[]{:S(2)}) collective-permute-start(bf16[128,128]{1,0:T(8,128)(2,1)S(1)} %double.2.refs_3_.refs_0_), channel_id=1, source_target_pairs={{0,16},{4,20},{8,24},{12,28},{16,0},{20,4},{24,8},{28,12},{1,17},{... | collective-permute-start | bytes 98312 | tf_op jit(solution)/shard_map/ppermute | solution.py:72
  16.3 9.4 %collective-permute-start.9 = (bf16[64,2048]{1,0:T(8,128)(2,1)S(1)}, bf16[64,2048]{1,0:T(8,128)(2,1)S(1)}, u32[]{:S(2)}, u32[]{:S(2)}) collective-permute-start(bf16[64,2048]{1,0:T(8,128)(2,1)S(1)} %get-tuple-element.34.refs_4_), channel_id=1, source_target_pairs={{0,1},{1,0},{2,3},{3,2},{4,5},{5,4},{6,7},{7,6},{8,9},{9,8},{10,11... | collective-permute-start | bytes 786440 | tf_op jit(solution)/shard_map/ppermute | solution.py:72
  16.5 21.6 %collective-permute-start.15 = (bf16[32,5120]{1,0:T(8,128)(2,1)S(1)}, bf16[32,5120]{1,0:T(8,128)(2,1)S(1)}, u32[]{:S(2)}, u32[]{:S(2)}) collective-permute-start(bf16[32,5120]{1,0:T(8,128)(2,1)S(1)} %get-tuple-element.48), channel_id=1, source_target_pairs={{0,2},{1,3},{2,0},{3,1},{4,6},{5,7},{6,4},{7,5},{8,10},{9,11},{10,... | collective-permute-start | bytes 983048 | tf_op jit(solution)/shard_map/ppermute | solution.py:72
  18.0 2.0 %copy-start.7 = (s32[8]{0:T(128)S(1)}, s32[8]{0:T(128)}, u32[]{:S(2)}) copy-start(s32[8]{0:T(128)} %param.12) | copy-start | bytes 100
  18.1 2.0 %collective-permute-start.5 = (bf16[32,8192]{1,0:T(8,128)(2,1)S(1)}, bf16[32,8192]{1,0:T(8,128)(2,1)S(1)}, u32[]{:S(2)}, u32[]{:S(2)}) collective-permute-start(bf16[32,8192]{1,0:T(8,128)(2,1)S(1)} %relay.3.refs_3_.refs_4_.refs_1_.refs_5_), channel_id=1, source_target_pairs={{0,1},{1,0},{2,3},{3,2},{4,5},{5,4},{6,7},{7,6},{8,9},{9,8},{10,11... | collective-permute-start | bytes 1572872 | tf_op jit(solution)/shard_map/ppermute | solution.py:72
  19.7 6.1 %collective-permute-start.10 = (bf16[64,2048]{1,0:T(8,128)(2,1)S(1)}, bf16[64,2048]{1,0:T(8,128)(2,1)S(1)}, u32[]{:S(2)}, u32[]{:S(2)}) collective-permute-start(bf16[64,2048]{1,0:T(8,128)(2,1)S(1)} %get-tuple-element.36.refs_7_), channel_id=1, source_target_pairs={{0,1},{1,0},{2,3},{3,2},{4,5},{5,4},{6,7},{7,6},{8,9},{9,8},{10,11... | collective-permute-start | bytes 786440 | tf_op jit(solution)/shard_map/ppermute | solution.py:72
  20.7 2.2 %collective-permute-start.6 = (bf16[1024,128]{1,0:T(8,128)(2,1)S(1)}, bf16[1024,128]{1,0:T(8,128)(2,1)S(1)}, u32[]{:S(2)}, u32[]{:S(2)}) collective-permute-start(bf16[1024,128]{1,0:T(8,128)(2,1)S(1)} %get-tuple-element.38.refs_2_), channel_id=1, source_target_pairs={{0,1},{1,0},{2,3},{3,2},{4,5},{5,4},{6,7},{7,6},{8,9},{9,8},{10,11... | collective-permute-start | bytes 786440 | tf_op jit(solution)/shard_map/ppermute | solution.py:72
  21.2 4.3 %collective-permute-start.11 = (bf16[256,128]{1,0:T(8,128)(2,1)S(1)}, bf16[256,128]{1,0:T(8,128)(2,1)S(1)}, u32[]{:S(2)}, u32[]{:S(2)}) collective-permute-start(bf16[256,128]{1,0:T(8,128)(2,1)S(1)} %double.3.refs_2_.refs_1_), channel_id=1, source_target_pairs={{0,8},{4,12},{8,0},{12,4},{16,24},{20,28},{24,16},{28,20},{1,9},{5... | collective-permute-start | bytes 196616 | tf_op jit(solution)/shard_map/ppermute | solution.py:72
  22.9 5.3 %collective-permute-start.8 = (bf16[512,128]{1,0:T(8,128)(2,1)S(1)}, bf16[512,128]{1,0:T(8,128)(2,1)S(1)}, u32[]{:S(2)}, u32[]{:S(2)}) collective-permute-start(bf16[512,128]{1,0:T(8,128)(2,1)S(1)} %get-tuple-element.40.refs_3_), channel_id=1, source_target_pairs={{0,4},{4,0},{8,12},{12,8},{16,20},{20,16},{24,28},{28,24},{1,5},{5... | collective-permute-start | bytes 393224 | tf_op jit(solution)/shard_map/ppermute | solution.py:72
  25.9 8.9 %collective-permute-start.12 = (bf16[32,5120]{1,0:T(8,128)(2,1)S(1)}, bf16[32,5120]{1,0:T(8,128)(2,1)S(1)}, u32[]{:S(2)}, u32[]{:S(2)}) collective-permute-start(bf16[32,5120]{1,0:T(8,128)(2,1)S(1)} %get-tuple-element.45), channel_id=1, source_target_pairs={{0,2},{1,3},{2,0},{3,1},{4,6},{5,7},{6,4},{7,5},{8,10},{9,11},{10,... | collective-permute-start | bytes 983048 | tf_op jit(solution)/shard_map/ppermute | solution.py:72
  28.3 4.3 %collective-permute-start.13 = (bf16[256,128]{1,0:T(8,128)(2,1)S(1)}, bf16[256,128]{1,0:T(8,128)(2,1)S(1)}, u32[]{:S(2)}, u32[]{:S(2)}) collective-permute-start(bf16[256,128]{1,0:T(8,128)(2,1)S(1)} %get-tuple-element.44.refs_5_), channel_id=1, source_target_pairs={{0,8},{4,12},{8,0},{12,4},{16,24},{20,28},{24,16},{28,20},{1,9},{5... | collective-permute-start | bytes 196616 | tf_op jit(solution)/shard_map/ppermute | solution.py:72
  32.6 4.9 %collective-permute-start.16 = (bf16[128,128]{1,0:T(8,128)(2,1)S(1)}, bf16[128,128]{1,0:T(8,128)(2,1)S(1)}, u32[]{:S(2)}, u32[]{:S(2)}) collective-permute-start(bf16[128,128]{1,0:T(8,128)(2,1)S(1)} %get-tuple-element.47.refs_2_), channel_id=1, source_target_pairs={{0,16},{4,20},{8,24},{12,28},{16,0},{20,4},{24,8},{28,12},{1,17},{... | collective-permute-start | bytes 98312 | tf_op jit(solution)/shard_map/ppermute | solution.py:72
  34.8 3.3 %collective-permute-start.14 = (bf16[512,128]{1,0:T(8,128)(2,1)S(1)}, bf16[512,128]{1,0:T(8,128)(2,1)S(1)}, u32[]{:S(2)}, u32[]{:S(2)}) collective-permute-start(bf16[512,128]{1,0:T(8,128)(2,1)S(1)} %unride.1.refs_2_.refs_1_), channel_id=1, source_target_pairs={{0,1},{1,0},{2,3},{3,2},{4,5},{5,4},{6,7},{7,6},{8,9},{9,8},{10,11... | collective-permute-start | bytes 393224 | tf_op jit(solution)/shard_map/ppermute | solution.py:72
  37.5 3.8 %collective-permute-start.17 = (bf16[64,128]{1,0:T(8,128)(2,1)S(1)}, bf16[64,128]{1,0:T(8,128)(2,1)S(1)}, u32[]{:S(2)}, u32[]{:S(2)}) collective-permute-start(bf16[64,128]{1,0:T(8,128)(2,1)S(1)} %get-tuple-element.50.refs_6_), channel_id=1, source_target_pairs={{0,2},{1,3},{2,0},{3,1},{4,6},{5,7},{6,4},{7,5},{8,10},{9,11},{10,... | collective-permute-start | bytes 49160 | tf_op jit(solution)/shard_map/ppermute | solution.py:72
  39.3 2.0 %copy-start.2 = (f32[2,4096]{1,0:T(2,128)S(1)}, f32[2,4096]{1,0:T(2,128)}, u32[]{:S(2)}) copy-start(f32[2,4096]{1,0:T(2,128)} %refs_3_.1) | copy-start | bytes 98308
  39.3 2.0 %copy-start.3 = (f32[2,4096]{1,0:T(2,128)S(1)}, f32[2,4096]{1,0:T(2,128)}, u32[]{:S(2)}) copy-start(f32[2,4096]{1,0:T(2,128)} %refs_4_.3) | copy-start | bytes 98308
  39.3 2.0 %copy-start.5 = (bf16[2,4096]{1,0:T(2,128)(2,1)S(1)}, bf16[2,4096]{1,0:T(2,128)(2,1)}, u32[]{:S(2)}) copy-start(bf16[2,4096]{1,0:T(2,128)(2,1)} %refs_2_.11) | copy-start | bytes 49156

commit v5 on v4

--- a/solution.py
+++ b/solution.py
@@ -546,7 +546,7 @@
     part = HEAD_DIM // nt
     outer = bits_of(nt)[1:]
     grad_bits = bits_of(nd)
-    delta_bits = grad_bits[:1] + grad_bits[:0:-1]
+    delta_bits = grad_bits
     grad_ways = [("tensor", 1)] + [("dp", bit) for bit in grad_bits] + [("tensor", bit) for bit in outer]
     index = block_index.T
     owner = block_owner.reshape(1, -1)

time: 42.2 us -> 42.6 us (level)
  starting transfers between devices: 19.4 us -> 21.4 us
  waiting for transfers between devices: 7.44 us -> 5.65 us
    ppermute x18, starting transfers between devices: 19.4 us -> 21.4 us  [xor_permute(): return lax.ppermute(x, axis, [(i, i ^ bit) for i in range(count)])]
    ppermute x18, waiting for transfers between devices: 7.44 us -> 5.65 us  [xor_permute(): return lax.ppermute(x, axis, [(i, i ^ bit) for i in range(count)])]
  transfers between devices with their start and end apart: 18 -> 18, of which waited for: 6 -> 4; matrix products, arithmetic and copies ran while one was open for 0% -> 0% of each run, Pallas kernels for 27% -> 27%
where the time goes in v5:
time: 42.6 us; the launch traced here: 42.2 us
  starting transfers between devices  21.4 us (50%)
  Pallas kernels  12.1 us (28%)
  waiting for transfers between devices  5.65 us (13%)
  local copies, waits for them, and re-layouts  2.23 us (5%)
  between operations  0.85 us (2%)
    ppermute x18, starting transfers between devices, xor_permute(): return lax.ppermute(x, axis, [(i, i ^ bit) for i in range(count)])  21.4 us
    ppermute x18, waiting for transfers between devices, xor_permute(): return lax.ppermute(x, axis, [(i, i ^ bit) for i in range(count)])  5.65 us
    pallas_call x4, Pallas kernels, back(): pl.pallas_call(with_deps(functools.partial(back_kernel, nt, nb, piece * w...  5.25 us
    pallas_call x1, Pallas kernels, forward(): pl.pallas_call(with_deps(functools.partial(forward_kernel, count), count...  2.42 us
    unnamed x24, local copies, waits for them, and re-layouts  2.23 us
    pallas_call x1, Pallas kernels, project(): pl.pallas_call(with_deps(functools.partial(project_kernel, nt, nb), 4 + n...  1.16 us
    pallas_call x1, Pallas kernels, final(): pl.pallas_call(with_deps(final_kernel, 2, deps), out_shape=jax.ShapeDtype...  0.89 us
  transfers between devices with their start and end apart: 18, of which 4 were waited for; matrix products, arithmetic and copies ran while one was open for 0% of the time, Pallas kernels for 27%

profile of v5, /device:TPU:0, one launch (start us, length us, event | category | flops | bytes accessed | tf_op | source)
XLA Modules:
  0.0 42.2 jit_solution(14189204632592593779)
XLA Ops:
  0.7 1.0 %copy-done = bf16[32,8192]{1,0:T(8,128)(2,1)S(1)} copy-done((bf16[32,8192]{1,0:T(8,128)(2,1)S(1)}, bf16[32,8192]{1,0:T(8,128)(2,1)}, u32[]{:S(2)}) %copy-start) | copy-done | bytes 524312
  1.8 3.0 %collective-permute-start = (bf16[32,8192]{1,0:T(8,128)(2,1)S(1)}, bf16[32,8192]{1,0:T(8,128)(2,1)S(1)}, u32[]{:S(2)}, u32[]{:S(2)}) collective-permute-start(bf16[32,8192]{1,0:T(8,128)(2,1)S(1)} %relay.2.refs_1_.refs_3_.refs_0_.refs_4_), channel_id=1, source_target_pairs={{0,2},{1,3},{2,0},{3,1},{4,6},{5,7},{6,4},{7,5},{8,10},{9,11},{10,... | collective-permute-start | bytes 1572872 | tf_op jit(solution)/shard_map/ppermute | solution.py:72
  4.8 1.6 %collective-permute-start.1 = (bf16[64,128]{1,0:T(8,128)(2,1)S(1)}, bf16[64,128]{1,0:T(8,128)(2,1)S(1)}, u32[]{:S(2)}, u32[]{:S(2)}) collective-permute-start(bf16[64,128]{1,0:T(8,128)(2,1)S(1)} %lines.1.refs_0_), channel_id=1, source_target_pairs={{0,4},{4,0},{8,12},{12,8},{16,20},{20,16},{24,28},{28,24},{1,5},{5... | collective-permute-start | bytes 49160 | tf_op jit(solution)/shard_map/ppermute | solution.py:72
  6.4 1.2 %slice-done.3 = s8[4194304]{0:T(1024)(128)(4,1)S(1)} async-done(((s8[16777216]{0:T(1024)(128)(4,1)}), s8[4194304]{0:T(1024)(128)(4,1)S(1)}, s32[]{:S(2)}) %slice-start.3) | async-done | bytes 4194328
  7.6 1.3 %back.4 = (bf16[64,2048]{1,0:T(8,128)(2,1)S(1)}, bf16[64,2048]{1,0:T(8,128)(2,1)S(1)}) custom-call(s32[2,8]{1,0:T(2,128)S(1)} %bitcast.4, bf16[128,1024]{1,0:T(8,128)(2,1)S(1)} %copy-done.1, bf16[8192,1024]{1,0:T(8,128)(2,1)S(1)} %bitcast.3, f32[8,128]{1,0:T(8,128)S(1)} %pause.3.refs_3_), custom_call_target="tpu_custom_call" | custom-call | flops 10000000000 | bytes 10000000 | tf_op jit(solution)/shard_map/back/pallas_call | solution.py:372
  8.9 0.5 %collective-permute-start.2 = (bf16[64,2048]{1,0:T(8,128)(2,1)S(1)}, bf16[64,2048]{1,0:T(8,128)(2,1)S(1)}, u32[]{:S(2)}, u32[]{:S(2)}) collective-permute-start(bf16[64,2048]{1,0:T(8,128)(2,1)S(1)} %get-tuple-element.31.refs_2_), channel_id=1, source_target_pairs={{0,1},{1,0},{2,3},{3,2},{4,5},{5,4},{6,7},{7,6},{8,9},{9,8},{10,11... | collective-permute-start | bytes 786440 | tf_op jit(solution)/shard_map/ppermute | solution.py:72
  9.4 1.3 %back.5 = (bf16[64,3072]{1,0:T(8,128)(2,1)S(1)}, bf16[64,3072]{1,0:T(8,128)(2,1)S(1)}) custom-call(s32[2,8]{1,0:T(2,128)S(1)} %bitcast.5, bf16[128,1024]{1,0:T(8,128)(2,1)S(1)} %copy-done.1, bf16[8192,1024]{1,0:T(8,128)(2,1)S(1)} %bitcast.3, bf16[128,128]{1,0:T(8,128)(2,1)S(1)} %double.2.refs_3_.refs_0_), custom_call_target="tpu_custom_call" | custom-call | flops 10000000000 | bytes 10000000 | tf_op jit(solution)/shard_map/back/pallas_call | solution.py:372
  10.9 1.3 %back.6 = (bf16[64,2048]{1,0:T(8,128)(2,1)S(1)}, bf16[64,2048]{1,0:T(8,128)(2,1)S(1)}) custom-call(s32[2,8]{1,0:T(2,128)S(1)} %bitcast.6, bf16[128,1024]{1,0:T(8,128)(2,1)S(1)} %copy-done.1, bf16[8192,1024]{1,0:T(8,128)(2,1)S(1)} %bitcast.3, bf16[64,3072]{1,0:T(8,128)(2,1)S(1)} %get-tuple-element.33.refs_3_), custom_call_target="tpu_custom_call" | custom-call | flops 10000000000 | bytes 10000000 | tf_op jit(solution)/shard_map/back/pallas_call | solution.py:372
  12.2 3.1 %collective-permute-start.7 = (bf16[128,128]{1,0:T(8,128)(2,1)S(1)}, bf16[128,128]{1,0:T(8,128)(2,1)S(1)}, u32[]{:S(2)}, u32[]{:S(2)}) collective-permute-start(bf16[128,128]{1,0:T(8,128)(2,1)S(1)} %double.2.refs_3_.refs_0_), channel_id=1, source_target_pairs={{0,8},{4,12},{8,0},{12,4},{16,24},{20,28},{24,16},{28,20},{1,9},{5... | collective-permute-start | bytes 98312 | tf_op jit(solution)/shard_map/ppermute | solution.py:72
  15.3 0.2 merge.2
  15.4 1.5 %collective-permute-start.15 = (bf16[32,5120]{1,0:T(8,128)(2,1)S(1)}, bf16[32,5120]{1,0:T(8,128)(2,1)S(1)}, u32[]{:S(2)}, u32[]{:S(2)}) collective-permute-start(bf16[32,5120]{1,0:T(8,128)(2,1)S(1)} %get-tuple-element.48), channel_id=1, source_target_pairs={{0,2},{1,3},{2,0},{3,1},{4,6},{5,7},{6,4},{7,5},{8,10},{9,11},{10,... | collective-permute-start | bytes 983048 | tf_op jit(solution)/shard_map/ppermute | solution.py:72
  17.0 0.3 collective-permute-start.5
  17.3 1.3 %back.7 = (bf16[64,2048]{1,0:T(8,128)(2,1)S(1)}, bf16[64,2048]{1,0:T(8,128)(2,1)S(1)}) custom-call(s32[2,8]{1,0:T(2,128)S(1)} %bitcast.7, bf16[128,1024]{1,0:T(8,128)(2,1)S(1)} %copy-done.1, bf16[8192,1024]{1,0:T(8,128)(2,1)S(1)} %bitcast.3, bf16[32,8192]{1,0:T(8,128)(2,1)S(1)} %relay.3.refs_3_.refs_4_.refs_1_.refs_5_), custom_call_target="tpu_custom_call" | custom-call | flops 10000000000 | bytes 10000000 | tf_op jit(solution)/shard_map/back/pallas_call | solution.py:372
  18.7 0.3 collective-permute-start.10
  19.0 0.7 %block_grads.1 = (bf16[1024,128]{1,0:T(8,128)(2,1)S(1)}, bf16[1024,128]{1,0:T(8,128)(2,1)S(1)}) custom-call(s32[2,8]{1,0:T(2,128)S(1)} %bitcast.8, s32[1,8]{1,0:T(1,128)S(1)} %bitcast.11, bf16[128,1024]{1,0:T(8,128)(2,1)S(1)} %copy-done.1, bf16[32,8192]{1,0:T(8,128)(2,1)S(1)} %relay.2.refs_1_.refs_3_.refs_0_.refs_4_, ...), custom_call_target="tpu_custom_call" | custom-call | flops 10000000000 | bytes 10000000 | tf_op jit(solution)/shard_map/block_grads/pallas_call | solution.py:274
  19.7 0.3 collective-permute-start.6
  20.0 2.7 %collective-permute-start.11 = (bf16[256,128]{1,0:T(8,128)(2,1)S(1)}, bf16[256,128]{1,0:T(8,128)(2,1)S(1)}, u32[]{:S(2)}, u32[]{:S(2)}) collective-permute-start(bf16[256,128]{1,0:T(8,128)(2,1)S(1)} %double.3.refs_2_.refs_1_), channel_id=1, source_target_pairs={{0,16},{4,20},{8,24},{12,28},{16,0},{20,4},{24,8},{28,12},{1,17},{... | collective-permute-start | bytes 196616 | tf_op jit(solution)/shard_map/ppermute | solution.py:72
  22.7 1.6 %collective-permute-start.8 = (bf16[512,128]{1,0:T(8,128)(2,1)S(1)}, bf16[512,128]{1,0:T(8,128)(2,1)S(1)}, u32[]{:S(2)}, u32[]{:S(2)}) collective-permute-start(bf16[512,128]{1,0:T(8,128)(2,1)S(1)} %get-tuple-element.40.refs_3_), channel_id=1, source_target_pairs={{0,4},{4,0},{8,12},{12,8},{16,20},{20,16},{24,28},{28,24},{1,5},{5... | collective-permute-start | bytes 393224 | tf_op jit(solution)/shard_map/ppermute | solution.py:72
  24.3 2.3 %collective-permute-done.11.refs_2_ = bf16[256,128]{1,0:T(8,128)(2,1)S(1)} collective-permute-done((bf16[256,128]{1,0:T(8,128)(2,1)S(1)}, bf16[256,128]{1,0:T(8,128)(2,1)S(1)}, u32[]{:S(2)}, u32[]{:S(2)}) %collective-permute-start.11) | collective-permute-done | bytes 65568 | tf_op jit(solution)/shard_map/ppermute | solution.py:72
  26.6 0.2 compact_step.1.refs_4_.refs_5_.refs_0_
  27.0 1.5 %collective-permute-start.12 = (bf16[32,5120]{1,0:T(8,128)(2,1)S(1)}, bf16[32,5120]{1,0:T(8,128)(2,1)S(1)}, u32[]{:S(2)}, u32[]{:S(2)}) collective-permute-start(bf16[32,5120]{1,0:T(8,128)(2,1)S(1)} %get-tuple-element.45), channel_id=1, source_target_pairs={{0,2},{1,3},{2,0},{3,1},{4,6},{5,7},{6,4},{7,5},{8,10},{9,11},{10,... | collective-permute-start | bytes 983048 | tf_op jit(solution)/shard_map/ppermute | solution.py:72
  28.5 1.3 %collective-permute-start.13 = (bf16[256,128]{1,0:T(8,128)(2,1)S(1)}, bf16[256,128]{1,0:T(8,128)(2,1)S(1)}, u32[]{:S(2)}, u32[]{:S(2)}) collective-permute-start(bf16[256,128]{1,0:T(8,128)(2,1)S(1)} %get-tuple-element.44.refs_5_), channel_id=1, source_target_pairs={{0,8},{4,12},{8,0},{12,4},{16,24},{20,28},{24,16},{28,20},{1,9},{5... | collective-permute-start | bytes 196616 | tf_op jit(solution)/shard_map/ppermute | solution.py:72
  29.8 2.4 %forward.1.refs_2_.refs_1_ = f32[128,1024]{1,0:T(8,128)S(1)} custom-call(bf16[32,8192]{1,0:T(8,128)(2,1)S(1)} %relay.2.refs_1_.refs_3_.refs_0_.refs_4_, bf16[32,8192]{1,0:T(8,128)(2,1)S(1)} %relay.3.refs_3_.refs_4_.refs_1_.refs_5_, bf16[32,8192]{1,0:T(8,128)(2,1)S(1)} %collective-permute-done.4.refs_5_.refs_2_.refs_6_, ...), custom_call_target="tpu_custom_call" | custom-call | flops 10000000000 | bytes 10000000 | tf_op jit(solution)/shard_map/forward/pallas_call | solution.py:435
  32.2 0.6 %collective-permute-done.13.refs_1_ = bf16[256,128]{1,0:T(8,128)(2,1)S(1)} collective-permute-done((bf16[256,128]{1,0:T(8,128)(2,1)S(1)}, bf16[256,128]{1,0:T(8,128)(2,1)S(1)}, u32[]{:S(2)}, u32[]{:S(2)}) %collective-permute-start.13) | collective-permute-done | bytes 65568 | tf_op jit(solution)/shard_map/ppermute | solution.py:72
  32.9 2.3 %collective-permute-start.16 = (bf16[128,128]{1,0:T(8,128)(2,1)S(1)}, bf16[128,128]{1,0:T(8,128)(2,1)S(1)}, u32[]{:S(2)}, u32[]{:S(2)}) collective-permute-start(bf16[128,128]{1,0:T(8,128)(2,1)S(1)} %get-tuple-element.47.refs_2_), channel_id=1, source_target_pairs={{0,16},{4,20},{8,24},{12,28},{16,0},{20,4},{24,8},{28,12},{1,17},{... | collective-permute-start | bytes 98312 | tf_op jit(solution)/shard_map/ppermute | solution.py:72
  35.3 2.5 %collective-permute-done.16.refs_1_ = bf16[128,128]{1,0:T(8,128)(2,1)S(1)} collective-permute-done((bf16[128,128]{1,0:T(8,128)(2,1)S(1)}, bf16[128,128]{1,0:T(8,128)(2,1)S(1)}, u32[]{:S(2)}, u32[]{:S(2)}) %collective-permute-start.16) | collective-permute-done | bytes 32800 | tf_op jit(solution)/shard_map/ppermute | solution.py:72
  37.7 1.2 %collective-permute-start.17 = (bf16[64,128]{1,0:T(8,128)(2,1)S(1)}, bf16[64,128]{1,0:T(8,128)(2,1)S(1)}, u32[]{:S(2)}, u32[]{:S(2)}) collective-permute-start(bf16[64,128]{1,0:T(8,128)(2,1)S(1)} %get-tuple-element.50.refs_6_), channel_id=1, source_target_pairs={{0,2},{1,3},{2,0},{3,1},{4,6},{5,7},{6,4},{7,5},{8,10},{9,11},{10,... | collective-permute-start | bytes 49160 | tf_op jit(solution)/shard_map/ppermute | solution.py:72
  39.0 0.3 correct.1.refs_8_.refs_0_.refs_2_.refs_5_
  39.3 0.9 %final.1 = bf16[32,8192]{1,0:T(8,128)(2,1)} custom-call(f32[32,8192]{1,0:T(8,128)S(1)} %correct.1.refs_8_.refs_0_.refs_2_.refs_5_, bf16[32,5120]{1,0:T(8,128)(2,1)S(1)} %collective-permute-done.12.refs_1_, f32[32,8192]{1,0:T(8,128)S(1)} %correct.1.refs_8_.refs_0_.refs_2_.refs_5_), custom_call_target="tpu_custom_call" | custom-call | flops 10000000000 | bytes 10000000 | tf_op jit(solution)/shard_map/final/pallas_call | solution.py:531
  40.2 1.2 %project.1 = bf16[128,1024]{1,0:T(8,128)(2,1)} custom-call(s32[2,8]{1,0:T(2,128)S(1)} %bitcast.10, f32[128,1024]{1,0:T(8,128)S(1)} %forward.1.refs_2_.refs_1_, bf16[512,128]{1,0:T(8,128)(2,1)S(1)} %unride.1.refs_2_.refs_1_, bf16[512,128]{1,0:T(8,128)(2,1)S(1)} %collective-permute-done.14.refs_2_.refs_3_, ...), custom_call_target="tpu_custom_call" | custom-call | flops 10000000000 | bytes 10000000 | tf_op jit(solution)/shard_map/project/pallas_call | solution.py:474
  41.4 0.2 collective-permute-done.17.refs_1_
  41.6 0.7 %adam.1 = (bf16[2,4096]{1,0:T(2,128)(2,1)}, f32[2,4096]{1,0:T(2,128)}, f32[2,4096]{1,0:T(2,128)}) custom-call(bf16[64,128]{1,0:T(8,128)(2,1)S(1)} %get-tuple-element.51.refs_0_, bf16[64,128]{1,0:T(8,128)(2,1)S(1)} %collective-permute-done.17.refs_1_, bf16[2,4096]{1,0:T(2,128)(2,1)S(1)} %copy-done.5, f32[2,4096]{1,0:T(2,128)S(1)} %copy-done.2, ...), custom_call_target="tpu_custom_call" | custom-call | flops 10000000000 | bytes 10000000 | tf_op jit(solution)/shard_map/adam/pallas_call | solution.py:325
  (54 shorter events, 0.7 us)
Async XLA Ops:
  0.6 1.0 %copy-start = (bf16[32,8192]{1,0:T(8,128)(2,1)S(1)}, bf16[32,8192]{1,0:T(8,128)(2,1)}, u32[]{:S(2)}) copy-start(bf16[32,8192]{1,0:T(8,128)(2,1)} %refs_0_.2) | copy-start | bytes 1572868
  1.7 3.1 %copy-start.4 = (bf16[2,4096]{1,0:T(2,128)(2,1)S(1)}, bf16[2,4096]{1,0:T(2,128)(2,1)}, u32[]{:S(2)}) copy-start(bf16[2,4096]{1,0:T(2,128)(2,1)} %refs_2_.11) | copy-start | bytes 49156
  1.7 4.7 %slice-start = ((s8[16777216]{0:T(1024)(128)(4,1)}), s8[4194304]{0:T(1024)(128)(4,1)S(1)}, s32[]{:S(2)}) async-start(s8[16777216]{0:T(1024)(128)(4,1)} %bitcast.2), calls=%async_computation | async-start | bytes 8388608
  1.7 4.7 %slice-start.1 = ((s8[16777216]{0:T(1024)(128)(4,1)}), s8[4194304]{0:T(1024)(128)(4,1)S(1)}, s32[]{:S(2)}) async-start(s8[16777216]{0:T(1024)(128)(4,1)} %bitcast.2), calls=%async_computation.1 | async-start | bytes 8388608
  1.7 4.7 %slice-start.2 = ((s8[16777216]{0:T(1024)(128)(4,1)}), s8[4194304]{0:T(1024)(128)(4,1)S(1)}, s32[]{:S(2)}) async-start(s8[16777216]{0:T(1024)(128)(4,1)} %bitcast.2), calls=%async_computation.2 | async-start | bytes 8388608
  1.7 5.8 %slice-start.3 = ((s8[16777216]{0:T(1024)(128)(4,1)}), s8[4194304]{0:T(1024)(128)(4,1)S(1)}, s32[]{:S(2)}) async-start(s8[16777216]{0:T(1024)(128)(4,1)} %bitcast.2), calls=%async_computation.3 | async-start | bytes 8388608
  1.7 5.8 %copy-start.1 = (bf16[128,1024]{1,0:T(8,128)(2,1)S(1)}, bf16[128,1024]{1,0:T(8,128)(2,1)}, u32[]{:S(2)}) copy-start(bf16[128,1024]{1,0:T(8,128)(2,1)} %refs_2_.10) | copy-start | bytes 786436
  1.8 5.8 %copy-start.6 = (s32[8,2]{0,1:T(2,128)S(1)}, s32[8,2]{0,1:T(2,128)}, u32[]{:S(2)}) copy-start(s32[8,2]{0,1:T(2,128)} %param.11) | copy-start | bytes 196
  1.8 15.2 %collective-permute-start = (bf16[32,8192]{1,0:T(8,128)(2,1)S(1)}, bf16[32,8192]{1,0:T(8,128)(2,1)S(1)}, u32[]{:S(2)}, u32[]{:S(2)}) collective-permute-start(bf16[32,8192]{1,0:T(8,128)(2,1)S(1)} %relay.2.refs_1_.refs_3_.refs_0_.refs_4_), channel_id=1, source_target_pairs={{0,2},{1,3},{2,0},{3,1},{4,6},{5,7},{6,4},{7,5},{8,10},{9,11},{10,... | collective-permute-start | bytes 1572872 | tf_op jit(solution)/shard_map/ppermute | solution.py:72
  4.8 13.9 %collective-permute-start.4 = (bf16[32,8192]{1,0:T(8,128)(2,1)S(1)}, bf16[32,8192]{1,0:T(8,128)(2,1)S(1)}, u32[]{:S(2)}, u32[]{:S(2)}) collective-permute-start(bf16[32,8192]{1,0:T(8,128)(2,1)S(1)} %relay.2.refs_1_.refs_3_.refs_0_.refs_4_), channel_id=1, source_target_pairs={{0,1},{1,0},{2,3},{3,2},{4,5},{5,4},{6,7},{7,6},{8,9},{9,8},{10,11... | collective-permute-start | bytes 1572872 | tf_op jit(solution)/shard_map/ppermute | solution.py:72
  4.8 4.6 %collective-permute-start.1 = (bf16[64,128]{1,0:T(8,128)(2,1)S(1)}, bf16[64,128]{1,0:T(8,128)(2,1)S(1)}, u32[]{:S(2)}, u32[]{:S(2)}) collective-permute-start(bf16[64,128]{1,0:T(8,128)(2,1)S(1)} %lines.1.refs_0_), channel_id=1, source_target_pairs={{0,4},{4,0},{8,12},{12,8},{16,20},{20,16},{24,28},{28,24},{1,5},{5... | collective-permute-start | bytes 49160 | tf_op jit(solution)/shard_map/ppermute | solution.py:72
  8.9 6.4 %collective-permute-start.2 = (bf16[64,2048]{1,0:T(8,128)(2,1)S(1)}, bf16[64,2048]{1,0:T(8,128)(2,1)S(1)}, u32[]{:S(2)}, u32[]{:S(2)}) collective-permute-start(bf16[64,2048]{1,0:T(8,128)(2,1)S(1)} %get-tuple-element.31.refs_2_), channel_id=1, source_target_pairs={{0,1},{1,0},{2,3},{3,2},{4,5},{5,4},{6,7},{7,6},{8,9},{9,8},{10,11... | collective-permute-start | bytes 786440 | tf_op jit(solution)/shard_map/ppermute | solution.py:72
  10.7 4.5 %collective-permute-start.3 = (bf16[64,3072]{1,0:T(8,128)(2,1)S(1)}, bf16[64,3072]{1,0:T(8,128)(2,1)S(1)}, u32[]{:S(2)}, u32[]{:S(2)}) collective-permute-start(bf16[64,3072]{1,0:T(8,128)(2,1)S(1)} %get-tuple-element.33.refs_3_), channel_id=1, source_target_pairs={{0,1},{1,0},{2,3},{3,2},{4,5},{5,4},{6,7},{7,6},{8,9},{9,8},{10,11... | collective-permute-start | bytes 1179656 | tf_op jit(solution)/shard_map/ppermute | solution.py:72
  12.2 7.8 %collective-permute-start.7 = (bf16[128,128]{1,0:T(8,128)(2,1)S(1)}, bf16[128,128]{1,0:T(8,128)(2,1)S(1)}, u32[]{:S(2)}, u32[]{:S(2)}) collective-permute-start(bf16[128,128]{1,0:T(8,128)(2,1)S(1)} %double.2.refs_3_.refs_0_), channel_id=1, source_target_pairs={{0,8},{4,12},{8,0},{12,4},{16,24},{20,28},{24,16},{28,20},{1,9},{5... | collective-permute-start | bytes 98312 | tf_op jit(solution)/shard_map/ppermute | solution.py:72
  15.3 11.5 %collective-permute-start.9 = (bf16[64,2048]{1,0:T(8,128)(2,1)S(1)}, bf16[64,2048]{1,0:T(8,128)(2,1)S(1)}, u32[]{:S(2)}, u32[]{:S(2)}) collective-permute-start(bf16[64,2048]{1,0:T(8,128)(2,1)S(1)} %get-tuple-element.34.refs_4_), channel_id=1, source_target_pairs={{0,1},{1,0},{2,3},{3,2},{4,5},{5,4},{6,7},{7,6},{8,9},{9,8},{10,11... | collective-permute-start | bytes 786440 | tf_op jit(solution)/shard_map/ppermute | solution.py:72
  15.4 23.5 %collective-permute-start.15 = (bf16[32,5120]{1,0:T(8,128)(2,1)S(1)}, bf16[32,5120]{1,0:T(8,128)(2,1)S(1)}, u32[]{:S(2)}, u32[]{:S(2)}) collective-permute-start(bf16[32,5120]{1,0:T(8,128)(2,1)S(1)} %get-tuple-element.48), channel_id=1, source_target_pairs={{0,2},{1,3},{2,0},{3,1},{4,6},{5,7},{6,4},{7,5},{8,10},{9,11},{10,... | collective-permute-start | bytes 983048 | tf_op jit(solution)/shard_map/ppermute | solution.py:72
  17.0 2.0 %copy-start.7 = (s32[8]{0:T(128)S(1)}, s32[8]{0:T(128)}, u32[]{:S(2)}) copy-start(s32[8]{0:T(128)} %param.12) | copy-start | bytes 100
  17.0 2.0 %collective-permute-start.5 = (bf16[32,8192]{1,0:T(8,128)(2,1)S(1)}, bf16[32,8192]{1,0:T(8,128)(2,1)S(1)}, u32[]{:S(2)}, u32[]{:S(2)}) collective-permute-start(bf16[32,8192]{1,0:T(8,128)(2,1)S(1)} %relay.3.refs_3_.refs_4_.refs_1_.refs_5_), channel_id=1, source_target_pairs={{0,1},{1,0},{2,3},{3,2},{4,5},{5,4},{6,7},{7,6},{8,9},{9,8},{10,11... | collective-permute-start | bytes 1572872 | tf_op jit(solution)/shard_map/ppermute | solution.py:72
  18.7 8.2 %collective-permute-start.10 = (bf16[64,2048]{1,0:T(8,128)(2,1)S(1)}, bf16[64,2048]{1,0:T(8,128)(2,1)S(1)}, u32[]{:S(2)}, u32[]{:S(2)}) collective-permute-start(bf16[64,2048]{1,0:T(8,128)(2,1)S(1)} %get-tuple-element.36.refs_7_), channel_id=1, source_target_pairs={{0,1},{1,0},{2,3},{3,2},{4,5},{5,4},{6,7},{7,6},{8,9},{9,8},{10,11... | collective-permute-start | bytes 786440 | tf_op jit(solution)/shard_map/ppermute | solution.py:72
  19.7 3.0 %collective-permute-start.6 = (bf16[1024,128]{1,0:T(8,128)(2,1)S(1)}, bf16[1024,128]{1,0:T(8,128)(2,1)S(1)}, u32[]{:S(2)}, u32[]{:S(2)}) collective-permute-start(bf16[1024,128]{1,0:T(8,128)(2,1)S(1)} %get-tuple-element.38.refs_2_), channel_id=1, source_target_pairs={{0,1},{1,0},{2,3},{3,2},{4,5},{5,4},{6,7},{7,6},{8,9},{9,8},{10,11... | collective-permute-start | bytes 786440 | tf_op jit(solution)/shard_map/ppermute | solution.py:72
  20.0 6.6 %collective-permute-start.11 = (bf16[256,128]{1,0:T(8,128)(2,1)S(1)}, bf16[256,128]{1,0:T(8,128)(2,1)S(1)}, u32[]{:S(2)}, u32[]{:S(2)}) collective-permute-start(bf16[256,128]{1,0:T(8,128)(2,1)S(1)} %double.3.refs_2_.refs_1_), channel_id=1, source_target_pairs={{0,16},{4,20},{8,24},{12,28},{16,0},{20,4},{24,8},{28,12},{1,17},{... | collective-permute-start | bytes 196616 | tf_op jit(solution)/shard_map/ppermute | solution.py:72
  22.7 5.7 %collective-permute-start.8 = (bf16[512,128]{1,0:T(8,128)(2,1)S(1)}, bf16[512,128]{1,0:T(8,128)(2,1)S(1)}, u32[]{:S(2)}, u32[]{:S(2)}) collective-permute-start(bf16[512,128]{1,0:T(8,128)(2,1)S(1)} %get-tuple-element.40.refs_3_), channel_id=1, source_target_pairs={{0,4},{4,0},{8,12},{12,8},{16,20},{20,16},{24,28},{28,24},{1,5},{5... | collective-permute-start | bytes 393224 | tf_op jit(solution)/shard_map/ppermute | solution.py:72
  27.0 8.2 %collective-permute-start.12 = (bf16[32,5120]{1,0:T(8,128)(2,1)S(1)}, bf16[32,5120]{1,0:T(8,128)(2,1)S(1)}, u32[]{:S(2)}, u32[]{:S(2)}) collective-permute-start(bf16[32,5120]{1,0:T(8,128)(2,1)S(1)} %get-tuple-element.45), channel_id=1, source_target_pairs={{0,2},{1,3},{2,0},{3,1},{4,6},{5,7},{6,4},{7,5},{8,10},{9,11},{10,... | collective-permute-start | bytes 983048 | tf_op jit(solution)/shard_map/ppermute | solution.py:72
  28.5 4.3 %collective-permute-start.13 = (bf16[256,128]{1,0:T(8,128)(2,1)S(1)}, bf16[256,128]{1,0:T(8,128)(2,1)S(1)}, u32[]{:S(2)}, u32[]{:S(2)}) collective-permute-start(bf16[256,128]{1,0:T(8,128)(2,1)S(1)} %get-tuple-element.44.refs_5_), channel_id=1, source_target_pairs={{0,8},{4,12},{8,0},{12,4},{16,24},{20,28},{24,16},{28,20},{1,9},{5... | collective-permute-start | bytes 196616 | tf_op jit(solution)/shard_map/ppermute | solution.py:72
  32.9 4.9 %collective-permute-start.16 = (bf16[128,128]{1,0:T(8,128)(2,1)S(1)}, bf16[128,128]{1,0:T(8,128)(2,1)S(1)}, u32[]{:S(2)}, u32[]{:S(2)}) collective-permute-start(bf16[128,128]{1,0:T(8,128)(2,1)S(1)} %get-tuple-element.47.refs_2_), channel_id=1, source_target_pairs={{0,16},{4,20},{8,24},{12,28},{16,0},{20,4},{24,8},{28,12},{1,17},{... | collective-permute-start | bytes 98312 | tf_op jit(solution)/shard_map/ppermute | solution.py:72
  35.2 3.8 %collective-permute-start.14 = (bf16[512,128]{1,0:T(8,128)(2,1)S(1)}, bf16[512,128]{1,0:T(8,128)(2,1)S(1)}, u32[]{:S(2)}, u32[]{:S(2)}) collective-permute-start(bf16[512,128]{1,0:T(8,128)(2,1)S(1)} %unride.1.refs_2_.refs_1_), channel_id=1, source_target_pairs={{0,1},{1,0},{2,3},{3,2},{4,5},{5,4},{6,7},{7,6},{8,9},{9,8},{10,11... | collective-permute-start | bytes 393224 | tf_op jit(solution)/shard_map/ppermute | solution.py:72
  37.7 3.8 %collective-permute-start.17 = (bf16[64,128]{1,0:T(8,128)(2,1)S(1)}, bf16[64,128]{1,0:T(8,128)(2,1)S(1)}, u32[]{:S(2)}, u32[]{:S(2)}) collective-permute-start(bf16[64,128]{1,0:T(8,128)(2,1)S(1)} %get-tuple-element.50.refs_6_), channel_id=1, source_target_pairs={{0,2},{1,3},{2,0},{3,1},{4,6},{5,7},{6,4},{7,5},{8,10},{9,11},{10,... | collective-permute-start | bytes 49160 | tf_op jit(solution)/shard_map/ppermute | solution.py:72
  40.2 1.3 %copy-start.2 = (f32[2,4096]{1,0:T(2,128)S(1)}, f32[2,4096]{1,0:T(2,128)}, u32[]{:S(2)}) copy-start(f32[2,4096]{1,0:T(2,128)} %refs_3_.1) | copy-start | bytes 98308
  40.2 1.3 %copy-start.3 = (f32[2,4096]{1,0:T(2,128)S(1)}, f32[2,4096]{1,0:T(2,128)}, u32[]{:S(2)}) copy-start(f32[2,4096]{1,0:T(2,128)} %refs_4_.3) | copy-start | bytes 98308
  40.2 1.3 %copy-start.5 = (bf16[2,4096]{1,0:T(2,128)(2,1)S(1)}, bf16[2,4096]{1,0:T(2,128)(2,1)}, u32[]{:S(2)}) copy-start(bf16[2,4096]{1,0:T(2,128)(2,1)} %refs_2_.11) | copy-start | bytes 49156
